TPU v7x, 32 devices: a whole 2x2x4 slice. The times are simulated.
32 devices in a mesh: dp: 8 (over z, y), sp: 4 (over x, core).
Axes of the slice: x: 2, y: 2, z: 4, core: 2. Of those that a mesh axis runs over, the one named last changes fastest.
Arguments:
- inputs: bfloat16 [16, 2048, 1024], P('dp', 'sp'), may hold values from -6 to 6
- cotangent: bfloat16 [16, 2048, 1024], P('dp', 'sp'), may hold values from -6 to 6
- group_ids: int32 [16], P('dp'), may hold values from 0 to 7
- group_scale: float32 [8], replicated, may hold values from 0.3 to 3
- norm_gain: bfloat16 [1024], P(('dp', 'sp')), may hold values from 0.5 to 1.5
- w_query: bfloat16 [1024, 1024], P(('dp', 'sp')), may hold values from -0.1875 to 0.1875
- w_latent: bfloat16 [1024, 512], P(('dp', 'sp')), may hold values from -0.1875 to 0.1875
- expansion_weight: bfloat16 [2, 256, 1024], P(None, ('dp', 'sp')), may hold values from -0.375 to 0.375
- w_output: bfloat16 [1024, 1024], P(('dp', 'sp')), may hold values from -3 to 3
- ffn_gain: bfloat16 [1024], P(('dp', 'sp')), may hold values from 0.5 to 1.5
- w_gate: bfloat16 [1024, 2816], P(('dp', 'sp')), may hold values from -0.1875 to 0.1875
- w_up: bfloat16 [1024, 2816], P(('dp', 'sp')), may hold values from -0.1875 to 0.1875
- w_down: bfloat16 [2816, 1024], P(('dp', 'sp')), may hold values from -0.109375 to 0.109375
Outputs:
- output: bfloat16 [16, 2048, 1024], P('dp', 'sp')
- input_grad: bfloat16 [16, 2048, 1024], P('dp', 'sp')
- norm_gain_grad: float32 [1024], P(('dp', 'sp'))
- query_grad: float32 [1024, 1024], P(('dp', 'sp'))
- latent_grad: float32 [1024, 512], P(('dp', 'sp'))
- expand_grad: float32 [2, 256, 1024], P(None, ('dp', 'sp'))
- output_grad: float32 [1024, 1024], P(('dp', 'sp'))
- ffn_gain_grad: float32 [1024], P(('dp', 'sp'))
- gate_grad: float32 [1024, 2816], P(('dp', 'sp'))
- up_grad: float32 [1024, 2816], P(('dp', 'sp'))
- down_grad: float32 [2816, 1024], P(('dp', 'sp'))
All inputs are finite; a program needn't handle non-finite values.
Results may differ from a plain program's by a relative error of at most 0.02.
Values may be sent and summed in bfloat16 or wider, within the bound.
A program may use at most 192 MiB of HBM per device.

v0:
```python
import jax
import jax.numpy as jnp
from jax import lax
from jax.sharding import PartitionSpec as P

HEADS = 16
DH = 64
KVH = 2
LATD = 256
HG = 8
GROUPS = 8


EPSILON = 1e-05


def dot_low(left, right):
    return jnp.dot(left, right, preferred_element_type=jnp.float32)


def norm_parts(values, gain):
    inverse = lax.rsqrt(jnp.mean(values * values, axis=-1, keepdims=True) + EPSILON)
    return (values * inverse * gain, inverse)


def norm_back(values, inverse, gain, upstream):
    scaled = upstream * gain
    gain_grad = jnp.sum(upstream * values * inverse, axis=0)
    input_part = inverse * scaled - values * inverse**3 * jnp.mean(
        scaled * values, axis=-1, keepdims=True
    )
    return (input_part, gain_grad)


def masked_scores(query_block, seq_keys, block_start, block_rows, scale):
    seq_length = seq_keys.shape[0]
    scores = (
        jnp.einsum("qhd,khd->hqk", query_block, seq_keys, preferred_element_type=jnp.float32)
        * scale
    )
    row_index = block_start + jnp.arange(block_rows)
    positions = jnp.arange(seq_length)
    return jnp.where(row_index[None, :, None] >= positions[None, None, :], scores, -1e30)


def attention_forward(head_queries, key_heads, value_heads, scale):
    seq_count, seq_length, local_heads, head_size = head_queries.shape
    block_rows = min(512, seq_length)
    block_count = seq_length // block_rows

    def one_sequence(seq_item):
        sequence_queries, seq_keys, seq_values = seq_item

        def one_block(index):
            block_start = index * block_rows
            query_block = lax.dynamic_slice_in_dim(sequence_queries, block_start, block_rows, 0)
            scores = masked_scores(query_block, seq_keys, block_start, block_rows, scale)
            top_score = jnp.max(scores, axis=-1, keepdims=True)
            expo = jnp.exp(scores - top_score)
            total = jnp.sum(expo, axis=-1, keepdims=True)
            probabilities = (expo / total).astype(jnp.bfloat16)
            mixed = jnp.einsum(
                "hqk,khd->qhd", probabilities, seq_values, preferred_element_type=jnp.float32
            )
            return (mixed.astype(jnp.bfloat16), (top_score + jnp.log(total))[..., 0])

        mixed_blocks, logsum = lax.map(one_block, jnp.arange(block_count))
        return (mixed_blocks.reshape(seq_length, local_heads, head_size), logsum)

    return lax.map(one_sequence, (head_queries, key_heads, value_heads))


def attention_backward(head_queries, key_heads, value_heads, logsum, head_upstream, scale):
    seq_count, seq_length, local_heads, head_size = head_queries.shape
    block_rows = min(512, seq_length)
    block_count = seq_length // block_rows

    def one_sequence(seq_item):
        sequence_queries, seq_keys, seq_values, seq_logsum, seq_upstream = seq_item

        def one_block(carry, index):
            key_total, value_total = carry
            block_start = index * block_rows
            query_block = lax.dynamic_slice_in_dim(sequence_queries, block_start, block_rows, 0)
            upstream_block = lax.dynamic_slice_in_dim(seq_upstream, block_start, block_rows, 0)
            scores = masked_scores(query_block, seq_keys, block_start, block_rows, scale)
            probabilities = jnp.exp(scores - seq_logsum[index][..., None])
            rounded = probabilities.astype(jnp.bfloat16)
            value_total = value_total + jnp.einsum(
                "hqk,qhd->khd", rounded, upstream_block, preferred_element_type=jnp.float32
            )
            prob_back = jnp.einsum(
                "qhd,khd->hqk", upstream_block, seq_values, preferred_element_type=jnp.float32
            )
            center = jnp.sum(probabilities * prob_back, axis=-1, keepdims=True)
            score_back = (probabilities * (prob_back - center)).astype(jnp.bfloat16)
            query_back = (
                jnp.einsum("hqk,khd->qhd", score_back, seq_keys, preferred_element_type=jnp.float32)
                * scale
            )
            key_total = (
                key_total
                + jnp.einsum(
                    "hqk,qhd->khd", score_back, query_block, preferred_element_type=jnp.float32
                )
                * scale
            )
            return ((key_total, value_total), query_back)

        zero_heads = jnp.zeros(seq_keys.shape, jnp.float32)
        (key_total, value_total), query_blocks = lax.scan(
            one_block, (zero_heads, zero_heads), jnp.arange(block_count)
        )
        query_total = query_blocks.reshape(seq_length, local_heads, head_size)
        return (
            query_total.astype(jnp.bfloat16),
            key_total.astype(jnp.bfloat16),
            value_total.astype(jnp.bfloat16),
        )

    return lax.map(one_sequence, (head_queries, key_heads, value_heads, logsum, head_upstream))


def local(
    inputs,
    cotangent,
    group_ids,
    group_scale,
    norm_gain,
    w_query,
    w_latent,
    expansion_weight,
    w_output,
    ffn_gain,
    w_gate,
    w_up,
    w_down,
):
    parts = lax.axis_size("sp")
    local_heads = HEADS // parts
    seq_count, seq_tokens, width = inputs.shape
    token_count = seq_count * seq_tokens
    full_length = seq_tokens * parts
    scale = DH ** (-0.5)
    gain_one, query_full, latent_full, expand_full, output_full = (
        lax.all_gather(norm_gain, ("dp", "sp"), axis=0, tiled=True),
        lax.all_gather(w_query, ("dp", "sp"), axis=0, tiled=True),
        lax.all_gather(w_latent, ("dp", "sp"), axis=0, tiled=True),
        lax.all_gather(expansion_weight, ("dp", "sp"), axis=1, tiled=True),
        lax.all_gather(w_output, ("dp", "sp"), axis=0, tiled=True),
    )
    gain_two, gate_full, up_full, down_full = (
        lax.all_gather(ffn_gain, ("dp", "sp"), axis=0, tiled=True),
        lax.all_gather(w_gate, ("dp", "sp"), axis=0, tiled=True),
        lax.all_gather(w_up, ("dp", "sp"), axis=0, tiled=True),
        lax.all_gather(w_down, ("dp", "sp"), axis=0, tiled=True),
    )
    gain_one = gain_one.astype(jnp.float32)
    gain_two = gain_two.astype(jnp.float32)
    token_rows = inputs.astype(jnp.float32).reshape(token_count, width)
    normed, inverse_one = norm_parts(token_rows, gain_one)
    normed_low = normed.astype(jnp.bfloat16)
    queries = dot_low(normed_low, query_full).astype(jnp.bfloat16)
    latent_state = dot_low(normed_low, latent_full).astype(jnp.bfloat16)
    latent_groups = latent_state.reshape(token_count, KVH, LATD)
    query_send = queries.reshape(seq_count, seq_tokens, parts, local_heads * DH)
    head_first = lax.axis_index("sp") * local_heads
    group_index = head_first // HG
    column_first = head_first % HG * 2 * DH
    latent_send = jnp.repeat(
        latent_groups.reshape(seq_count, seq_tokens, KVH, LATD), parts // KVH, axis=2
    )
    head_queries, head_latent = (
        lax.all_to_all(query_send, "sp", split_axis=2, concat_axis=1, tiled=True),
        lax.all_to_all(latent_send, "sp", split_axis=2, concat_axis=1, tiled=True),
    )
    expand_local = lax.dynamic_slice(
        expand_full, (group_index, 0, column_first), (1, LATD, local_heads * 2 * DH)
    )[0]
    head_latent = head_latent.reshape(seq_count * full_length, LATD)
    head_pairs = dot_low(head_latent, expand_local).astype(jnp.bfloat16)
    head_pairs = head_pairs.reshape(seq_count, full_length, local_heads, 2, DH)
    head_queries = head_queries.reshape(seq_count, full_length, local_heads, DH)
    key_heads = head_pairs[:, :, :, 0]
    value_heads = head_pairs[:, :, :, 1]
    attended, logsum = attention_forward(head_queries, key_heads, value_heads, scale)
    attended_send = attended.reshape(seq_count, full_length, 1, local_heads * DH)
    token_attended = lax.all_to_all(
        attended_send, "sp", split_axis=1, concat_axis=2, tiled=True
    ).reshape(token_count, HEADS * DH)
    middle = token_rows + dot_low(token_attended, output_full)
    normed_two, inverse_two = norm_parts(middle, gain_two)
    normed_two_low = normed_two.astype(jnp.bfloat16)
    gate_pre = dot_low(normed_two_low, gate_full)
    upward = dot_low(normed_two_low, up_full)
    sigmoid = jax.nn.sigmoid(gate_pre)
    activated = gate_pre * sigmoid
    hidden = (activated * upward).astype(jnp.bfloat16)
    result = middle + dot_low(hidden, down_full)
    output = result.astype(jnp.bfloat16).reshape(seq_count, seq_tokens, width)
    chosen = (group_ids[:, None] == jnp.arange(GROUPS)[None, :]).astype(jnp.float32)
    seq_scale = jnp.sum(chosen * group_scale[None, :], axis=1)
    upstream = (cotangent.astype(jnp.float32) * seq_scale[:, None, None]).reshape(
        token_count, width
    )
    upstream_low = upstream.astype(jnp.bfloat16)
    down_grad = jnp.einsum("rf,rd->fd", hidden, upstream_low, preferred_element_type=jnp.float32)
    hidden_back = jnp.einsum(
        "rd,fd->rf", upstream_low, down_full, preferred_element_type=jnp.float32
    )
    gate_back = (hidden_back * upward * sigmoid * (1.0 + gate_pre * (1.0 - sigmoid))).astype(
        jnp.bfloat16
    )
    up_back = (hidden_back * activated).astype(jnp.bfloat16)
    gate_grad = jnp.einsum(
        "rd,rf->df", normed_two_low, gate_back, preferred_element_type=jnp.float32
    )
    up_grad = jnp.einsum("rd,rf->df", normed_two_low, up_back, preferred_element_type=jnp.float32)
    normed_two_back = jnp.einsum(
        "rf,df->rd", gate_back, gate_full, preferred_element_type=jnp.float32
    ) + jnp.einsum("rf,df->rd", up_back, up_full, preferred_element_type=jnp.float32)
    middle_part, gain_two_grad = norm_back(middle, inverse_two, gain_two, normed_two_back)
    middle_grad = upstream + middle_part
    ffn_block = (
        lax.psum_scatter(
            gain_two_grad.astype(jnp.bfloat16), "dp", scatter_dimension=0, tiled=True
        ).astype(jnp.float32),
        lax.psum_scatter(
            gate_grad.astype(jnp.bfloat16), "dp", scatter_dimension=0, tiled=True
        ).astype(jnp.float32),
        lax.psum_scatter(
            up_grad.astype(jnp.bfloat16), "dp", scatter_dimension=0, tiled=True
        ).astype(jnp.float32),
        lax.psum_scatter(
            down_grad.astype(jnp.bfloat16), "dp", scatter_dimension=0, tiled=True
        ).astype(jnp.float32),
    )
    ffn_shares = (
        lax.psum_scatter(
            ffn_block[0].astype(jnp.bfloat16), "sp", scatter_dimension=0, tiled=True
        ).astype(jnp.float32),
        lax.psum_scatter(
            ffn_block[1].astype(jnp.bfloat16), "sp", scatter_dimension=0, tiled=True
        ).astype(jnp.float32),
        lax.psum_scatter(
            ffn_block[2].astype(jnp.bfloat16), "sp", scatter_dimension=0, tiled=True
        ).astype(jnp.float32),
        lax.psum_scatter(
            ffn_block[3].astype(jnp.bfloat16), "sp", scatter_dimension=0, tiled=True
        ).astype(jnp.float32),
    )
    branch_low = middle_grad.astype(jnp.bfloat16)
    output_grad = jnp.einsum(
        "re,rd->ed", token_attended, branch_low, preferred_element_type=jnp.float32
    )
    attended_back = jnp.einsum(
        "rd,ed->re", branch_low, output_full, preferred_element_type=jnp.float32
    ).astype(jnp.bfloat16)
    attended_back_send = attended_back.reshape(seq_count, seq_tokens, parts, local_heads * DH)
    head_upstream = lax.all_to_all(
        attended_back_send, "sp", split_axis=2, concat_axis=1, tiled=True
    ).reshape(seq_count, full_length, local_heads, DH)
    query_back, key_back, value_back = attention_backward(
        head_queries, key_heads, value_heads, logsum, head_upstream, scale
    )
    pair_back = jnp.stack([key_back, value_back], axis=3)
    pair_flat = pair_back.reshape(seq_count * full_length, local_heads * 2 * DH)
    latent_terms = jnp.einsum(
        "rc,lc->rl", pair_flat, expand_local, preferred_element_type=jnp.float32
    )
    expand_part = jnp.einsum(
        "rl,rc->lc", head_latent, pair_flat, preferred_element_type=jnp.float32
    )
    expand_grad = lax.dynamic_update_slice(
        jnp.zeros(expand_full.shape, jnp.float32), expand_part[None], (group_index, 0, column_first)
    )
    query_narrow = query_back.reshape(seq_count, full_length, 1, local_heads * DH)
    latent_wide = latent_terms.reshape(seq_count, full_length, 1, LATD)
    back_query = lax.all_to_all(query_narrow, "sp", split_axis=1, concat_axis=2, tiled=True)
    back_latent = lax.all_to_all(
        latent_wide.astype(jnp.bfloat16), "sp", split_axis=1, concat_axis=2, tiled=True
    ).astype(latent_wide.dtype)
    query_token_back = back_query.reshape(token_count, HEADS * DH)
    latent_sum = jnp.sum(
        back_latent.reshape(seq_count, seq_tokens, KVH, parts // KVH, LATD), axis=3
    )
    latent_token_back = latent_sum.reshape(token_count, KVH * LATD).astype(jnp.bfloat16)
    query_grad = jnp.einsum(
        "rd,re->de", normed_low, query_token_back, preferred_element_type=jnp.float32
    )
    latent_grad = jnp.einsum(
        "rd,re->de", normed_low, latent_token_back, preferred_element_type=jnp.float32
    )
    normed_back = jnp.einsum(
        "re,de->rd", query_token_back, query_full, preferred_element_type=jnp.float32
    ) + jnp.einsum("re,de->rd", latent_token_back, latent_full, preferred_element_type=jnp.float32)
    input_part, first_gain_gradient = norm_back(token_rows, inverse_one, gain_one, normed_back)
    input_grad = (
        (middle_grad + input_part).astype(jnp.bfloat16).reshape(seq_count, seq_tokens, width)
    )
    attn_block = (
        lax.psum_scatter(
            first_gain_gradient.astype(jnp.bfloat16), "dp", scatter_dimension=0, tiled=True
        ).astype(jnp.float32),
        lax.psum_scatter(
            query_grad.astype(jnp.bfloat16), "dp", scatter_dimension=0, tiled=True
        ).astype(jnp.float32),
        lax.psum_scatter(
            latent_grad.astype(jnp.bfloat16), "dp", scatter_dimension=0, tiled=True
        ).astype(jnp.float32),
        lax.psum_scatter(
            expand_grad.astype(jnp.bfloat16), "dp", scatter_dimension=1, tiled=True
        ).astype(jnp.float32),
        lax.psum_scatter(
            output_grad.astype(jnp.bfloat16), "dp", scatter_dimension=0, tiled=True
        ).astype(jnp.float32),
    )
    attn_shares = (
        lax.psum_scatter(
            attn_block[0].astype(jnp.bfloat16), "sp", scatter_dimension=0, tiled=True
        ).astype(jnp.float32),
        lax.psum_scatter(
            attn_block[1].astype(jnp.bfloat16), "sp", scatter_dimension=0, tiled=True
        ).astype(jnp.float32),
        lax.psum_scatter(
            attn_block[2].astype(jnp.bfloat16), "sp", scatter_dimension=0, tiled=True
        ).astype(jnp.float32),
        lax.psum_scatter(
            attn_block[3].astype(jnp.bfloat16), "sp", scatter_dimension=1, tiled=True
        ).astype(jnp.float32),
        lax.psum_scatter(
            attn_block[4].astype(jnp.bfloat16), "sp", scatter_dimension=0, tiled=True
        ).astype(jnp.float32),
    )
    return (
        output,
        input_grad,
        attn_shares[0],
        attn_shares[1],
        attn_shares[2],
        attn_shares[3],
        attn_shares[4],
        ffn_shares[0],
        ffn_shares[1],
        ffn_shares[2],
        ffn_shares[3],
    )


def solution(mesh):
    return jax.shard_map(
        local,
        mesh=mesh,
        in_specs=(
            P("dp", "sp", None),
            P("dp", "sp", None),
            P("dp"),
            P(),
            P(("dp", "sp")),
            P(("dp", "sp"), None),
            P(("dp", "sp"), None),
            P(None, ("dp", "sp"), None),
            P(("dp", "sp"), None),
            P(("dp", "sp")),
            P(("dp", "sp"), None),
            P(("dp", "sp"), None),
            P(("dp", "sp"), None),
        ),
        out_specs=(
            P("dp", "sp", None),
            P("dp", "sp", None),
            P(("dp", "sp")),
            P(("dp", "sp"), None),
            P(("dp", "sp"), None),
            P(None, ("dp", "sp"), None),
            P(("dp", "sp"), None),
            P(("dp", "sp")),
            P(("dp", "sp"), None),
            P(("dp", "sp"), None),
            P(("dp", "sp"), None),
        ),
        check_vma=False,
    )
```

profile of v0, /device:TPU:0, one launch (start us, length us, event | category | flops | bytes accessed | tf_op | source)
XLA Modules:
  0.0 1780.1 jit_solution(15177313077735888325)
XLA Ops:
  12.8 42.1 %all-reduce.6 = (bf16[1024]{0:T(1024)(128)(2,1)S(1)}, bf16[1024]{0:T(1024)(128)(2,1)}) all-reduce(bf16[1024]{0:T(1024)(128)(2,1)S(1)} %dynamic-update-slice, bf16[1024]{0:T(1024)(128)(2,1)S(1)} %dynamic-update-slice.1), channel_id=1, replica_groups=mesh['dp'=8,'sp'=4] {'dp','sp'}, use_global_device_ids=true, to_apply=%add | all-reduce | flops 2048 | bytes 8192
  75.3 51.7 %all-gather.8.cloned.1.call-done = bf16[1024,1024]{1,0:T(8,128)(2,1)} async-done(((bf16[32,1024]{1,0:T(8,128)(2,1)}), bf16[1024,1024]{1,0:T(8,128)(2,1)}) %all-gather.8.cloned.1.call-update) | async-done | bytes 2097168 | tf_op jit(solution)/shard_map/all_gather | solution.py:147
  147.6 35.4 %all-gather.12.cloned.1.call-done = bf16[2,256,1024]{2,1,0:T(8,128)(2,1)} async-done(((bf16[2,8,1024]{2,1,0:T(8,128)(2,1)}), bf16[2,256,1024]{2,1,0:T(8,128)(2,1)}) %all-gather.12.cloned.1.call-update) | async-done | bytes 1048592 | tf_op jit(solution)/shard_map/all_gather | solution.py:149
  218.4 141.3 %while.54 = (s32[]{:T(128)}, bf16[2,2048,4,64]{1,3,2,0:T(8,128)(2,1)}, f32[2,4,4,512]{3,2,1,0:T(4,128)}, bf16[2,2048,4,64]{1,3,2,0:T(8,128)(2,1)}, bf16[2,2048,4...) while((s32[]{:T(128)}, ...), condition=%wide.region_6.7_spmd, body=%wide.region_1.6_spmd.sunk | while | flops 1125251584 | bytes 69865912 | solution.py:70
  221.4 61.8 %while.57 = (s32[]{:T(128)}, bf16[4,512,4,64]{1,3,2,0:T(8,128)(2,1)}, f32[4,4,512]{2,1,0:T(4,128)S(1)}, s32[4]{0:T(128)S(1)}, bf16[2048,4,64]{0,2,1:T(8,128)(2,1...) while((s32[]{:T(128)}, ...), condition=%wide.region_5.5_spmd, body=%wide.region_2.4_spmd.sunk | while | flops 1125251584 | bytes 57217216 | solution.py:67
  292.1 61.8 %while.57 = (s32[]{:T(128)}, bf16[4,512,4,64]{1,3,2,0:T(8,128)(2,1)}, f32[4,4,512]{2,1,0:T(4,128)S(1)}, s32[4]{0:T(128)S(1)}, bf16[2048,4,64]{0,2,1:T(8,128)(2,1...) while((s32[]{:T(128)}, ...), condition=%wide.region_5.5_spmd, body=%wide.region_2.4_spmd.sunk | while | flops 1125251584 | bytes 57217216 | solution.py:67
  376.2 20.7 %all-to-all-done.2 = bf16[2,2048,1,256]{3,0,2,1:T(2,128)(2,1)S(1)} async-done(((bf16[2,2048,1,256]{3,0,2,1:T(2,128)(2,1)}), bf16[2,2048,1,256]{3,0,2,1:T(2,128)(2,1)S(1)}, u32[]{:S(2)}, u32[]{:S(2)}) %all-to-all-start.2) | async-done | bytes 2097184 | tf_op jit(solution)/shard_map/all_to_all | solution.py:188
  449.1 21.8 %multiply_convert_fusion.1 = (bf16[1024,2816]{1,0:T(8,128)(2,1)}, bf16[1024,2816]{1,0:T(8,128)(2,1)}, bf16[1024,2816]{1,0:T(8,128)(2,1)}) fusion(f32[1024,2816]{1,0:T(8,128)} %fusion.62, f32[1024,2816]{1,0:T(8,128)} %fusion.63, bf16[1024,1024]{1,0:T(8,128)(2,1)S(1)} %copy-done.17, bf16[2816,1024]{1,0:T(8,128)(2,1)} %all-gather.20.cloned.1.call-done), kind=kOutput, calls=%fused_computation.59 | convolution fusion | flops 5948833792 | bytes 48234496 | tf_op jit(solution)/shard_map/rd,fd->rf/dot_general | solution.py:208
  506.5 25.6 %all-to-all-done.3 = bf16[2,512,4,256]{3,1,0,2:T(8,128)(2,1)S(1)} async-done(((bf16[2,512,4,256]{3,1,0,2:T(8,128)(2,1)}), bf16[2,512,4,256]{3,1,0,2:T(8,128)(2,1)S(1)}, u32[]{:S(2)}, u32[]{:S(2)}) %all-to-all-start.3) | async-done | bytes 2097184 | tf_op jit(solution)/shard_map/all_to_all | solution.py:260
  544.5 435.3 %while.56 = (s32[]{:T(128)}, bf16[2,2048,4,64]{1,3,2,0:T(8,128)(2,1)}, bf16[2,2048,4,64]{1,3,2,0:T(8,128)(2,1)}, bf16[2,2048,4,64]{1,3,2,0:T(8,128)(2,1)}, bf16[...) while((s32[]{:T(128)}, ...), condition=%wide.region_14.15_spmd, body=%wide.region_10.14_spmd.sunk | while | flops 2752117248 | bytes 206435024 | solution.py:121
  554.7 195.9 %while.58 = (s32[]{:T(128)}, f32[2048,4,64]{0,2,1:T(8,128)}, f32[2048,4,64]{0,2,1:T(8,128)}, bf16[4,512,4,64]{1,3,2,0:T(8,128)(2,1)}, s32[4]{0:T(128)S(1)}, /*in...) while((s32[]{:T(128)}, f32[2048,4,64]{0,2,1:T(8,128)}, ...), condition=%wide.region_13.13_spmd.clone, body=%wide.region_11.12_spmd.clone.sunk | while | flops 2751068672 | bytes 177009008 | solution.py:111
  772.1 195.9 %while.58 = (s32[]{:T(128)}, f32[2048,4,64]{0,2,1:T(8,128)}, f32[2048,4,64]{0,2,1:T(8,128)}, bf16[4,512,4,64]{1,3,2,0:T(8,128)(2,1)}, s32[4]{0:T(128)S(1)}, /*in...) while((s32[]{:T(128)}, f32[2048,4,64]{0,2,1:T(8,128)}, ...), condition=%wide.region_13.13_spmd.clone, body=%wide.region_11.12_spmd.clone.sunk | while | flops 2751068672 | bytes 177009008 | solution.py:111
  1032.2 17.7 all-to-all-done.5
  1129.3 66.1 %reduce-scatter.21.cloned.1.call-done = bf16[128,512]{1,0:T(8,128)(2,1)} async-done(((bf16[1024,512]{1,0:T(8,128)(2,1)}), bf16[128,512]{1,0:T(8,128)(2,1)}) %reduce-scatter.21.cloned.1.call-update) | async-done | bytes 131088 | tf_op jit(solution)/shard_map/reduce_scatter | solution.py:308
  1195.4 71.0 %reduce-scatter.17.cloned.1.call-done = bf16[128,1024]{1,0:T(8,128)(2,1)} async-done(((bf16[1024,1024]{1,0:T(8,128)(2,1)}), bf16[128,1024]{1,0:T(8,128)(2,1)}) %reduce-scatter.17.cloned.1.call-update) | async-done | bytes 262160 | tf_op jit(solution)/shard_map/reduce_scatter | solution.py:305
  1266.5 112.4 %reduce-scatter.35.cloned.1.call-done = bf16[128,2816]{1,0:T(8,128)(2,1)} async-done(((bf16[1024,2816]{1,0:T(8,128)(2,1)}), bf16[128,2816]{1,0:T(8,128)(2,1)}) %reduce-scatter.35.cloned.1.call-update) | async-done | bytes 720912 | tf_op jit(solution)/shard_map/reduce_scatter | solution.py:231
  1381.5 110.9 %reduce-scatter.31.cloned.1.call-done = bf16[128,2816]{1,0:T(8,128)(2,1)} async-done(((bf16[1024,2816]{1,0:T(8,128)(2,1)}), bf16[128,2816]{1,0:T(8,128)(2,1)}) %reduce-scatter.31.cloned.1.call-update) | async-done | bytes 720912 | tf_op jit(solution)/shard_map/reduce_scatter | solution.py:228
  1508.7 97.0 %reduce-scatter.39.cloned.1.call-done = bf16[352,1024]{1,0:T(8,128)(2,1)} async-done(((bf16[2816,1024]{1,0:T(8,128)(2,1)}), bf16[352,1024]{1,0:T(8,128)(2,1)}) %reduce-scatter.39.cloned.1.call-update) | async-done | bytes 720912 | tf_op jit(solution)/shard_map/reduce_scatter | solution.py:234
  1612.0 20.2 %all-reduce.7 = (bf16[1024]{0:T(1024)(128)(2,1)S(1)}, bf16[1024]{0:T(1024)(128)(2,1)S(1)}) all-reduce(bf16[1024]{0:T(1024)(128)(2,1)S(1)} %get-tuple-element.294, bf16[1024]{0:T(1024)(128)(2,1)S(1)} %copy-done.31), channel_id=2, replica_groups=mesh['dp'=8,'sp'=4] {'dp'}, use_global_device_ids=true, to_apply=%region_18.19.clone | all-reduce | flops 2048 | bytes 8192
  1652.0 20.4 %reduce-scatter.23.cloned.1.call-done = bf16[32,512]{1,0:T(8,128)(2,1)} async-done(((bf16[128,512]{1,0:T(8,128)(2,1)}), bf16[32,512]{1,0:T(8,128)(2,1)}) %reduce-scatter.23.cloned.1.call-update) | async-done | bytes 32784 | tf_op jit(solution)/shard_map/reduce_scatter | solution.py:325
  1673.7 21.1 %reduce-scatter.19.cloned.1.call-done = bf16[32,1024]{1,0:T(8,128)(2,1)} async-done(((bf16[128,1024]{1,0:T(8,128)(2,1)}), bf16[32,1024]{1,0:T(8,128)(2,1)}) %reduce-scatter.19.cloned.1.call-update) | async-done | bytes 65552 | tf_op jit(solution)/shard_map/reduce_scatter | solution.py:322
  1696.3 23.9 %reduce-scatter.37.cloned.1.call-done = bf16[32,2816]{1,0:T(8,128)(2,1)} async-done(((bf16[128,2816]{1,0:T(8,128)(2,1)}), bf16[32,2816]{1,0:T(8,128)(2,1)}) %reduce-scatter.37.cloned.1.call-update) | async-done | bytes 180240 | tf_op jit(solution)/shard_map/reduce_scatter | solution.py:245
  1721.9 23.7 %reduce-scatter.33.cloned.1.call-done = bf16[32,2816]{1,0:T(8,128)(2,1)} async-done(((bf16[128,2816]{1,0:T(8,128)(2,1)}), bf16[32,2816]{1,0:T(8,128)(2,1)}) %reduce-scatter.33.cloned.1.call-update) | async-done | bytes 180240 | tf_op jit(solution)/shard_map/reduce_scatter | solution.py:242
  1747.3 23.7 %reduce-scatter.41.cloned.1.call-done = bf16[88,1024]{1,0:T(8,128)(2,1)} async-done(((bf16[352,1024]{1,0:T(8,128)(2,1)}), bf16[88,1024]{1,0:T(8,128)(2,1)}) %reduce-scatter.41.cloned.1.call-update) | async-done | bytes 180240 | tf_op jit(solution)/shard_map/reduce_scatter | solution.py:248
  (456 shorter events, 930.6 us)
Async XLA Ops:
  7.2 60.1 %all-gather.10.cloned.1.call-start = ((), (), s32[]{:S(2)}) async-start(), calls=%async_computation.21 | async-start | bytes 1081344 | tf_op jit(solution)/shard_map/all_gather | solution.py:148
  7.9 119.1 %all-gather.8.cloned.1.call-start = ((), (), s32[]{:S(2)}) async-start(), calls=%async_computation.20 | async-start | bytes 2162688 | tf_op jit(solution)/shard_map/all_gather | solution.py:147
  8.7 174.3 %all-gather.12.cloned.1.call-start = ((), (), s32[]{:S(2)}) async-start(), calls=%async_computation.22 | async-start | bytes 1081344 | tf_op jit(solution)/shard_map/all_gather | solution.py:149
  9.4 394.0 %all-gather.14.cloned.1.call-start = ((), (), s32[]{:S(2)}) async-start(), calls=%async_computation.23 | async-start | bytes 2162688 | tf_op jit(solution)/shard_map/all_gather | solution.py:150
  10.0 400.7 %all-gather.18.cloned.1.call-start = ((), (), s32[]{:S(2)}) async-start(), calls=%async_computation.25 | async-start | bytes 5947392 | tf_op jit(solution)/shard_map/all_gather | solution.py:155
  10.6 412.9 %all-gather.16.cloned.1.call-start = ((), (), s32[]{:S(2)}) async-start(), calls=%async_computation.24 | async-start | bytes 5947392 | tf_op jit(solution)/shard_map/all_gather | solution.py:154
  71.7 68.8 %all-to-all-start.1 = ((bf16[2,512,4,256]{3,1,0,2:T(8,128)(2,1)}), bf16[2,512,4,256]{3,1,0,2:T(8,128)(2,1)S(1)}, u32[]{:S(2)}, u32[]{:S(2)}) async-start(bf16[2,512,4,256]{3,1,0,2:T(8,128)(2,1)} %bitcast.261), calls=%async_computation.1 | async-start | bytes 4194304 | tf_op jit(solution)/shard_map/all_to_all | solution.py:175
  140.5 70.2 %all-to-all-start = ((bf16[2,512,4,256]{3,1,0,2:T(8,128)(2,1)}), bf16[2,512,4,256]{3,1,0,2:T(8,128)(2,1)}, u32[]{:S(2)}, u32[]{:S(2)}) async-start(bf16[2,512,4,256]{3,1,0,2:T(8,128)(2,1)} %copy.102), calls=%async_computation | async-start | bytes 4194304 | tf_op jit(solution)/shard_map/all_to_all | solution.py:174
  145.0 304.1 %all-gather.20.cloned.1.call-start = ((), (), s32[]{:S(2)}) async-start(), calls=%async_computation.26 | async-start | bytes 5947392 | tf_op jit(solution)/shard_map/all_gather | solution.py:156
  366.0 31.0 %all-to-all-start.2 = ((bf16[2,2048,1,256]{3,0,2,1:T(2,128)(2,1)}), bf16[2,2048,1,256]{3,0,2,1:T(2,128)(2,1)S(1)}, u32[]{:S(2)}, u32[]{:S(2)}) async-start(bf16[2,2048,1,256]{3,0,2,1:T(2,128)(2,1)} %copy.110), calls=%async_computation.2 | async-start | bytes 4194304 | tf_op jit(solution)/shard_map/all_to_all | solution.py:188
  506.4 616.3 %reduce-scatter.25.cloned.1.call-start = ((), (), s32[]{:S(2)}) async-start(), calls=%async_computation.31 | async-start | bytes 1179648 | tf_op jit(solution)/shard_map/reduce_scatter | solution.py:311
  995.9 133.3 %reduce-scatter.27.cloned.1.call-start = ((), (), s32[]{:S(2)}) async-start(), calls=%async_computation.32 | async-start | bytes 2359296 | tf_op jit(solution)/shard_map/reduce_scatter | solution.py:314
  1054.3 141.0 %reduce-scatter.21.cloned.1.call-start = ((), (), s32[]{:S(2)}) async-start(), calls=%async_computation.29 | async-start | bytes 1179648 | tf_op jit(solution)/shard_map/reduce_scatter | solution.py:308
  1063.5 202.9 %reduce-scatter.17.cloned.1.call-start = ((), (), s32[]{:S(2)}) async-start(), calls=%async_computation.27 | async-start | bytes 2359296 | tf_op jit(solution)/shard_map/reduce_scatter | solution.py:305
  1089.1 289.8 %reduce-scatter.35.cloned.1.call-start = ((), (), s32[]{:S(2)}) async-start(), calls=%async_computation.36 | async-start | bytes 6488064 | tf_op jit(solution)/shard_map/reduce_scatter | solution.py:231
  1100.4 392.0 %reduce-scatter.31.cloned.1.call-start = ((), (), s32[]{:S(2)}) async-start(), calls=%async_computation.34 | async-start | bytes 6488064 | tf_op jit(solution)/shard_map/reduce_scatter | solution.py:228
  1111.5 494.2 %reduce-scatter.39.cloned.1.call-start = ((), (), s32[]{:S(2)}) async-start(), calls=%async_computation.38 | async-start | bytes 6488064 | tf_op jit(solution)/shard_map/reduce_scatter | solution.py:234
  1122.7 521.0 %reduce-scatter.43.cloned.1.call-start = ((), (), s32[]{:S(2)}) async-start(), calls=%async_computation.40 | async-start | bytes 163840
  1124.5 526.0 %reduce-scatter.29.cloned.1.call-start = ((), (), s32[]{:S(2)}) async-start(), calls=%async_computation.33 | async-start | bytes 327680 | tf_op jit(solution)/shard_map/reduce_scatter | solution.py:331
  1129.2 543.1 %reduce-scatter.23.cloned.1.call-start = ((), (), s32[]{:S(2)}) async-start(), calls=%async_computation.30 | async-start | bytes 163840 | tf_op jit(solution)/shard_map/reduce_scatter | solution.py:325
  1195.4 499.5 %reduce-scatter.19.cloned.1.call-start = ((), (), s32[]{:S(2)}) async-start(), calls=%async_computation.28 | async-start | bytes 327680 | tf_op jit(solution)/shard_map/reduce_scatter | solution.py:322
  1266.4 453.8 %reduce-scatter.37.cloned.1.call-start = ((), (), s32[]{:S(2)}) async-start(), calls=%async_computation.37 | async-start | bytes 901120 | tf_op jit(solution)/shard_map/reduce_scatter | solution.py:245
  1378.9 366.7 %reduce-scatter.33.cloned.1.call-start = ((), (), s32[]{:S(2)}) async-start(), calls=%async_computation.35 | async-start | bytes 901120 | tf_op jit(solution)/shard_map/reduce_scatter | solution.py:242
  1492.4 278.7 %reduce-scatter.41.cloned.1.call-start = ((), (), s32[]{:S(2)}) async-start(), calls=%async_computation.39 | async-start | bytes 901120 | tf_op jit(solution)/shard_map/reduce_scatter | solution.py:248
  (64 other events, 1264.2 us)
Sparse Core Ops, SparseCore 0:
  10.9 56.4 all-gather.9
  70.2 56.7 all-gather.7
  129.9 52.9 all-gather.11
  185.6 55.3 all-gather.13
  243.7 66.1 all-gather.17
  312.6 66.2 all-gather.15
  381.8 67.2 all-gather.19
  996.1 62.4 reduce-scatter.24
  1062.5 66.7 reduce-scatter.26
  1132.8 62.4 reduce-scatter.20
  1199.5 66.8 reduce-scatter.16
  1269.9 108.9 reduce-scatter.34
  1382.5 109.7 reduce-scatter.30
  1495.8 109.7 reduce-scatter.38
  1608.5 19.3 reduce-scatter.42
  1630.4 19.9 reduce-scatter.28
  1652.7 19.5 reduce-scatter.22
  1674.8 20.0 reduce-scatter.18
  1697.4 22.8 reduce-scatter.36
  1722.8 22.8 reduce-scatter.32
  1748.2 22.8 reduce-scatter.40
where the time goes:
time: 1790 us; the launch traced here: 1780 us
  waiting for transfers between devices  773 us (43%)
  matrix products  505 us (28%)
  local copies, waits for them, and re-layouts  189 us (11%)
  other arithmetic  175 us (10%)
  blocking collectives  67.9 us (4%)
  loops' own time  27.3 us (2%)
  starting transfers between devices  26.4 us (1%)
    reduce_scatter x1, waiting for transfers between devices, local(): lax.psum_scatter(up_grad.astype(jnp.bfloat16), 'dp', scatter_dimension=0,...  112 us
    reduce_scatter x1, waiting for transfers between devices, local(): lax.psum_scatter(gate_grad.astype(jnp.bfloat16), 'dp', scatter_dimension=...  111 us
    reduce_scatter x1, waiting for transfers between devices, local(): lax.psum_scatter(down_grad.astype(jnp.bfloat16), 'dp', scatter_dimension=...  97 us
    dot_general x8, matrix products, one_block(): jnp.einsum('qhd,khd->hqk', upstream_block, seq_values, preferred_element_...  90.9 us
    convert_element_type x8, other arithmetic, one_block(): score_back = (probabilities * (prob_back - center)).astype(jnp.bfloat16)  87.1 us
    reduce_scatter x1, waiting for transfers between devices, local(): lax.psum_scatter(query_grad.astype(jnp.bfloat16), 'dp', scatter_dimension...  71 us
    unnamed x3, blocking collectives  67.9 us
    reduce_scatter x1, waiting for transfers between devices, local(): lax.psum_scatter(latent_grad.astype(jnp.bfloat16), 'dp', scatter_dimensio...  66.1 us
  transfers between devices with their start and end apart: 27, of which 20 were waited for; matrix products, arithmetic and copies ran while one was open for 20% of the time, Pallas kernels for 0%

commit v1 on v0

v1 whole, which is shorter than its diff:
```python
import functools
import jax
import jax.numpy as jnp
from jax import lax
from jax.sharding import Mesh
from jax.sharding import PartitionSpec as P
from jax.experimental import pallas as pl
from jax.experimental.pallas import tpu as pltpu

DH = 64
F32 = jnp.float32
BF = jnp.bfloat16


def low_half(x):
    return jnp.concatenate([x[:, :DH], jnp.zeros((x.shape[0], DH), x.dtype)], axis=1)


def dot_nt(a, b):
    return lax.dot_general(a, b, (((1,), (1,)), ((), ())), preferred_element_type=F32)


def dot_nn(a, b):
    return lax.dot_general(a, b, (((1,), (0,)), ((), ())), preferred_element_type=F32)


def causal(s, first_key, first_query):
    keys = first_key + lax.broadcasted_iota(jnp.int32, s.shape, 0)
    rows = first_query + lax.broadcasted_iota(jnp.int32, s.shape, 1)
    return jnp.where(rows >= keys, s, -1e30)


def forward_kernel(q_ref, kv_ref, o_ref, lse_ref, vt_s):
    groups, chunks, rows, _ = q_ref.shape
    seq = kv_ref.shape[0]
    for h in range(2):
        vt_s[h] = kv_ref[:, h * 128 : (h + 1) * 128].astype(F32).T[DH:].astype(BF)
    for i in range(groups * chunks):
        q = q_ref[i % groups, i // groups].astype(F32) * 0.125
        outs = []
        for h in range(2):
            qh = q[:, h * DH : (h + 1) * DH]
            qp = jnp.concatenate([qh, jnp.zeros_like(qh)], axis=1).astype(BF)
            width = (i + 1) * rows
            s = dot_nt(kv_ref[0:width, h * 128 : (h + 1) * 128], qp)
            tail = causal(s[i * rows :], 0, 0)
            if i > 0:
                head = s[: i * rows]
                top = jnp.maximum(
                    jnp.max(head, axis=0, keepdims=True), jnp.max(tail, axis=0, keepdims=True)
                )
                ph = jnp.exp(head - top)
                pt = jnp.exp(tail - top)
                total = jnp.sum(ph, axis=0, keepdims=True) + jnp.sum(pt, axis=0, keepdims=True)
                o = dot_nn(vt_s[h, :, 0 : i * rows], ph.astype(BF)) + dot_nn(
                    vt_s[h, :, i * rows : width], pt.astype(BF)
                )
            else:
                top = jnp.max(tail, axis=0, keepdims=True)
                pt = jnp.exp(tail - top)
                total = jnp.sum(pt, axis=0, keepdims=True)
                o = dot_nn(vt_s[h, :, 0:width], pt.astype(BF))
            outs.append(o / total)
            lse_ref[h, i * rows : (i + 1) * rows] = (top + jnp.log(total))[0]
        o_ref[i % groups, i // groups] = jnp.concatenate(outs, axis=0).T.astype(BF)


def attention_forward(q, kv):
    groups, chunks, rows, cols = q.shape
    seq = kv.shape[0]
    pairs = cols // 128
    return pl.pallas_call(
        forward_kernel,
        grid=(pairs,),
        in_specs=[
            pl.BlockSpec((groups, chunks, rows, 128), lambda p: (0, 0, 0, p)),
            pl.BlockSpec((seq, 256), lambda p: (0, p)),
        ],
        out_specs=[
            pl.BlockSpec((groups, chunks, rows, 128), lambda p: (0, 0, 0, p)),
            pl.BlockSpec((None, 2, seq), lambda p: (p, 0, 0)),
        ],
        out_shape=[
            jax.ShapeDtypeStruct(q.shape, BF),
            jax.ShapeDtypeStruct((pairs, 2, seq), F32),
        ],
        scratch_shapes=[pltpu.VMEM((2, DH, seq), BF)],
        compiler_params=pltpu.CompilerParams(vmem_limit_bytes=56 * 2**20),
    )(q, kv)


def backward_kernel(blk, q_ref, kv_ref, do_ref, o_ref, lse_ref, dq_ref, dkv_ref,
                    kt_s, acc_s, dqt_s, qp_s, dop_s, delta_s):
    groups, chunks, rows, _ = q_ref.shape
    seq = kv_ref.shape[0]
    n = groups * chunks
    for h in range(2):
        kt_s[h] = kv_ref[:, h * 128 : (h + 1) * 128].astype(F32).T[:DH].astype(BF)
    acc_s[...] = jnp.zeros_like(acc_s)
    for i in range(n):
        at = pl.ds(i * rows, rows)
        q = q_ref[i % groups, i // groups].astype(F32) * 0.125
        do = do_ref[i % groups, i // groups].astype(F32)
        o = o_ref[i % groups, i // groups].astype(F32)
        prod = (do * o).T
        zero = jnp.zeros((rows, DH), F32)
        for h in range(2):
            cut = slice(h * DH, (h + 1) * DH)
            qp_s[h, at] = jnp.concatenate([q[:, cut], zero], axis=1).astype(BF)
            dop_s[h, at] = jnp.concatenate([zero, do[:, cut]], axis=1).astype(BF)
            delta_s[h, at] = jnp.sum(prod[cut], axis=0)

    def block(i, j, masked):
        qat = pl.ds(pl.multiple_of(i * blk, blk), blk)
        kat = pl.ds(pl.multiple_of(j * blk, blk), blk)
        for h in range(2):
            kv = kv_ref[kat, h * 128 : (h + 1) * 128]
            qp = qp_s[h, qat]
            dop = dop_s[h, qat]
            s = dot_nt(kv, qp)
            dp = dot_nt(kv, dop)
            if masked:
                s = causal(s, 0, 0)
            p = jnp.exp(s - lse_ref[h : h + 1, qat])
            ds = (p * (dp - delta_s[h : h + 1, qat])).astype(BF)
            acc_s[h, kat] += dot_nn(p.astype(BF), dop) + dot_nn(ds, qp)
            part = dot_nn(kt_s[h, :, kat], ds)
            if masked:
                dqt_s[h * DH : (h + 1) * DH, qat] = part
            else:
                dqt_s[h * DH : (h + 1) * DH, qat] += part

    m = seq // blk

    def outer(i, _):
        block(i, i, True)

        def inner(j, _):
            block(i, j, False)
            return 0

        lax.fori_loop(0, i, inner, 0)
        return 0

    lax.fori_loop(0, m, outer, 0)
    for i in range(n):
        at = pl.ds(i * rows, rows)
        dq_ref[i % groups, i // groups] = (dqt_s[:, at].T * 0.125).astype(BF)
    for h in range(2):
        dkv_ref[:, h * 128 : (h + 1) * 128] = acc_s[h].astype(BF)


def attention_backward(q, kv, do, o, lse, blk=512):
    groups, chunks, rows, cols = q.shape
    seq = kv.shape[0]
    pairs = cols // 128
    tok = pl.BlockSpec((groups, chunks, rows, 128), lambda p: (0, 0, 0, p))
    return pl.pallas_call(
        functools.partial(backward_kernel, blk),
        grid=(pairs,),
        in_specs=[tok, pl.BlockSpec((seq, 256), lambda p: (0, p)), tok, tok,
                  pl.BlockSpec((None, 2, seq), lambda p: (p, 0, 0))],
        out_specs=[tok, pl.BlockSpec((seq, 256), lambda p: (0, p))],
        out_shape=[jax.ShapeDtypeStruct(q.shape, BF), jax.ShapeDtypeStruct(kv.shape, BF)],
        scratch_shapes=[
            pltpu.VMEM((2, DH, seq), BF),
            pltpu.VMEM((2, seq, 128), F32),
            pltpu.VMEM((128, seq), F32),
            pltpu.VMEM((2, seq, 128), BF),
            pltpu.VMEM((2, seq, 128), BF),
            pltpu.VMEM((2, seq), F32),
        ],
        compiler_params=pltpu.CompilerParams(vmem_limit_bytes=56 * 2**20),
    )(q, kv, do, o, lse)


HEADS = 16
KVH = 2
LATD = 256
HG = 8
GROUPS = 8
EPSILON = 1e-05
ALL = ("dp", "seq", "grp")


def norm_parts(values, gain):
    inverse = lax.rsqrt(jnp.mean(values * values, axis=-1, keepdims=True) + EPSILON)
    return (values * inverse * gain, inverse)


def norm_back(values, inverse, gain, upstream):
    scaled = upstream * gain
    gain_grad = jnp.sum(upstream * values * inverse, axis=0)
    input_part = inverse * scaled - values * inverse**3 * jnp.mean(
        scaled * values, axis=-1, keepdims=True
    )
    return (input_part, gain_grad)


def dot_tn(a, b):
    return lax.dot_general(a, b, (((0,), (0,)), ((), ())), preferred_element_type=F32)


def swap_sequences(blocks, count):
    if count == 2:
        me = lax.axis_index("seq")
        sent = lax.ppermute(blocks[1 - me], "seq", [(0, 1), (1, 0)])
        kept = blocks[me]
        first = me == 0
        return jnp.stack([jnp.where(first, kept, sent), jnp.where(first, sent, kept)])
    return lax.all_to_all(blocks, "seq", 0, 0, tiled=True)


def swap_group(blocks):
    return lax.all_to_all(blocks, "grp", 0, 0, tiled=True)


def local(
    inputs,
    cotangent,
    group_ids,
    group_scale,
    norm_gain,
    w_query,
    w_latent,
    expansion_weight,
    w_output,
    ffn_gain,
    w_gate,
    w_up,
    w_down,
):
    devices = lax.axis_size("dp") * lax.axis_size("seq") * lax.axis_size("grp")
    groups = lax.axis_size("grp")
    me = lax.axis_index("grp")
    seqs, rows, width = inputs.shape
    count = seqs * rows
    hidden_size = w_gate.shape[1]
    heads = HEADS // groups
    cols = heads * DH
    drows = width // devices

    gains = jnp.concatenate(
        [norm_gain[:, None], ffn_gain[:, None], jnp.zeros((drows, 126), BF)], axis=1
    )
    expand_rows = expansion_weight.reshape(drows, -1)
    attn_weights = jnp.concatenate([w_query, w_latent, w_output, expand_rows, gains], axis=1)
    attn_full = lax.all_gather(attn_weights, ALL, axis=0, tiled=True)
    ffn_full = lax.all_gather(jnp.concatenate([w_gate, w_up], axis=1), ALL, axis=0, tiled=True)
    down_full = lax.all_gather(w_down, ALL, axis=0, tiled=True)
    query_full = attn_full[:, :width]
    latent_full = attn_full[:, width : width + KVH * LATD]
    output_full = attn_full[:, width + KVH * LATD : 2 * width + KVH * LATD]
    ecols = expand_rows.shape[1]
    at = 2 * width + KVH * LATD
    expand_full = attn_full[:, at : at + ecols].reshape(devices, KVH, LATD // devices, -1)
    expand_full = expand_full.transpose(1, 0, 2, 3).reshape(KVH, LATD, -1)
    gain_one = attn_full[:, at + ecols].astype(F32)
    gain_two = attn_full[:, at + ecols + 1].astype(F32)
    gate_full = ffn_full[:, :hidden_size]
    up_full = ffn_full[:, hidden_size:]

    own_inputs = swap_sequences(inputs, seqs)
    own_cotangent = swap_sequences(cotangent, seqs)

    token_rows = own_inputs.astype(F32).reshape(count, width)
    normed, inverse_one = norm_parts(token_rows, gain_one)
    normed_low = normed.astype(BF)
    query_send = jnp.stack(
        [dot_nn(normed_low, query_full[:, j * cols : (j + 1) * cols]).astype(BF) for j in range(groups)]
    ).reshape(groups, seqs, rows, cols)
    latent_state = [
        dot_nn(normed_low, latent_full[:, g * LATD : (g + 1) * LATD]).astype(BF) for g in range(KVH)
    ]
    latent_send = jnp.stack([latent_state[j * heads // HG] for j in range(groups)]).reshape(
        groups, seqs, rows, LATD
    )
    head_queries = swap_group(query_send)
    head_latent = swap_group(latent_send).transpose(1, 0, 2, 3).reshape(-1, LATD)
    expand_local = lax.dynamic_slice(
        expand_full, (me * heads // HG, 0, me * heads % HG * 2 * DH), (1, LATD, heads * 2 * DH)
    )[0]
    head_pairs = dot_nn(head_latent, expand_local).astype(BF)
    attended, logsum = attention_forward(head_queries, head_pairs)
    token_attended = swap_group(attended).reshape(groups, count, cols)
    branch = sum(
        dot_nn(token_attended[j], output_full[j * cols : (j + 1) * cols]) for j in range(groups)
    )
    middle = token_rows + branch
    normed_two, inverse_two = norm_parts(middle, gain_two)
    normed_two_low = normed_two.astype(BF)
    gate_pre = dot_nn(normed_two_low, gate_full)
    upward = dot_nn(normed_two_low, up_full)
    sigmoid = jax.nn.sigmoid(gate_pre)
    activated = gate_pre * sigmoid
    hidden = (activated * upward).astype(BF)
    result = middle + dot_nn(hidden, down_full)
    output = swap_sequences(result.astype(BF).reshape(seqs, rows, width), seqs)

    seq_group = lax.dynamic_index_in_dim(group_ids, lax.axis_index("seq"), 0, keepdims=False)
    chosen = (seq_group == jnp.arange(GROUPS)).astype(F32)
    seq_scale = jnp.sum(chosen * group_scale)
    upstream = own_cotangent.astype(F32).reshape(count, width) * seq_scale
    upstream_low = upstream.astype(BF)
    down_grad = dot_tn(hidden, upstream_low)
    hidden_back = dot_nt(upstream_low, down_full)
    gate_back = (hidden_back * upward * sigmoid * (1.0 + gate_pre * (1.0 - sigmoid))).astype(BF)
    up_back = (hidden_back * activated).astype(BF)
    gate_grad = dot_tn(normed_two_low, gate_back)
    up_grad = dot_tn(normed_two_low, up_back)
    normed_two_back = dot_nt(gate_back, gate_full) + dot_nt(up_back, up_full)
    middle_part, gain_two_grad = norm_back(middle, inverse_two, gain_two, normed_two_back)
    middle_grad = upstream + middle_part
    ffn_share = lax.psum_scatter(
        jnp.concatenate([gate_grad.astype(BF), up_grad.astype(BF)], axis=1),
        ALL,
        scatter_dimension=0,
        tiled=True,
    ).astype(F32)
    down_share = lax.psum_scatter(
        down_grad.astype(BF), ALL, scatter_dimension=0, tiled=True
    ).astype(F32)

    branch_low = middle_grad.astype(BF)
    output_grad = jnp.concatenate(
        [dot_tn(token_attended[j], branch_low) for j in range(groups)], axis=0
    )
    back_send = jnp.stack(
        [
            dot_nt(branch_low, output_full[j * cols : (j + 1) * cols]).astype(BF)
            for j in range(groups)
        ]
    ).reshape(groups, seqs, rows, cols)
    head_upstream = swap_group(back_send)
    query_back, pair_back = attention_backward(
        head_queries, head_pairs, head_upstream, attended, logsum
    )
    latent_terms = dot_nt(pair_back, expand_local).astype(BF)
    expand_part = dot_tn(head_latent, pair_back)
    expand_grad = lax.dynamic_update_slice(
        jnp.zeros(expand_full.shape, F32),
        expand_part[None],
        (me * heads // HG, 0, me * heads % HG * 2 * DH),
    )
    query_token = swap_group(query_back).reshape(groups, count, cols)
    latent_token = swap_group(
        latent_terms.reshape(seqs, groups, rows, LATD).transpose(1, 0, 2, 3)
    ).reshape(KVH, groups // KVH, count, LATD)
    latent_token = jnp.sum(latent_token.astype(F32), axis=1).astype(BF)
    query_grad = jnp.concatenate([dot_tn(normed_low, query_token[j]) for j in range(groups)], axis=1)
    latent_grad = jnp.concatenate([dot_tn(normed_low, latent_token[g]) for g in range(KVH)], axis=1)
    normed_back = sum(
        dot_nt(query_token[j], query_full[:, j * cols : (j + 1) * cols]) for j in range(groups)
    ) + sum(
        dot_nt(latent_token[g], latent_full[:, g * LATD : (g + 1) * LATD]) for g in range(KVH)
    )
    input_part, gain_one_grad = norm_back(token_rows, inverse_one, gain_one, normed_back)
    input_grad = swap_sequences(
        (middle_grad + input_part).astype(BF).reshape(seqs, rows, width), seqs
    )
    expand_out = (
        expand_grad.astype(BF)
        .reshape(KVH, devices, LATD // devices, -1)
        .transpose(1, 0, 2, 3)
        .reshape(width, -1)
    )
    gain_grads = jnp.concatenate(
        [gain_one_grad[:, None], gain_two_grad[:, None], jnp.zeros((width, 126), F32)], axis=1
    )
    attn_share = lax.psum_scatter(
        jnp.concatenate(
            [
                query_grad.astype(BF),
                latent_grad.astype(BF),
                output_grad.astype(BF),
                expand_out,
                gain_grads.astype(BF),
            ],
            axis=1,
        ),
        ALL,
        scatter_dimension=0,
        tiled=True,
    ).astype(F32)
    return (
        output,
        input_grad,
        attn_share[:, at + ecols],
        attn_share[:, :width],
        attn_share[:, width : width + KVH * LATD],
        attn_share[:, at : at + ecols].reshape(expansion_weight.shape),
        attn_share[:, width + KVH * LATD : at],
        attn_share[:, at + ecols + 1],
        ffn_share[:, :hidden_size],
        ffn_share[:, hidden_size:],
        down_share,
    )


def solution(mesh):
    def run(*arrays):
        dp, sp = mesh.shape["dp"], mesh.shape["sp"]
        seqs = arrays[0].shape[0] // dp
        grid = Mesh(mesh.devices.reshape(dp, seqs, sp // seqs), ALL)
        tokens = P("dp", ("seq", "grp"), None)
        matrix = P(ALL, None)
        expand = P(None, ALL, None)
        return jax.shard_map(
            local,
            mesh=grid,
            in_specs=(
                tokens,
                tokens,
                P("dp"),
                P(),
                P(ALL),
                matrix,
                matrix,
                expand,
                matrix,
                P(ALL),
                matrix,
                matrix,
                matrix,
            ),
            out_specs=(
                tokens,
                tokens,
                P(ALL),
                matrix,
                matrix,
                expand,
                matrix,
                P(ALL),
                matrix,
                matrix,
                matrix,
            ),
            check_vma=False,
        )(*arrays)

    return run
```

time: 1790 us -> 783 us (0.44)
  waiting for transfers between devices: 773 us -> 374 us
  matrix products: 505 us -> 162 us
  local copies, waits for them, and re-layouts: 189 us -> 49.3 us
  other arithmetic: 175 us -> 40.3 us
  Pallas kernels: 0 us -> 97.9 us
  blocking collectives: 67.9 us -> 17.8 us
  loops' own time: 27.3 us -> 0 us
    reduce_scatter x13 -> x3, waiting for transfers between devices: 580 us -> 167 us  [the longest x1 148 us: local(): lax.psum_scatter(jnp.concatenate([gate_grad.astype(BF), up_grad.astype(BF...]
    dot_general x77 -> x30, matrix products: 505 us -> 162 us  [the longest x10 63.9 us: dot_nt(): lax.dot_general(a, b, (((1,), (1,)), ((), ())), preferred_element_type=F32)]
    ppermute x0 -> x4, waiting for transfers between devices: none -> 132 us  [swap_sequences(): sent = lax.ppermute(blocks[1 - me], 'seq', [(0, 1), (1, 0)])]
    pallas_call x0 -> x2, Pallas kernels: none -> 97.9 us  [the longest x1 66 us: attention_backward(): pl.pallas_call(functools.partial(backward_kernel, blk), grid=(pairs,), in...]
    convert_element_type x23 -> x9, other arithmetic: 109 us -> 17.9 us  [the longest x1 4.53 us: local(): (middle_grad + input_part).astype(BF).reshape(seqs, rows, width)]
    all_to_all x6 -> x3, waiting for transfers between devices: 80.6 us -> 1.84 us  [swap_group(): return lax.all_to_all(blocks, 'grp', 0, 0, tiled=True)]
    unnamed x3 -> x0, blocking collectives: 67.9 us -> none
    all_gather x7 -> x3, waiting for transfers between devices: 108 us -> 72.6 us  [the longest x1 47.9 us: local(): down_full = lax.all_gather(w_down, ALL, axis=0, tiled=True)]
  transfers between devices with their start and end apart: 27 -> 13, of which waited for: 20 -> 10; matrix products, arithmetic and copies ran while one was open for 20% -> 27% of each run, Pallas kernels for 0% -> 13%
where the time goes in v1:
time: 783 us; the launch traced here: 776 us
  waiting for transfers between devices  374 us (48%)
  matrix products  162 us (21%)
  Pallas kernels  97.9 us (13%)
  local copies, waits for them, and re-layouts  49.3 us (6%)
  other arithmetic  40.3 us (5%)
  starting transfers between devices  18.9 us (2%)
  blocking collectives  17.8 us (2%)
  between operations  15.2 us (2%)
    reduce_scatter x1, waiting for transfers between devices, local(): lax.psum_scatter(jnp.concatenate([gate_grad.astype(BF), up_grad.astype(BF...  148 us
    ppermute x4, waiting for transfers between devices, swap_sequences(): sent = lax.ppermute(blocks[1 - me], 'seq', [(0, 1), (1, 0)])  132 us
    pallas_call x1, Pallas kernels, attention_backward(): pl.pallas_call(functools.partial(backward_kernel, blk), grid=(pairs,), in...  66 us
    dot_general x10, matrix products, dot_nt(): lax.dot_general(a, b, (((1,), (1,)), ((), ())), preferred_element_type=F32)  63.9 us
    dot_general x10, matrix products, dot_nn(): lax.dot_general(a, b, (((1,), (0,)), ((), ())), preferred_element_type=F32)  49.4 us
    dot_general x10, matrix products, dot_tn(): lax.dot_general(a, b, (((0,), (0,)), ((), ())), preferred_element_type=F32)  49 us
    all_gather x1, waiting for transfers between devices, local(): down_full = lax.all_gather(w_down, ALL, axis=0, tiled=True)  47.9 us
    pallas_call x1, Pallas kernels, attention_forward(): pl.pallas_call(forward_kernel, grid=(pairs,), in_specs=[pl.BlockSpec((gro...  31.9 us
  transfers between devices with their start and end apart: 13, of which 10 were waited for; matrix products, arithmetic and copies ran while one was open for 27% of the time, Pallas kernels for 13%

profile of v1, /device:TPU:0, one launch (start us, length us, event | category | flops | bytes accessed | tf_op | source)
XLA Modules:
  0.0 775.5 jit_solution(3832714614494867353)
XLA Ops:
  22.1 25.5 %collective-permute-done = bf16[512,1024]{1,0:T(8,128)(2,1)} collective-permute-done((bf16[512,1024]{1,0:T(8,128)(2,1)}, bf16[512,1024]{1,0:T(8,128)(2,1)}, u32[]{:S(2)}, u32[]{:S(2)}) %collective-permute-start) | collective-permute-done | bytes 1048608 | tf_op jit(solution)/shard_map/ppermute | solution.py:207
  51.2 27.0 %collective-permute-done.2 = bf16[512,1024]{1,0:T(8,128)(2,1)S(1)} collective-permute-done((bf16[512,1024]{1,0:T(8,128)(2,1)}, bf16[512,1024]{1,0:T(8,128)(2,1)S(1)}, u32[]{:S(2)}, u32[]{:S(2)}) %collective-permute-start.2) | collective-permute-done | bytes 1048608 | tf_op jit(solution)/shard_map/ppermute | solution.py:207
  83.3 12.3 %all-gather.4.cloned.1.call-done = bf16[1024,3200]{1,0:T(8,128)(2,1)} async-done(((bf16[32,3200]{1,0:T(8,128)(2,1)}), bf16[1024,3200]{1,0:T(8,128)(2,1)}) %all-gather.4.cloned.1.call-update) | async-done | bytes 6553616 | tf_op jit(solution)/shard_map/all_gather | solution.py:248
  128.2 31.9 %shard_map.212 = (bf16[2,2,512,512]{3,2,1,0:T(8,128)(2,1)}, f32[4,2,2048]{2,1,0:T(2,128)}) custom-call(bf16[2,2,512,512]{3,2,1,0:T(8,128)(2,1)} %all-to-all-done.q_ref, bf16[2048,1024]{1,0:T(8,128)(2,1)} %convolution_convert_fusion.3.kv_ref), custom_call_target="tpu_custom_call" | custom-call | tf_op jit(solution)/shard_map/pallas_call | solution.py:72
  160.1 6.9 all_to_all.30
  177.5 12.4 %all-gather.6.cloned.1.call-done = bf16[1024,5632]{1,0:T(8,128)(2,1)} async-done(((bf16[32,5632]{1,0:T(8,128)(2,1)}), bf16[1024,5632]{1,0:T(8,128)(2,1)}) %all-gather.6.cloned.1.call-update) | async-done | bytes 11534352 | tf_op jit(solution)/shard_map/all_gather | solution.py:249
  189.9 11.9 %fusion.3 = f32[1024,2816]{1,0:T(8,128)} fusion(bf16[1024,1024]{1,0:T(8,128)(2,1)} %multiply_convert_fusion.3, bf16[1024,5632]{1,0:T(8,128)(2,1)} %all-gather.6.cloned.1.call-done), kind=kOutput, calls=%fused_computation.11 | convolution fusion | flops 5905580032 | bytes 19398656 | tf_op jit(solution)/shard_map/dot_general | solution.py:24
  201.8 8.8 %fusion.7 = f32[1024,2816]{1,0:T(8,128)} fusion(bf16[1024,1024]{1,0:T(8,128)(2,1)S(1)} %copy-done.16, bf16[1024,5632]{1,0:T(8,128)(2,1)S(1)} %copy-done.26), kind=kOutput, calls=%fused_computation.15 | convolution fusion | flops 5905580032 | bytes 19398656 | tf_op jit(solution)/shard_map/dot_general | solution.py:24
  210.6 47.9 %all-gather.8.cloned.1.call-done = bf16[2816,1024]{1,0:T(8,128)(2,1)} async-done(((bf16[88,1024]{1,0:T(8,128)(2,1)}), bf16[2816,1024]{1,0:T(8,128)(2,1)}) %all-gather.8.cloned.1.call-update) | async-done | bytes 5767184 | tf_op jit(solution)/shard_map/all_gather | solution.py:250
  258.6 21.8 %multiply_convert_fusion.1 = (bf16[1024,2816]{1,0:T(8,128)(2,1)}, bf16[1024,2816]{1,0:T(8,128)(2,1)}, bf16[1024,2816]{1,0:T(8,128)(2,1)}) fusion(f32[1024,2816]{1,0:T(8,128)} %fusion.7, f32[1024,2816]{1,0:T(8,128)} %fusion.3, bf16[1024,1024]{1,0:T(8,128)(2,1)} %bitcast_convert_fusion, bf16[2816,1024]{1,0:T(8,128)(2,1)} %all-gather.8.cloned.1.call-done), kind=kOutput, calls=%fused_computation.2 | convolution fusion | flops 5948833792 | bytes 48234496 | tf_op jit(solution)/shard_map/dot_general | solution.py:20
  280.4 11.0 %convolution_convert_fusion = bf16[2816,1024]{1,0:T(8,128)(2,1)} fusion(bf16[1024,2816]{1,0:T(8,128)(2,1)} %get-tuple-element.31, bf16[1024,1024]{1,0:T(8,128)(2,1)} %bitcast_convert_fusion), kind=kOutput, calls=%fused_computation.6 | convolution fusion | flops 5908463616 | bytes 13631488 | tf_op jit(solution)/shard_map/dot_general | solution.py:201
  291.5 10.0 %fusion.1 = f32[1024,1024]{1,0:T(8,128)S(1)} fusion(bf16[1024,2816]{1,0:T(8,128)(2,1)} %get-tuple-element.30, bf16[1024,5632]{1,0:T(8,128)(2,1)} %all-gather.6.cloned.1.call-done), kind=kOutput, calls=%fused_computation.9 | convolution fusion | flops 5905580032 | bytes 15728640 | tf_op jit(solution)/shard_map/dot_general | solution.py:20
  301.5 10.9 %multiply_reduce_fusion = (bf16[1024]{0:T(1024)(128)(2,1)S(1)}, f32[1024]{0:T(1024)S(1)}, f32[1024,1024]{1,0:T(8,128)S(1)}) fusion(f32[1024,1024]{1,0:T(8,128)S(1)} %copy-done.1, f32[1024]{0:T(1024)S(1)} %get-tuple-element.55, f32[1024]{0:T(1024)S(1)} %get-tuple-element.21, f32[1024,1024]{1,0:T(8,128)S(1)} %fusion.1, ...), kind=kOutput, calls=%fused_computation.38 | convolution fusion | flops 5912918016 | bytes 24131584 | tf_op jit(solution)/shard_map/dot_general | solution.py:20
  321.6 6.3 all_to_all.31.do_ref
  327.9 66.0 %shard_map.213 = (bf16[2,2,512,512]{3,2,1,0:T(8,128)(2,1)}, bf16[2048,1024]{1,0:T(8,128)(2,1)}) custom-call(bf16[2,2,512,512]{3,2,1,0:T(8,128)(2,1)} %all-to-all-done.q_ref, bf16[2048,1024]{1,0:T(8,128)(2,1)} %convolution_convert_fusion.3.kv_ref, bf16[2,2,512,512]{3,2,1,0:T(8,128)(2,1)} %all_to_all.31.do_ref, ...), custom_call_target="tpu_custom_call" | custom-call | tf_op jit(solution)/shard_map/pallas_call | solution.py:158
  456.3 10.9 %concatenate.29 = bf16[1024,3200]{1,0:T(8,128)(2,1)} concatenate(bf16[1024,512]{1,0:T(8,128)(2,1)S(1)} %copy-done.13, bf16[1024,512]{1,0:T(8,128)(2,1)} %copy.60, bf16[1024,256]{1,0:T(8,128)(2,1)} %copy.61, bf16[1024,256]{1,0:T(8,128)(2,1)} %copy.62, bf16[1024,1024]{1,0:T(8,128)(2,1)} %pad_maximum_fusion.6, bf16[1024,512]{1,0:T(8,128)(2,1)} %reshape.335, ...), dimensions={1} | concatenate | bytes 13107200 | tf_op jit(solution)/shard_map/concatenate | solution.py:371
  467.4 9.8 %convolution_convert_fusion.1 = bf16[1024,2816]{1,0:T(8,128)(2,1)S(1)} fusion(bf16[1024,1024]{1,0:T(8,128)(2,1)} %multiply_convert_fusion.3, bf16[1024,2816]{1,0:T(8,128)(2,1)} %get-tuple-element.30), kind=kOutput, calls=%fused_computation.7 | convolution fusion | flops 5908463616 | bytes 13631488 | tf_op jit(solution)/shard_map/dot_general | solution.py:201
  477.1 9.2 %convolution_convert_fusion.2 = bf16[1024,2816]{1,0:T(8,128)(2,1)S(1)} fusion(bf16[1024,1024]{1,0:T(8,128)(2,1)S(1)} %copy-done.17, bf16[1024,2816]{1,0:T(8,128)(2,1)} %get-tuple-element.29), kind=kOutput, calls=%fused_computation.8 | convolution fusion | flops 5908463616 | bytes 13631488 | tf_op jit(solution)/shard_map/dot_general | solution.py:201
  486.3 6.9 pad_maximum_fusion
  499.4 9.8 %add_convert_fusion = bf16[1024,1024]{1,0:T(8,128)(2,1)S(1)} fusion(f32[1024,1024]{1,0:T(8,128)S(1)} %copy-done.2, bf16[1024,2816]{1,0:T(8,128)(2,1)} %get-tuple-element.31, bf16[2816,1024]{1,0:T(8,128)(2,1)} %all-gather.8.cloned.1.call-done), kind=kOutput, calls=%fused_computation.42 | convolution fusion | flops 5907677184 | bytes 17825792 | tf_op jit(solution)/shard_map/dot_general | solution.py:24
  510.0 35.9 %collective-permute-done.3 = bf16[512,1024]{1,0:T(8,128)(2,1)S(1)} collective-permute-done((bf16[512,1024]{1,0:T(8,128)(2,1)S(1)}, bf16[512,1024]{1,0:T(8,128)(2,1)S(1)}, u32[]{:S(2)}, u32[]{:S(2)}) %collective-permute-start.3) | collective-permute-done | bytes 1048608 | tf_op jit(solution)/shard_map/ppermute | solution.py:207
  547.5 43.2 %collective-permute-done.1 = bf16[512,1024]{1,0:T(8,128)(2,1)S(1)} collective-permute-done((bf16[512,1024]{1,0:T(8,128)(2,1)S(1)}, bf16[512,1024]{1,0:T(8,128)(2,1)S(1)}, u32[]{:S(2)}, u32[]{:S(2)}) %collective-permute-start.1) | collective-permute-done | bytes 1048608 | tf_op jit(solution)/shard_map/ppermute | solution.py:207
  594.0 18.7 %reduce-scatter.4.cloned.1.call-done = bf16[32,3200]{1,0:T(8,128)(2,1)} async-done(((bf16[1024,3200]{1,0:T(8,128)(2,1)}), bf16[32,3200]{1,0:T(8,128)(2,1)}) %reduce-scatter.4.cloned.1.call-update) | async-done | bytes 204816 | tf_op jit(solution)/shard_map/reduce_scatter | solution.py:370
  618.0 148.4 %reduce-scatter.6.cloned.1.call-done = bf16[32,5632]{1,0:T(8,128)(2,1)} async-done(((bf16[1024,5632]{1,0:T(8,128)(2,1)}), bf16[32,5632]{1,0:T(8,128)(2,1)}) %reduce-scatter.6.cloned.1.call-update) | async-done | bytes 360464 | tf_op jit(solution)/shard_map/reduce_scatter | solution.py:314
  (166 shorter events, 157.0 us)
Async XLA Ops:
  7.2 12.0 %copy-start.14 = (bf16[2,512,1024]{2,1,0:T(8,128)(2,1)S(1)}, bf16[2,512,1024]{2,1,0:T(8,128)(2,1)}, u32[]{:S(2)}) copy-start(bf16[2,512,1024]{2,1,0:T(8,128)(2,1)} %param.14) | copy-start | bytes 6291460
  7.2 13.0 %copy-start.27 = (s32[2]{0:T(128)S(1)}, s32[2]{0:T(128)}, u32[]{:S(2)}) copy-start(s32[2]{0:T(128)} %param.15) | copy-start | bytes 28
  7.2 13.6 %copy-start.28 = (f32[8]{0:T(128)S(1)}, f32[8]{0:T(128)}, u32[]{:S(2)}) copy-start(f32[8]{0:T(128)} %param.16) | copy-start | bytes 100
  7.2 88.4 %all-gather.4.cloned.1.call-start = ((), (), s32[]{:S(2)}) async-start(), calls=%async_computation.9 | async-start | bytes 6758400 | tf_op jit(solution)/shard_map/all_gather | solution.py:248
  11.4 178.6 %all-gather.6.cloned.1.call-start = ((), (), s32[]{:S(2)}) async-start(), calls=%async_computation.10 | async-start | bytes 11894784 | tf_op jit(solution)/shard_map/all_gather | solution.py:249
  13.2 245.4 %all-gather.8.cloned.1.call-start = ((), (), s32[]{:S(2)}) async-start(), calls=%async_computation.11 | async-start | bytes 5947392 | tf_op jit(solution)/shard_map/all_gather | solution.py:250
  16.2 31.3 %collective-permute-start = (bf16[512,1024]{1,0:T(8,128)(2,1)}, bf16[512,1024]{1,0:T(8,128)(2,1)}, u32[]{:S(2)}, u32[]{:S(2)}) collective-permute-start(bf16[512,1024]{1,0:T(8,128)(2,1)} %dynamic-slice_bitcast_fusion.3), channel_id=1, source_target_pairs={{0,2},{2,0},{1,3},{3,1},{4,6},{6,4},{5,7},{7,5},{8,10},{10,8},{9,1... | collective-permute-start | bytes 3145736 | tf_op jit(solution)/shard_map/ppermute | solution.py:207
  20.2 58.1 %collective-permute-start.2 = (bf16[512,1024]{1,0:T(8,128)(2,1)}, bf16[512,1024]{1,0:T(8,128)(2,1)S(1)}, u32[]{:S(2)}, u32[]{:S(2)}) collective-permute-start(bf16[512,1024]{1,0:T(8,128)(2,1)} %dynamic-slice_bitcast_fusion.1), channel_id=1, source_target_pairs={{0,2},{2,0},{1,3},{3,1},{4,6},{6,4},{5,7},{7,5},{8,10},{10,8},{9,1... | collective-permute-start | bytes 3145736 | tf_op jit(solution)/shard_map/ppermute | solution.py:207
  49.2 29.1 %copy-start.15 = (bf16[2,512,1024]{2,1,0:T(8,128)(2,1)S(1)}, bf16[2,512,1024]{2,1,0:T(8,128)(2,1)}, u32[]{:S(2)}) copy-start(bf16[2,512,1024]{2,1,0:T(8,128)(2,1)} %param.14) | copy-start | bytes 6291460
  49.7 47.3 %copy-start.24 = (f32[1,4,2,128]{3,1,2,0:T(4,128)}, f32[1,4,2,128]{3,1,2,0:T(4,128)S(1)}, u32[]{:S(2)}) copy-start(f32[1,4,2,128]{3,1,2,0:T(4,128)S(1)} %copy.65) | copy-start | bytes 12292
  102.6 15.4 %all-to-all-start.1 = ((bf16[2,2,512,256]{3,2,1,0:T(8,128)(2,1)}), bf16[2,2,512,256]{3,2,1,0:T(8,128)(2,1)S(1)}, u32[]{:S(2)}, u32[]{:S(2)}) async-start(bf16[2,2,512,256]{3,2,1,0:T(8,128)(2,1)} %pad_maximum_fusion.7), calls=%async_computation.1 | async-start | bytes 2097152 | tf_op jit(solution)/shard_map/all_to_all | solution.py:215
  118.0 10.2 %all-to-all-start = ((bf16[2,2,512,512]{3,2,1,0:T(8,128)(2,1)}), bf16[2,2,512,512]{3,2,1,0:T(8,128)(2,1)}, u32[]{:S(2)}, u32[]{:S(2)}) async-start(bf16[2,2,512,512]{3,2,1,0:T(8,128)(2,1)} %pad_maximum_fusion.2), calls=%async_computation | async-start | bytes 4194304 | tf_op jit(solution)/shard_map/all_to_all | solution.py:215
  122.9 469.5 %reduce-scatter.8.cloned.1.call-start = ((), (), s32[]{:S(2)}) async-start(), calls=%async_computation.14 | async-start | bytes 5947392 | tf_op jit(solution)/shard_map/reduce_scatter | solution.py:320
  189.9 11.9 %copy-start.16 = (bf16[1024,1024]{1,0:T(8,128)(2,1)S(1)}, bf16[1024,1024]{1,0:T(8,128)(2,1)}, u32[]{:S(2)}) copy-start(bf16[1024,1024]{1,0:T(8,128)(2,1)} %multiply_convert_fusion.3) | copy-start | bytes 6291460
  189.9 11.9 %copy-start.26 = (bf16[1024,5632]{1,0:T(8,128)(2,1)S(1)}, bf16[1024,5632]{1,0:T(8,128)(2,1)}, u32[]{:S(2)}) copy-start(bf16[1024,5632]{1,0:T(8,128)(2,1)} %all-gather.6.cloned.1.call-done) | copy-start | bytes 34603012
  291.4 10.0 %copy-start.1 = (f32[1024,1024]{1,0:T(8,128)S(1)}, f32[1024,1024]{1,0:T(8,128)}, u32[]{:S(2)}) copy-start(f32[1024,1024]{1,0:T(8,128)} %copy-done) | copy-start | bytes 12582916
  301.5 10.9 %copy-start.4 = (f32[2,512,1024]{2,1,0:T(8,128)S(1)}, f32[2,512,1024]{2,1,0:T(8,128)}, u32[]{:S(2)}) copy-start(f32[2,512,1024]{2,1,0:T(8,128)} %copy-done.3) | copy-start | bytes 12582916
  402.1 7.8 %all-to-all-start.4 = ((bf16[2,2,512,512]{3,2,1,0:T(8,128)(2,1)}), bf16[2,2,512,512]{3,2,1,0:T(8,128)(2,1)}, u32[]{:S(2)}, u32[]{:S(2)}) async-start(bf16[2,2,512,512]{3,2,1,0:T(8,128)(2,1)} %get-tuple-element.17), calls=%async_computation.4 | async-start | bytes 4194304 | tf_op jit(solution)/shard_map/all_to_all | solution.py:215
  406.9 205.8 %reduce-scatter.4.cloned.1.call-start = ((), (), s32[]{:S(2)}) async-start(), calls=%async_computation.12 | async-start | bytes 6758400 | tf_op jit(solution)/shard_map/reduce_scatter | solution.py:370
  441.7 8.1 %copy-start.8 = (bf16[1,2,512,512]{3,2,1,0:T(8,128)(2,1)S(1)}, bf16[1,2,512,512]{3,2,1,0:T(8,128)(2,1)}, u32[]{:S(2)}) copy-start(bf16[1,2,512,512]{3,2,1,0:T(8,128)(2,1)} %copy-done.7) | copy-start | bytes 3145732
  467.3 299.1 %reduce-scatter.6.cloned.1.call-start = ((), (), s32[]{:S(2)}) async-start(), calls=%async_computation.13 | async-start | bytes 11894784 | tf_op jit(solution)/shard_map/reduce_scatter | solution.py:314
  467.3 9.8 %copy-start.17 = (bf16[1024,1024]{1,0:T(8,128)(2,1)S(1)}, bf16[1024,1024]{1,0:T(8,128)(2,1)}, u32[]{:S(2)}) copy-start(bf16[1024,1024]{1,0:T(8,128)(2,1)} %multiply_convert_fusion.3) | copy-start | bytes 6291460
  497.8 48.0 %collective-permute-start.3 = (bf16[512,1024]{1,0:T(8,128)(2,1)S(1)}, bf16[512,1024]{1,0:T(8,128)(2,1)S(1)}, u32[]{:S(2)}, u32[]{:S(2)}) collective-permute-start(bf16[512,1024]{1,0:T(8,128)(2,1)S(1)} %dynamic-slice_bitcast_fusion), channel_id=1, source_target_pairs={{0,2},{2,0},{1,3},{3,1},{4,6},{6,4},{5,7},{7,5},{8,10},{10,8},{9,1... | collective-permute-start | bytes 3145736 | tf_op jit(solution)/shard_map/ppermute | solution.py:207
  509.3 81.3 %collective-permute-start.1 = (bf16[512,1024]{1,0:T(8,128)(2,1)S(1)}, bf16[512,1024]{1,0:T(8,128)(2,1)S(1)}, u32[]{:S(2)}, u32[]{:S(2)}) collective-permute-start(bf16[512,1024]{1,0:T(8,128)(2,1)S(1)} %dynamic-slice_bitcast_fusion.2), channel_id=1, source_target_pairs={{0,2},{2,0},{1,3},{3,1},{4,6},{6,4},{5,7},{7,5},{8,10},{10,8},{9,1... | collective-permute-start | bytes 3145736 | tf_op jit(solution)/shard_map/ppermute | solution.py:207
  (18 other events, 64.3 us)
Sparse Core Ops, SparseCore 0:
  11.5 84.0 all-gather.3
  99.0 90.8 all-gather.5
  192.8 65.7 all-gather.7
  291.6 142.9 reduce-scatter.7
  467.4 145.1 reduce-scatter.3
  614.8 151.4 reduce-scatter.5

commit v2 on v1

--- a/solution.py
+++ b/solution.py
@@ -12,8 +12,8 @@
 BF = jnp.bfloat16
 
 
-def low_half(x):
-    return jnp.concatenate([x[:, :DH], jnp.zeros((x.shape[0], DH), x.dtype)], axis=1)
+def cost(flops):
+    return pl.CostEstimate(flops=flops, bytes_accessed=2**23, transcendentals=0)
 
 
 def dot_nt(a, b):
@@ -86,6 +86,7 @@
         ],
         scratch_shapes=[pltpu.VMEM((2, DH, seq), BF)],
         compiler_params=pltpu.CompilerParams(vmem_limit_bytes=56 * 2**20),
+        cost_estimate=cost(8 * pairs * seq * seq * 128),
     )(q, kv)
 
 
@@ -171,7 +172,233 @@
             pltpu.VMEM((2, seq), F32),
         ],
         compiler_params=pltpu.CompilerParams(vmem_limit_bytes=56 * 2**20),
+        cost_estimate=cost(16 * pairs * seq * seq * 128),
     )(q, kv, do, o, lse)
+
+
+MESH = pl.DeviceIdType.MESH
+
+
+def ring_place(dp, d, s):
+    even = lax.rem(d, 2)
+    p = d - even + lax.rem(even + lax.div(d, 2), 2)
+    return p + s * (2 * dp - 1 - 2 * p)
+
+
+def ring_device(dp, r):
+    s = lax.div(r, dp)
+    p = r + s * (2 * dp - 1 - 2 * r)
+    even = lax.rem(p, 2)
+    return p - even + lax.rem(even + lax.div(p, 2), 2), s
+
+
+def greet(neighbours):
+    barrier = pltpu.get_barrier_semaphore()
+    for there in neighbours:
+        pl.semaphore_signal(barrier, inc=1, device_id=there, device_id_type=MESH)
+    pl.semaphore_wait(barrier, len(neighbours))
+
+
+def remote(src, dst, send, recv, there):
+    return pltpu.make_async_remote_copy(
+        src_ref=src, dst_ref=dst, send_sem=send, recv_sem=recv, device_id=there, device_id_type=MESH
+    )
+
+
+def gather_kernel(dp, count, *refs):
+    srcs, x_in = refs[:count], refs[count]
+    outs, x_out = refs[count + 1 : 2 * count + 1], refs[2 * count + 1]
+    ring_send, ring_recv, pair_send, pair_recv, own_sem, x_sem = refs[2 * count + 2 :]
+    d, s, c = lax.axis_index("dp"), lax.axis_index("seq"), lax.axis_index("grp")
+    n = 2 * dp
+    r = ring_place(dp, d, s)
+    right = (*ring_device(dp, lax.rem(r + 1, n)), c)
+    left = (*ring_device(dp, lax.rem(r + n - 1, n)), c)
+    pair = (d, s, 1 - c)
+    across = (d, 1 - s, c)
+
+    def place(at, core):
+        dk, sk = ring_device(dp, lax.rem(at + n, n))
+        return (dk * 2 + sk) * 2 + core
+
+    greet((right, left, pair, across))
+    swap = remote(x_in.at[1 - s], x_out.at[s], x_sem.at[0], x_sem.at[1], across)
+    swap.start()
+    mine = place(r, c)
+    waits = []
+    hops = (n // 2, n - 1 - n // 2)
+    ways = (right, left)
+    for a in range(count):
+        for way in range(2):
+            copy = remote(
+                srcs[a], outs[a].at[mine], ring_send.at[way, 0, a], ring_recv.at[way, 0, a], ways[way]
+            )
+            copy.start()
+            waits.append(copy)
+        copy = remote(srcs[a], outs[a].at[mine], pair_send.at[0, a], pair_recv.at[0, a], pair)
+        copy.start()
+        waits.append(copy)
+        kept = pltpu.make_async_copy(srcs[a], outs[a].at[mine], own_sem.at[a])
+        kept.start()
+        waits.append(kept)
+    kept = pltpu.make_async_copy(x_in.at[s], x_out.at[s], x_sem.at[2])
+    kept.start()
+    slot = 1
+    pairs_in = [(0, place(r, 1 - c))]
+    for t in range(1, hops[0] + 1):
+        for way in range(2):
+            if t > hops[way]:
+                continue
+            at = place(r - t if way == 0 else r + t, c)
+            other = place(r - t if way == 0 else r + t, 1 - c)
+            for a in range(count):
+                here = outs[a].at[at]
+                remote(
+                    here, here, ring_send.at[way, t - 1, a], ring_recv.at[way, t - 1, a], ways[way]
+                ).wait_recv()
+                if t < hops[way]:
+                    copy = remote(
+                        here, here, ring_send.at[way, t, a], ring_recv.at[way, t, a], ways[way]
+                    )
+                    copy.start()
+                    waits.append(copy)
+                copy = remote(here, here, pair_send.at[slot, a], pair_recv.at[slot, a], pair)
+                copy.start()
+                waits.append(copy)
+            pairs_in.append((slot, other))
+            slot += 1
+    for number, other in pairs_in:
+        for a in range(count):
+            here = outs[a].at[other]
+            remote(here, here, pair_send.at[number, a], pair_recv.at[number, a], pair).wait_recv()
+    for copy in waits:
+        if copy.is_remote:
+            copy.wait_send()
+        else:
+            copy.wait()
+    swap.wait()
+    kept.wait()
+
+
+def ring_gather(dp, shards, blocks):
+    count = len(shards)
+    n = 2 * dp
+    anywhere = pl.BlockSpec(memory_space=pl.ANY)
+    sem = pltpu.SemaphoreType.DMA
+    out = pl.pallas_call(
+        functools.partial(gather_kernel, dp, count),
+        in_specs=[anywhere] * (count + 1),
+        out_specs=[anywhere] * (count + 1),
+        out_shape=[jax.ShapeDtypeStruct((2 * n, *w.shape), w.dtype) for w in shards]
+        + [jax.ShapeDtypeStruct(blocks.shape, blocks.dtype)],
+        scratch_shapes=[
+            sem((2, n // 2, count)),
+            sem((2, n // 2, count)),
+            sem((n, count)),
+            sem((n, count)),
+            sem((count,)),
+            sem((3,)),
+        ],
+        compiler_params=pltpu.CompilerParams(collective_id=0, has_side_effects=True),
+    )(*shards, blocks)
+    return out[:-1], out[-1]
+
+
+def scatter_kernel(dp, ways_of, *refs):
+    count = len(ways_of)
+    terms, x_in = refs[:count], refs[count]
+    outs, x_out = refs[count + 1 : 2 * count + 1], refs[2 * count + 1]
+    rest = refs[2 * count + 2 :]
+    pair_bufs, ring_bufs = rest[:count], rest[count : 2 * count]
+    ring_send, ring_recv, pair_send, pair_recv, x_sem = rest[2 * count :]
+    d, s, c = lax.axis_index("dp"), lax.axis_index("seq"), lax.axis_index("grp")
+    n = 2 * dp
+    r = ring_place(dp, d, s)
+    right = (*ring_device(dp, lax.rem(r + 1, n)), c)
+    left = (*ring_device(dp, lax.rem(r + n - 1, n)), c)
+    pair = (d, s, 1 - c)
+    across = (d, 1 - s, c)
+    ways = (right, left)
+
+    def place(t, way, core):
+        at = r - 1 - t if way == 0 else r + 1 + t
+        dk, sk = ring_device(dp, lax.rem(at + n, n))
+        return (dk * 2 + sk) * 2 + core
+
+    greet((right, left, pair, across))
+    for t in range(n):
+        for a in range(count):
+            remote(
+                terms[a].at[place(t, ways_of[a], 1 - c)],
+                pair_bufs[a].at[t],
+                pair_send.at[t, a],
+                pair_recv.at[t, a],
+                pair,
+            ).start()
+    swap = remote(x_in.at[1 - s], x_out.at[s], x_sem.at[0], x_sem.at[1], across)
+    swap.start()
+    kept = pltpu.make_async_copy(x_in.at[s], x_out.at[s], x_sem.at[2])
+    kept.start()
+
+    def pair_copy(t, a):
+        return remote(
+            terms[a].at[place(t, ways_of[a], 1 - c)],
+            pair_bufs[a].at[t],
+            pair_send.at[t, a],
+            pair_recv.at[t, a],
+            pair,
+        )
+
+    def ring_copy(t, a):
+        src = pair_bufs[a].at[0] if t == 0 else ring_bufs[a].at[t - 1]
+        return remote(
+            src, ring_bufs[a].at[t], ring_send.at[t, a], ring_recv.at[t, a], ways[ways_of[a]]
+        )
+
+    for t in range(n):
+        for a in range(count):
+            pair_copy(t, a).wait_recv()
+            total = terms[a][place(t, ways_of[a], c)].astype(F32) + pair_bufs[a][t].astype(F32)
+            if t > 0:
+                ring_copy(t - 1, a).wait_recv()
+                total = total + ring_bufs[a][t - 1].astype(F32)
+            if t == n - 1:
+                outs[a][...] = total
+            elif t == 0:
+                pair_bufs[a][0] = total.astype(BF)
+            else:
+                ring_bufs[a][t - 1] = total.astype(BF)
+            if t < n - 1:
+                ring_copy(t, a).start()
+    for t in range(n):
+        for a in range(count):
+            pair_copy(t, a).wait_send()
+            if t < n - 1:
+                ring_copy(t, a).wait_send()
+    swap.wait()
+    kept.wait()
+
+
+def ring_scatter(dp, terms, ways_of, blocks):
+    count = len(terms)
+    n = 2 * dp
+    anywhere = pl.BlockSpec(memory_space=pl.ANY)
+    inside = pl.BlockSpec(memory_space=pltpu.VMEM)
+    sem = pltpu.SemaphoreType.DMA
+    out = pl.pallas_call(
+        functools.partial(scatter_kernel, dp, ways_of),
+        in_specs=[inside] * count + [anywhere],
+        out_specs=[inside] * count + [anywhere],
+        out_shape=[jax.ShapeDtypeStruct(w.shape[1:], F32) for w in terms]
+        + [jax.ShapeDtypeStruct(blocks.shape, blocks.dtype)],
+        scratch_shapes=[pltpu.VMEM((n, *w.shape[1:]), BF) for w in terms]
+        + [pltpu.VMEM((n - 1, *w.shape[1:]), BF) for w in terms]
+        + [sem((n - 1, count)), sem((n - 1, count)), sem((n, count)), sem((n, count)), sem((3,))],
+        compiler_params=pltpu.CompilerParams(
+            collective_id=1, has_side_effects=True, vmem_limit_bytes=48 * 2**20
+        ),
+    )(*terms, blocks)
+    return out[:-1], out[-1]
 
 
 HEADS = 16
@@ -240,27 +467,27 @@
     cols = heads * DH
     drows = width // devices
 
-    gains = jnp.concatenate(
-        [norm_gain[:, None], ffn_gain[:, None], jnp.zeros((drows, 126), BF)], axis=1
-    )
-    expand_rows = expansion_weight.reshape(drows, -1)
-    attn_weights = jnp.concatenate([w_query, w_latent, w_output, expand_rows, gains], axis=1)
-    attn_full = lax.all_gather(attn_weights, ALL, axis=0, tiled=True)
+    dp = lax.axis_size("dp")
+    ring = groups == 2 and seqs == 2 and dp % 2 == 0
+    expand_rows = expansion_weight.reshape(-1, expansion_weight.shape[2])
+    gains = jnp.pad(jnp.concatenate([norm_gain, ffn_gain])[None], ((0, 15), (0, 128 - 2 * drows)))
+    shards = (w_query, w_latent, w_output, expand_rows, gains)
+    if ring:
+        full, own_inputs = ring_gather(dp, shards, inputs)
+    else:
+        full = [lax.all_gather(w, ALL, axis=0) for w in shards]
+        own_inputs = swap_sequences(inputs, seqs)
     ffn_full = lax.all_gather(jnp.concatenate([w_gate, w_up], axis=1), ALL, axis=0, tiled=True)
     down_full = lax.all_gather(w_down, ALL, axis=0, tiled=True)
-    query_full = attn_full[:, :width]
-    latent_full = attn_full[:, width : width + KVH * LATD]
-    output_full = attn_full[:, width + KVH * LATD : 2 * width + KVH * LATD]
-    ecols = expand_rows.shape[1]
-    at = 2 * width + KVH * LATD
-    expand_full = attn_full[:, at : at + ecols].reshape(devices, KVH, LATD // devices, -1)
-    expand_full = expand_full.transpose(1, 0, 2, 3).reshape(KVH, LATD, -1)
-    gain_one = attn_full[:, at + ecols].astype(F32)
-    gain_two = attn_full[:, at + ecols + 1].astype(F32)
+    query_full = full[0].reshape(width, -1)
+    latent_full = full[1].reshape(width, -1)
+    output_full = full[2].reshape(-1, width)
+    expand_full = full[3].reshape(devices, KVH, LATD // devices, -1)
+    gain_one = full[4][:, 0, :drows].reshape(width).astype(F32)
+    gain_two = full[4][:, 0, drows : 2 * drows].reshape(width).astype(F32)
     gate_full = ffn_full[:, :hidden_size]
     up_full = ffn_full[:, hidden_size:]
 
-    own_inputs = swap_sequences(inputs, seqs)
     own_cotangent = swap_sequences(cotangent, seqs)
 
     token_rows = own_inputs.astype(F32).reshape(count, width)
@@ -278,8 +505,10 @@
     head_queries = swap_group(query_send)
     head_latent = swap_group(latent_send).transpose(1, 0, 2, 3).reshape(-1, LATD)
     expand_local = lax.dynamic_slice(
-        expand_full, (me * heads // HG, 0, me * heads % HG * 2 * DH), (1, LATD, heads * 2 * DH)
-    )[0]
+        expand_full,
+        (0, me * heads // HG, 0, me * heads % HG * 2 * DH),
+        (devices, 1, LATD // devices, heads * 2 * DH),
+    ).reshape(LATD, -1)
     head_pairs = dot_nn(head_latent, expand_local).astype(BF)
     attended, logsum = attention_forward(head_queries, head_pairs)
     token_attended = swap_group(attended).reshape(groups, count, cols)
@@ -311,15 +540,39 @@
     normed_two_back = dot_nt(gate_back, gate_full) + dot_nt(up_back, up_full)
     middle_part, gain_two_grad = norm_back(middle, inverse_two, gain_two, normed_two_back)
     middle_grad = upstream + middle_part
-    ffn_share = lax.psum_scatter(
-        jnp.concatenate([gate_grad.astype(BF), up_grad.astype(BF)], axis=1),
-        ALL,
-        scatter_dimension=0,
-        tiled=True,
-    ).astype(F32)
-    down_share = lax.psum_scatter(
-        down_grad.astype(BF), ALL, scatter_dimension=0, tiled=True
-    ).astype(F32)
+    if ring:
+        both = jnp.concatenate([gate_grad.astype(BF), up_grad.astype(BF)], axis=1).reshape(
+            devices, drows, -1
+        )
+        whole = both.shape[2] // width * width
+        half = drows // 2
+        packed = jnp.concatenate(
+            [both[:, :, a : a + width] for a in range(0, whole, width)]
+            + [
+                jnp.concatenate([both[:, :half, whole:], both[:, half:, whole:]], axis=2),
+                down_grad.astype(BF).reshape(devices, -1, width),
+            ],
+            axis=1,
+        )
+        share = lax.psum_scatter(packed, ALL, scatter_dimension=0, tiled=True)[0].astype(F32)
+        tall = whole // width * drows
+        tail = share[tall : tall + half]
+        ffn_share = jnp.concatenate(
+            [share[a : a + drows] for a in range(0, tall, drows)]
+            + [jnp.concatenate([tail[:, : width // 2], tail[:, width // 2 :]], axis=0)],
+            axis=1,
+        )
+        down_share = share[tall + half :]
+    else:
+        ffn_share = lax.psum_scatter(
+            jnp.concatenate([gate_grad.astype(BF), up_grad.astype(BF)], axis=1),
+            ALL,
+            scatter_dimension=0,
+            tiled=True,
+        ).astype(F32)
+        down_share = lax.psum_scatter(
+            down_grad.astype(BF), ALL, scatter_dimension=0, tiled=True
+        ).astype(F32)
 
     branch_low = middle_grad.astype(BF)
     output_grad = jnp.concatenate(
@@ -338,9 +591,9 @@
     latent_terms = dot_nt(pair_back, expand_local).astype(BF)
     expand_part = dot_tn(head_latent, pair_back)
     expand_grad = lax.dynamic_update_slice(
-        jnp.zeros(expand_full.shape, F32),
-        expand_part[None],
-        (me * heads // HG, 0, me * heads % HG * 2 * DH),
+        jnp.zeros(expand_full.shape, BF),
+        expand_part.astype(BF).reshape(devices, 1, LATD // devices, -1),
+        (0, me * heads // HG, 0, me * heads % HG * 2 * DH),
     )
     query_token = swap_group(query_back).reshape(groups, count, cols)
     latent_token = swap_group(
@@ -355,42 +608,41 @@
         dot_nt(latent_token[g], latent_full[:, g * LATD : (g + 1) * LATD]) for g in range(KVH)
     )
     input_part, gain_one_grad = norm_back(token_rows, inverse_one, gain_one, normed_back)
-    input_grad = swap_sequences(
-        (middle_grad + input_part).astype(BF).reshape(seqs, rows, width), seqs
-    )
-    expand_out = (
-        expand_grad.astype(BF)
-        .reshape(KVH, devices, LATD // devices, -1)
-        .transpose(1, 0, 2, 3)
-        .reshape(width, -1)
-    )
+    own_input_grad = (middle_grad + input_part).astype(BF).reshape(seqs, rows, width)
     gain_grads = jnp.concatenate(
-        [gain_one_grad[:, None], gain_two_grad[:, None], jnp.zeros((width, 126), F32)], axis=1
-    )
-    attn_share = lax.psum_scatter(
-        jnp.concatenate(
-            [
-                query_grad.astype(BF),
-                latent_grad.astype(BF),
-                output_grad.astype(BF),
-                expand_out,
-                gain_grads.astype(BF),
-            ],
-            axis=1,
-        ),
-        ALL,
-        scatter_dimension=0,
-        tiled=True,
-    ).astype(F32)
+        [gain_one_grad.reshape(devices, 1, drows), gain_two_grad.reshape(devices, 1, drows)], axis=2
+    ).astype(BF)
+    gain_grads = jnp.pad(gain_grads, ((0, 0), (0, 15), (0, 128 - 2 * drows)))
+    terms = (
+        query_grad.astype(BF).reshape(devices, drows, -1),
+        latent_grad.astype(BF).reshape(devices, drows, -1),
+        output_grad.astype(BF).reshape(devices, drows, -1),
+        expand_grad.reshape(devices, -1, expand_grad.shape[3]),
+        gain_grads,
+    )
+    if ring:
+        half = drows // 2
+        sums, input_grad = ring_scatter(
+            dp,
+            (terms[0], terms[2][:, :half], terms[2][:, half:], terms[1], terms[3], terms[4]),
+            (0, 0, 1, 1, 1, 1),
+            own_input_grad,
+        )
+        sums = (sums[0], sums[3], jnp.concatenate(sums[1:3], axis=0), sums[4], sums[5])
+    else:
+        sums = [
+            lax.psum_scatter(w, ALL, scatter_dimension=0, tiled=True)[0].astype(F32) for w in terms
+        ]
+        input_grad = swap_sequences(own_input_grad, seqs)
     return (
         output,
         input_grad,
-        attn_share[:, at + ecols],
-        attn_share[:, :width],
-        attn_share[:, width : width + KVH * LATD],
-        attn_share[:, at : at + ecols].reshape(expansion_weight.shape),
-        attn_share[:, width + KVH * LATD : at],
-        attn_share[:, at + ecols + 1],
+        sums[4][0, :drows],
+        sums[0],
+        sums[1],
+        sums[3].reshape(expansion_weight.shape),
+        sums[2],
+        sums[4][0, drows : 2 * drows],
         ffn_share[:, :hidden_size],
         ffn_share[:, hidden_size:],
         down_share,

time: 783 us -> 574 us (0.73)
  waiting for transfers between devices: 374 us -> 28.1 us
  Pallas kernels: 97.9 us -> 278 us
  matrix products: 162 us -> 134 us
  blocking collectives: 17.8 us -> 6.54 us
    pallas_call x0 -> x2, Pallas kernels: none -> 180 us  [the longest x1 96.2 us: ring_scatter(): pl.pallas_call(functools.partial(scatter_kernel, dp, ways_of), in_specs=[...]
    reduce_scatter x3 -> x1, waiting for transfers between devices: 167 us -> 0.01 us  [local(): lax.psum_scatter(packed, ALL, scatter_dimension=0, tiled=True)[0]]
    ppermute x4 -> x2, waiting for transfers between devices: 132 us -> 23.4 us  [swap_sequences(): sent = lax.ppermute(blocks[1 - me], 'seq', [(0, 1), (1, 0)])]
    all_gather x1, waiting for transfers between devices: 47.9 us -> 0.01 us  [local(): down_full = lax.all_gather(w_down, ALL, axis=0, tiled=True)]
    unnamed x59 -> x126, local copies, waits for them, and re-layouts: 2.59 us -> 25.5 us
    dot_general x10, matrix products: 49 us -> 32.7 us  [dot_tn(): lax.dot_general(a, b, (((0,), (0,)), ((), ())), preferred_element_type=F32)]
    all_gather x1, waiting for transfers between devices: 12.4 us -> 0.01 us  [local(): lax.all_gather(jnp.concatenate([w_gate, w_up], axis=1), ALL, axis=0, tile...]
    all_gather x1 -> x0, waiting for transfers between devices: 12.3 us -> none  [local(): attn_full = lax.all_gather(attn_weights, ALL, axis=0, tiled=True)]
  transfers between devices with their start and end apart: 13 -> 10, of which waited for: 10 -> 3; matrix products, arithmetic and copies ran while one was open for 27% -> 24% of each run, Pallas kernels for 13% -> 49%
where the time goes in v2:
time: 574 us; the launch traced here: 568 us
  Pallas kernels  278 us (48%)
  matrix products  134 us (23%)
  local copies, waits for them, and re-layouts  46.4 us (8%)
  other arithmetic  39.4 us (7%)
  waiting for transfers between devices  28.1 us (5%)
  starting transfers between devices  20.5 us (4%)
  between operations  15.1 us (3%)
  blocking collectives  6.54 us (1%)
    pallas_call x1, Pallas kernels, ring_scatter(): pl.pallas_call(functools.partial(scatter_kernel, dp, ways_of), in_specs=[...  96.2 us
    pallas_call x1, Pallas kernels, ring_gather(): pl.pallas_call(functools.partial(gather_kernel, dp, count), in_specs=[any...  83.8 us
    pallas_call x1, Pallas kernels, attention_backward(): pl.pallas_call(functools.partial(backward_kernel, blk), grid=(pairs,), in...  66.1 us
    dot_general x10, matrix products, dot_nt(): lax.dot_general(a, b, (((1,), (1,)), ((), ())), preferred_element_type=F32)  57.8 us
    dot_general x10, matrix products, dot_nn(): lax.dot_general(a, b, (((1,), (0,)), ((), ())), preferred_element_type=F32)  43.8 us
    dot_general x10, matrix products, dot_tn(): lax.dot_general(a, b, (((0,), (0,)), ((), ())), preferred_element_type=F32)  32.7 us
    pallas_call x1, Pallas kernels, attention_forward(): pl.pallas_call(forward_kernel, grid=(pairs,), in_specs=[pl.BlockSpec((gro...  31.9 us
    unnamed x126, local copies, waits for them, and re-layouts  25.5 us
  transfers between devices with their start and end apart: 10, of which 3 were waited for; matrix products, arithmetic and copies ran while one was open for 24% of the time, Pallas kernels for 49%

profile of v2, /device:TPU:0, one launch (start us, length us, event | category | flops | bytes accessed | tf_op | source)
XLA Modules:
  0.0 568.4 jit_solution(13032684570590570659)
XLA Ops:
  11.1 83.8 %shard_map.212 = (bf16[32,32,1024]{2,1,0:T(8,128)(2,1)}, bf16[32,32,512]{2,1,0:T(8,128)(2,1)}, bf16[32,32,1024]{2,1,0:T(8,128)(2,1)}, bf16[32,16,1024]{2,1,0:T(8...) custom-call(bf16[32,1024]{1,0:T(8,128)(2,1)} %refs_0_.1, bf16[32,512]{1,0:T(8,128)(2,1)} %refs_1_.1, ...), custom_call_target="tpu_custom_call" | custom-call | tf_op jit(solution)/shard_map/pallas_call | solution.py:288
  103.5 3.6 all-to-all-start.1
  112.6 4.1 all-to-all-start
  117.8 4.3 convolution_convert_fusion.3.kv_ref
  123.4 31.9 %shard_map.213 = (bf16[2,2,512,512]{3,2,1,0:T(8,128)(2,1)}, f32[4,2,2048]{2,1,0:T(2,128)}) custom-call(bf16[2,2,512,512]{3,2,1,0:T(8,128)(2,1)} %copy-done.21, bf16[2048,1024]{1,0:T(8,128)(2,1)} %convolution_convert_fusion.3.kv_ref), custom_call_target="tpu_custom_call" | custom-call | flops 17179869184 | bytes 8388608 | tf_op jit(solution)/shard_map/pallas_call | solution.py:72
  155.3 3.9 all-to-all-start.2
  174.4 23.4 %collective-permute-done.1 = bf16[512,1024]{1,0:T(8,128)(2,1)} collective-permute-done((bf16[512,1024]{1,0:T(8,128)(2,1)}, bf16[512,1024]{1,0:T(8,128)(2,1)}, u32[]{:S(2)}, u32[]{:S(2)}) %collective-permute-start.1) | collective-permute-done | bytes 1048608 | tf_op jit(solution)/shard_map/ppermute | solution.py:434
  204.1 12.1 %fusion.7 = f32[1024,2816]{1,0:T(8,128)} fusion(bf16[1024,1024]{1,0:T(8,128)(2,1)} %multiply_convert_fusion.3, bf16[1024,5632]{1,0:T(8,128)(2,1)} %all-gather.3.cloned.1.call-done), kind=kOutput, calls=%fused_computation.15 | convolution fusion | flops 5905580032 | bytes 19398656 | tf_op jit(solution)/shard_map/dot_general | solution.py:24
  216.2 8.8 %fusion.3 = f32[1024,2816]{1,0:T(8,128)} fusion(bf16[1024,1024]{1,0:T(8,128)(2,1)S(1)} %copy-done.24, bf16[1024,5632]{1,0:T(8,128)(2,1)S(1)} %copy-done.49), kind=kOutput, calls=%fused_computation.11 | convolution fusion | flops 5905580032 | bytes 19398656 | tf_op jit(solution)/shard_map/dot_general | solution.py:24
  225.0 21.4 %multiply_convert_fusion.1 = (bf16[1024,2816]{1,0:T(8,128)(2,1)}, bf16[1024,2816]{1,0:T(8,128)(2,1)}, bf16[1024,2816]{1,0:T(8,128)(2,1)}) fusion(f32[1024,2816]{1,0:T(8,128)} %fusion.7, f32[1024,2816]{1,0:T(8,128)} %fusion.3, bf16[1024,1024]{1,0:T(8,128)(2,1)} %bitcast_convert_fusion, bf16[2816,1024]{1,0:T(8,128)(2,1)} %all-gather.5.cloned.1.call-done), kind=kOutput, calls=%fused_computation.2 | convolution fusion | flops 5948833792 | bytes 48234496 | tf_op jit(solution)/shard_map/dot_general | solution.py:20
  246.4 10.0 %convolution_convert_fusion.1 = bf16[1024,2816]{1,0:T(8,128)(2,1)S(1)} fusion(bf16[1024,1024]{1,0:T(8,128)(2,1)} %multiply_convert_fusion.3, bf16[1024,2816]{1,0:T(8,128)(2,1)} %get-tuple-element.54), kind=kOutput, calls=%fused_computation.7 | convolution fusion | flops 5908463616 | bytes 13631488 | tf_op jit(solution)/shard_map/dot_general | solution.py:428
  256.4 6.8 %convolution_convert_fusion.2 = bf16[1024,2816]{1,0:T(8,128)(2,1)S(1)} fusion(bf16[1024,1024]{1,0:T(8,128)(2,1)S(1)} %copy-done.25, bf16[1024,2816]{1,0:T(8,128)(2,1)S(1)} %copy-done.53), kind=kOutput, calls=%fused_computation.8 | convolution fusion | flops 5908463616 | bytes 13631488 | tf_op jit(solution)/shard_map/dot_general | solution.py:428
  263.2 4.1 pad_maximum_fusion
  275.4 6.6 %convolution_convert_fusion = bf16[2816,1024]{1,0:T(8,128)(2,1)S(1)} fusion(bf16[1024,2816]{1,0:T(8,128)(2,1)S(1)} %bitcast.241, bf16[1024,1024]{1,0:T(8,128)(2,1)S(1)} %copy-done.20), kind=kOutput, calls=%fused_computation.6 | convolution fusion | flops 5908463616 | bytes 13631488 | tf_op jit(solution)/shard_map/dot_general | solution.py:428
  288.7 4.1 copy.33
  292.9 10.4 %add_convert_fusion = bf16[1024,1024]{1,0:T(8,128)(2,1)S(1)} fusion(f32[1024,1024]{1,0:T(8,128)} %copy-done.1, bf16[1024,2816]{1,0:T(8,128)(2,1)} %get-tuple-element.55, bf16[2816,1024]{1,0:T(8,128)(2,1)} %all-gather.5.cloned.1.call-done), kind=kOutput, calls=%fused_computation.42 | convolution fusion | flops 5907677184 | bytes 17825792 | tf_op jit(solution)/shard_map/dot_general | solution.py:24
  306.1 12.9 %fusion.1 = f32[1024,1024]{1,0:T(8,128)} fusion(bf16[1024,2816]{1,0:T(8,128)(2,1)} %get-tuple-element.54, bf16[1024,5632]{1,0:T(8,128)(2,1)} %all-gather.3.cloned.1.call-done), kind=kOutput, calls=%fused_computation.9 | convolution fusion | flops 5905580032 | bytes 15728640 | tf_op jit(solution)/shard_map/dot_general | solution.py:20
  319.0 10.2 %multiply_reduce_fusion = (bf16[1024]{0:T(1024)(128)(2,1)S(1)}, f32[1024]{0:T(1024)S(1)}, f32[1024,1024]{1,0:T(8,128)S(1)}) fusion(f32[1024,1024]{1,0:T(8,128)S(1)} %copy-done.2, f32[1024]{0:T(1024)S(1)} %copy-done.46, f32[1024]{0:T(1024)S(1)} %copy-done.44, f32[1024,1024]{1,0:T(8,128)} %fusion.1, bf16[1024,2816]{1,0:T(8,128)(2,1)S(1)} %bitcast.239, ...), kind=kOutput, calls=%fused_computation.38 | convolution fusion | flops 5912918016 | bytes 24131584 | tf_op jit(solution)/shard_map/dot_general | solution.py:20
  335.8 6.5 %all_to_all.30.do_ref = bf16[2,2,512,512]{3,2,1,0:T(8,128)(2,1)} all-to-all(bf16[2,2,512,512]{3,2,1,0:T(8,128)(2,1)S(1)} %pad_maximum_fusion.3), channel_id=1, replica_groups=mesh['dp'=8,'seq'=2,'grp'=2] {'grp'}, dimensions={0} | all-to-all | bytes 4194304 | tf_op jit(solution)/shard_map/all_to_all | solution.py:442
  342.4 66.1 %shard_map.214 = (bf16[2,2,512,512]{3,2,1,0:T(8,128)(2,1)}, bf16[2048,1024]{1,0:T(8,128)(2,1)}) custom-call(bf16[2,2,512,512]{3,2,1,0:T(8,128)(2,1)} %copy-done.21, bf16[2048,1024]{1,0:T(8,128)(2,1)} %convolution_convert_fusion.3.kv_ref, bf16[2,2,512,512]{3,2,1,0:T(8,128)(2,1)} %all_to_all.30.do_ref, bf16[2,2,512,512]{3,2,1,0:T(8,128)(2,1)} %get-tuple-element.33.o_ref, ...), custom_call_target="tpu_custom_call" | custom-call | flops 34359738368 | bytes 8388608 | tf_op jit(solution)/shard_map/pallas_call | solution.py:159
  408.4 3.7 convolution_convert_fusion.4
  418.9 4.9 all-to-all-start.4
  432.4 4.3 fusion.20
  454.6 96.2 %shard_map.215 = (f32[32,1024]{1,0:T(8,128)S(1)}, f32[16,1024]{1,0:T(8,128)S(1)}, f32[16,1024]{1,0:T(8,128)S(1)}, f32[32,512]{1,0:T(8,128)S(1)}, f32[16,1024]{1,...) custom-call(bf16[32,32,1024]{2,1,0:T(8,128)(2,1)} %pad_maximum_fusion.4.refs_0_, ...), custom_call_target="tpu_custom_call" | custom-call | tf_op jit(solution)/shard_map/pallas_call | solution.py:388
  (216 shorter events, 109.4 us)
Async XLA Ops:
  7.2 196.9 %all-gather.3.cloned.1.call-start = ((), (), s32[]{:S(2)}) async-start(), calls=%async_computation.7 | async-start | bytes 11894784 | tf_op jit(solution)/shard_map/all_gather | solution.py:480
  9.0 215.9 %all-gather.5.cloned.1.call-start = ((), (), s32[]{:S(2)}) async-start(), calls=%async_computation.8 | async-start | bytes 5947392 | tf_op jit(solution)/shard_map/all_gather | solution.py:481
  103.5 9.2 %all-to-all-start.1 = ((bf16[2,2,512,256]{3,2,1,0:T(8,128)(2,1)}), bf16[2,2,512,256]{3,2,1,0:T(8,128)(2,1)S(1)}, u32[]{:S(2)}, u32[]{:S(2)}) async-start(bf16[2,2,512,256]{3,2,1,0:T(8,128)(2,1)} %pad_maximum_fusion.6), calls=%async_computation.1 | async-start | bytes 2097152 | tf_op jit(solution)/shard_map/all_to_all | solution.py:442
  112.6 9.4 %all-to-all-start = ((bf16[2,2,512,512]{3,2,1,0:T(8,128)(2,1)}), bf16[2,2,512,512]{3,2,1,0:T(8,128)(2,1)S(1)}, u32[]{:S(2)}, u32[]{:S(2)}) async-start(bf16[2,2,512,512]{3,2,1,0:T(8,128)(2,1)} %pad_maximum_fusion.1), calls=%async_computation | async-start | bytes 4194304 | tf_op jit(solution)/shard_map/all_to_all | solution.py:442
  155.3 11.0 %all-to-all-start.2 = ((bf16[2,2,512,512]{3,2,1,0:T(8,128)(2,1)}), bf16[2,2,512,512]{3,2,1,0:T(8,128)(2,1)S(1)}, u32[]{:S(2)}, u32[]{:S(2)}) async-start(bf16[2,2,512,512]{3,2,1,0:T(8,128)(2,1)} %get-tuple-element.33.o_ref), calls=%async_computation.2 | async-start | bytes 4194304 | tf_op jit(solution)/shard_map/all_to_all | solution.py:442
  159.2 395.7 %reduce-scatter.2.cloned.1.call-start = ((), (), s32[]{:S(2)}) async-start(), calls=%async_computation.9 | async-start | bytes 17842176 | tf_op jit(solution)/shard_map/reduce_scatter | solution.py:557
  161.6 36.2 %collective-permute-start.1 = (bf16[512,1024]{1,0:T(8,128)(2,1)}, bf16[512,1024]{1,0:T(8,128)(2,1)}, u32[]{:S(2)}, u32[]{:S(2)}) collective-permute-start(bf16[512,1024]{1,0:T(8,128)(2,1)} %dynamic-slice_bitcast_fusion), channel_id=1, source_target_pairs={{0,2},{2,0},{1,3},{3,1},{4,6},{6,4},{5,7},{7,5},{8,10},{10,8},{9,1... | collective-permute-start | bytes 3145736 | tf_op jit(solution)/shard_map/ppermute | solution.py:434
  161.7 10.9 %copy-start.43 = (f32[1024]{0:T(1024)}, f32[1024]{0:T(1024)S(1)}, u32[]{:S(2)}) copy-start(f32[1024]{0:T(1024)S(1)} %reshape.291) | copy-start | bytes 12292
  172.0 27.2 %copy-start.1 = (f32[1024,1024]{1,0:T(8,128)}, f32[1024,1024]{1,0:T(8,128)S(1)}, u32[]{:S(2)}) copy-start(f32[1024,1024]{1,0:T(8,128)S(1)} %get-tuple-element.90) | copy-start | bytes 12582916
  172.0 25.8 %copy-start.17 = (bf16[2,512,1024]{2,1,0:T(8,128)(2,1)S(1)}, bf16[2,512,1024]{2,1,0:T(8,128)(2,1)}, u32[]{:S(2)}) copy-start(bf16[2,512,1024]{2,1,0:T(8,128)(2,1)} %param.14) | copy-start | bytes 6291460
  172.6 26.6 %copy-start.45 = (f32[1024]{0:T(1024)}, f32[1024]{0:T(1024)S(1)}, u32[]{:S(2)}) copy-start(f32[1024]{0:T(1024)S(1)} %get-tuple-element.86) | copy-start | bytes 12292
  204.1 12.1 %copy-start.24 = (bf16[1024,1024]{1,0:T(8,128)(2,1)S(1)}, bf16[1024,1024]{1,0:T(8,128)(2,1)}, u32[]{:S(2)}) copy-start(bf16[1024,1024]{1,0:T(8,128)(2,1)} %multiply_convert_fusion.3) | copy-start | bytes 6291460
  204.1 12.1 %copy-start.49 = (bf16[1024,5632]{1,0:T(8,128)(2,1)S(1)}, bf16[1024,5632]{1,0:T(8,128)(2,1)}, u32[]{:S(2)}) copy-start(bf16[1024,5632]{1,0:T(8,128)(2,1)} %all-gather.3.cloned.1.call-done) | copy-start | bytes 34603012
  304.6 14.3 %slice-start = ((s8[5767168]{0:T(1024)(128)(4,1)}), s8[4194304]{0:T(1024)(128)(4,1)S(1)}, s32[]{:S(2)}) async-start(s8[5767168]{0:T(1024)(128)(4,1)} %bitcast.238), calls=%async_computation.10 | async-start | bytes 8388608
  305.7 13.3 %copy-start.2 = (f32[1024,1024]{1,0:T(8,128)S(1)}, f32[1024,1024]{1,0:T(8,128)}, u32[]{:S(2)}) copy-start(f32[1024,1024]{1,0:T(8,128)} %copy-done.1) | copy-start | bytes 12582916
  305.7 13.3 %copy-start.44 = (f32[1024]{0:T(1024)S(1)}, f32[1024]{0:T(1024)}, u32[]{:S(2)}) copy-start(f32[1024]{0:T(1024)} %copy-done.43) | copy-start | bytes 12292
  305.7 13.3 %copy-start.46 = (f32[1024]{0:T(1024)S(1)}, f32[1024]{0:T(1024)}, u32[]{:S(2)}) copy-start(f32[1024]{0:T(1024)} %copy-done.45) | copy-start | bytes 12292
  305.7 13.3 %slice-start.1 = ((s8[5767168]{0:T(1024)(128)(4,1)}), s8[1572864]{0:T(1024)(128)(4,1)S(1)}, s32[]{:S(2)}) async-start(s8[5767168]{0:T(1024)(128)(4,1)} %bitcast.238), calls=%async_computation.11 | async-start | bytes 3145728
  305.7 246.3 %collective-permute-start = (bf16[512,1024]{1,0:T(8,128)(2,1)}, bf16[512,1024]{1,0:T(8,128)(2,1)}, u32[]{:S(2)}, u32[]{:S(2)}) collective-permute-start(bf16[512,1024]{1,0:T(8,128)(2,1)} %dynamic-slice_bitcast_fusion.1), channel_id=1, source_target_pairs={{0,2},{2,0},{1,3},{3,1},{4,6},{6,4},{5,7},{7,5},{8,10},{10,8},{9,1... | collective-permute-start | bytes 3145736 | tf_op jit(solution)/shard_map/ppermute | solution.py:434
  319.0 10.2 %copy-start.4 = (f32[2,512,1024]{2,1,0:T(8,128)S(1)}, f32[2,512,1024]{2,1,0:T(8,128)}, u32[]{:S(2)}) copy-start(f32[2,512,1024]{2,1,0:T(8,128)} %copy-done.3) | copy-start | bytes 12582916
  342.4 66.1 %copy-start.38 = (bf16[32,16,1024]{2,1,0:T(8,128)(2,1)S(1)}, bf16[32,16,1024]{2,1,0:T(8,128)(2,1)}, u32[]{:S(2)}) copy-start(bf16[32,16,1024]{2,1,0:T(8,128)(2,1)} %get-tuple-element.32) | copy-start | bytes 3145732
  413.2 5.7 %all-to-all-start.5 = ((bf16[2,2,512,256]{3,2,1,0:T(8,128)(2,1)}), bf16[2,2,512,256]{3,2,1,0:T(8,128)(2,1)S(1)}, u32[]{:S(2)}, u32[]{:S(2)}) async-start(bf16[2,2,512,256]{3,2,1,0:T(8,128)(2,1)} %bitcast.199), calls=%async_computation.5 | async-start | bytes 2097152 | tf_op jit(solution)/shard_map/all_to_all | solution.py:442
  418.9 7.9 %all-to-all-start.4 = ((bf16[2,2,512,512]{3,2,1,0:T(8,128)(2,1)}), bf16[2,2,512,512]{3,2,1,0:T(8,128)(2,1)}, u32[]{:S(2)}, u32[]{:S(2)}) async-start(bf16[2,2,512,512]{3,2,1,0:T(8,128)(2,1)} %get-tuple-element.36), calls=%async_computation.4 | async-start | bytes 4194304 | tf_op jit(solution)/shard_map/all_to_all | solution.py:442
  454.6 97.5 %copy-start.19 = (bf16[1024,1024]{1,0:T(8,128)(2,1)S(1)}, bf16[1024,1024]{1,0:T(8,128)(2,1)}, u32[]{:S(2)}) copy-start(bf16[1024,1024]{1,0:T(8,128)(2,1)} %copy-done.18) | copy-start | bytes 6291460
  (44 other events, 145.7 us)
Sparse Core Ops, SparseCore 0:
  11.4 109.5 all-gather.2
  123.9 74.2 all-gather.4
  286.3 206.2 reduce-scatter.1

commit v3 on v1

--- a/solution.py
+++ b/solution.py
@@ -12,8 +12,407 @@
 BF = jnp.bfloat16
 
 
-def low_half(x):
-    return jnp.concatenate([x[:, :DH], jnp.zeros((x.shape[0], DH), x.dtype)], axis=1)
+def cost(flops):
+    return pl.CostEstimate(flops=flops, bytes_accessed=2**23, transcendentals=0)
+
+
+MESH = pl.DeviceIdType.MESH
+
+
+class Place:
+
+    def __init__(self, dp):
+        self.sizes = {"x": 2, "y": 2, "z": dp // 2}
+        d = lax.axis_index("dp")
+        self.at = {"x": lax.axis_index("seq"), "y": lax.rem(d, 2), "z": lax.div(d, 2)}
+        self.core = lax.axis_index("grp")
+
+    def coords(self, offset):
+        at = {k: lax.rem(self.at[k] + o, self.sizes[k]) if o else self.at[k] for k, o in offset.items()}
+        return at["z"] * 2 + at["y"], at["x"]
+
+    def index(self, offset, other):
+        d, s = self.coords(offset)
+        core = 1 - self.core if other else self.core
+        return (d * 2 + s) * 2 + core
+
+    def device(self, offset):
+        return (*self.coords(offset), self.core)
+
+    def pair(self):
+        return (*self.coords({"x": 0, "y": 0, "z": 0}), 1 - self.core)
+
+    def greet(self):
+        there = [self.pair()]
+        for k in "xyz":
+            for o in range(1, self.sizes[k]):
+                there.append(self.device({"x": 0, "y": 0, "z": 0, k: o}))
+        barrier = pltpu.get_barrier_semaphore()
+        for device in there:
+            pl.semaphore_signal(barrier, inc=1, device_id=device, device_id_type=MESH)
+        pl.semaphore_wait(barrier, len(there))
+
+
+def offsets_of(order, dp):
+    sizes = {"x": 2, "y": 2, "z": dp // 2}
+    a, b, c = (sizes[k] for k in order)
+    return [(i, j, k) for i in range(a) for j in range(b) for k in range(c)]
+
+
+def named(order, steps):
+    return dict(zip(order, steps))
+
+
+def remote(src, dst, send, recv, there):
+    return pltpu.make_async_remote_copy(
+        src_ref=src, dst_ref=dst, send_sem=send, recv_sem=recv, device_id=there, device_id_type=MESH
+    )
+
+
+class Gather:
+
+    def __init__(self, place, dp, order, src, out, sems, number):
+        self.place, self.order, self.src, self.out = place, order, src, out
+        self.steps = offsets_of(order, dp)
+        self.sems, self.number = sems, number
+
+    def slot(self, steps, other=False):
+        return self.out(self.place.index(named(self.order, steps), other))
+
+    def source(self, steps):
+        last = max(i for i in range(3) if steps[i])
+        return tuple(0 if i == last else o for i, o in enumerate(steps))
+
+    def hop(self, steps):
+        last = max(i for i in range(3) if steps[i])
+        source = self.source(steps)
+        size = self.place.sizes[self.order[last]]
+        back = tuple(size - o if i == last else 0 for i, o in enumerate(steps))
+        number = self.steps.index(steps)
+        here = self.slot(source)
+        src = here if any(source) else self.src
+        return remote(
+            src,
+            here,
+            self.sems[0].at[self.number, number],
+            self.sems[1].at[self.number, number],
+            self.place.device(named(self.order, back)),
+        )
+
+    def across(self, steps):
+        number = self.steps.index(steps)
+        src = self.slot(steps) if any(steps) else self.src
+        return remote(
+            src,
+            self.slot(steps),
+            self.sems[2].at[self.number, number],
+            self.sems[3].at[self.number, number],
+            self.place.pair(),
+        )
+
+    def keep(self):
+        return pltpu.make_async_copy(self.src, self.slot((0, 0, 0)), self.sems[4].at[self.number])
+
+    def send_from(self, source):
+        for steps in self.steps:
+            if any(steps) and self.source(steps) == source:
+                self.hop(steps).start()
+        self.across(source).start()
+
+    def start(self):
+        self.send_from((0, 0, 0))
+        self.keep().start()
+
+    def arrivals(self):
+        return sorted((s for s in self.steps if any(s)), key=lambda s: [o > 0 for o in s][::-1])
+
+    def forward(self, steps):
+        number = self.steps.index(steps)
+        here = self.slot(steps)
+        remote(
+            here,
+            here,
+            self.sems[0].at[self.number, number],
+            self.sems[1].at[self.number, number],
+            self.place.pair(),
+        ).wait_recv()
+        self.send_from(steps)
+
+    def finish(self):
+        for steps in self.steps:
+            number = self.steps.index(steps)
+            here = self.slot(steps, True)
+            remote(
+                here,
+                here,
+                self.sems[2].at[self.number, number],
+                self.sems[3].at[self.number, number],
+                self.place.pair(),
+            ).wait_recv()
+            self.across(steps).wait_send()
+            if any(steps):
+                self.hop(steps).wait_send()
+        self.keep().wait()
+
+
+class Scatter:
+
+    def __init__(self, place, dp, order, term, pair_buf, ring_buf, sems, number, own=None):
+        self.place, self.order, self.term = place, order, term
+        self.own_buf, self.own_sem = own if own else (None, None)
+        self.steps = offsets_of(order, dp)
+        self.pair_buf, self.ring_buf = pair_buf, ring_buf
+        self.sems, self.number = sems, number
+
+    def turn(self):
+        def key(steps):
+            first = next((i for i in range(3) if steps[i]), 3)
+            return (first, [o == 0 for o in steps])
+
+        return sorted(self.steps, key=key)
+
+    def across(self, steps):
+        number = self.steps.index(steps)
+        return remote(
+            self.term(self.place.index(named(self.order, steps), True)),
+            self.pair_buf.at[number],
+            self.sems[2].at[self.number, number],
+            self.sems[3].at[self.number, number],
+            self.place.pair(),
+        )
+
+    def fetch(self, steps):
+        number = self.steps.index(steps)
+        return pltpu.make_async_copy(
+            self.term(self.place.index(named(self.order, steps), False)),
+            self.own_buf.at[number],
+            self.own_sem.at[self.number, number],
+        )
+
+    def start(self):
+        for steps in self.turn():
+            self.across(steps).start()
+            if self.own_buf is not None:
+                self.fetch(steps).start()
+
+    def hop(self, steps):
+        first = min(i for i in range(3) if steps[i])
+        there = tuple(o if i == first else 0 for i, o in enumerate(steps))
+        number = self.steps.index(steps)
+        return remote(
+            self.pair_buf.at[number],
+            self.ring_buf.at[number],
+            self.sems[0].at[self.number, number],
+            self.sems[1].at[self.number, number],
+            self.place.device(named(self.order, there)),
+        )
+
+    def add(self, steps, out=None):
+        number = self.steps.index(steps)
+        self.across(steps).wait_recv()
+        if self.own_buf is None:
+            mine = self.term(self.place.index(named(self.order, steps), False))
+        else:
+            self.fetch(steps).wait()
+            mine = self.own_buf.at[number]
+        total = mine[...].astype(F32) + self.pair_buf[number].astype(F32)
+        for came in self.steps:
+            if not any(came):
+                continue
+            first = min(i for i in range(3) if came[i])
+            if tuple(0 if i == first else o for i, o in enumerate(came)) == steps:
+                self.hop(came).wait_recv()
+                total = total + self.ring_buf[self.steps.index(came)].astype(F32)
+        if out is None:
+            self.pair_buf[number] = total.astype(BF)
+            self.hop(steps).start()
+        else:
+            out[...] = total
+
+    def finish(self):
+        for steps in self.steps:
+            self.across(steps).wait_send()
+            if any(steps):
+                self.hop(steps).wait_send()
+
+
+def block_swap(x_in, x_out, sem, place):
+    s = place.at["x"]
+    away = remote(
+        x_in.at[1 - s], x_out.at[s], sem.at[0], sem.at[1], place.device({"x": 1, "y": 0, "z": 0})
+    )
+    return away, pltpu.make_async_copy(x_in.at[s], x_out.at[s], sem.at[2])
+
+
+def gather_kernel(dp, orders, *refs):
+    count = len(orders)
+    srcs, x_in = refs[:count], refs[count]
+    outs, x_out = refs[count + 1 : 2 * count + 1], refs[2 * count + 1]
+    sems, x_sem = refs[2 * count + 2 : -1], refs[-1]
+    place = Place(dp)
+    place.greet()
+    works = [
+        Gather(place, dp, orders[a], srcs[a], lambda at, a=a: outs[a].at[at], sems, a)
+        for a in range(count)
+    ]
+    for work in works:
+        work.start()
+    swap, kept = block_swap(x_in, x_out, x_sem, place)
+    swap.start()
+    kept.start()
+    for i in range(2 * dp - 1):
+        for work in works:
+            work.forward(work.arrivals()[i])
+    for work in works:
+        work.finish()
+    swap.wait()
+    kept.wait()
+
+
+def gather_sems(dp, count):
+    sem = pltpu.SemaphoreType.DMA
+    return [sem((count, 2 * dp))] * 4 + [sem((count,))]
+
+
+def own_gather(dp, shards, blocks, orders):
+    count = len(shards)
+    anywhere = pl.BlockSpec(memory_space=pl.ANY)
+    out = pl.pallas_call(
+        functools.partial(gather_kernel, dp, orders),
+        in_specs=[anywhere] * (count + 1),
+        out_specs=[anywhere] * (count + 1),
+        out_shape=[jax.ShapeDtypeStruct((4 * dp, *w.shape), w.dtype) for w in shards]
+        + [jax.ShapeDtypeStruct(blocks.shape, blocks.dtype)],
+        scratch_shapes=gather_sems(dp, count) + [pltpu.SemaphoreType.DMA((3,))],
+        compiler_params=pltpu.CompilerParams(collective_id=0, has_side_effects=True),
+    )(*shards, blocks)
+    return out[:-1], out[-1]
+
+
+def scatter_kernel(dp, orders, late, *refs):
+    count = len(orders)
+    terms, x_in = refs[:count], refs[count]
+    outs, x_out = refs[count + 1 : 2 * count + 1], refs[2 * count + 1]
+    rest = refs[2 * count + 2 :]
+    pair_bufs, ring_bufs = rest[:count], rest[count : 2 * count]
+    sems, x_sem = rest[2 * count : -1], rest[-1]
+    place = Place(dp)
+    place.greet()
+    works = [
+        Scatter(
+            place, dp, orders[a], lambda at, a=a: terms[a].at[at], pair_bufs[a], ring_bufs[a], sems, a
+        )
+        for a in range(count)
+    ]
+    swap, kept = block_swap(x_in, x_out, x_sem, place)
+    for work in works:
+        work.start()
+    turns = [work.turn() for work in works]
+    for i in range(len(turns[0])):
+        if i == late:
+            swap.start()
+            kept.start()
+        for a in range(count):
+            works[a].add(turns[a][i], outs[a] if i == len(turns[0]) - 1 else None)
+    for work in works:
+        work.finish()
+    swap.wait()
+    kept.wait()
+
+
+def scatter_sems(dp, count):
+    return [pltpu.SemaphoreType.DMA((count, 2 * dp))] * 4
+
+
+def own_scatter(dp, terms, orders, blocks, late=0):
+    count = len(terms)
+    anywhere = pl.BlockSpec(memory_space=pl.ANY)
+    inside = pl.BlockSpec(memory_space=pltpu.VMEM)
+    out = pl.pallas_call(
+        functools.partial(scatter_kernel, dp, orders, late),
+        in_specs=[inside] * count + [anywhere],
+        out_specs=[inside] * count + [anywhere],
+        out_shape=[jax.ShapeDtypeStruct(w.shape[1:], F32) for w in terms]
+        + [jax.ShapeDtypeStruct(blocks.shape, blocks.dtype)],
+        scratch_shapes=[pltpu.VMEM((2 * dp, *w.shape[1:]), BF) for w in terms] * 2
+        + scatter_sems(dp, count)
+        + [pltpu.SemaphoreType.DMA((3,))],
+        compiler_params=pltpu.CompilerParams(
+            collective_id=1, has_side_effects=True, vmem_limit_bytes=48 * 2**20
+        ),
+    )(*terms, blocks)
+    return out[:-1], out[-1]
+
+
+def run_at(plan, point):
+    for step in sorted({k[0] for k in plan if k[1] == point}):
+        tasks = plan[step, point]
+
+        @pl.when(pl.program_id(0) == step)
+        def _(tasks=tasks):
+            for task in tasks:
+                task()
+
+
+def gather_plan(place, works, swap, steps, points):
+    arrivals = [work.arrivals() for work in works]
+    total = steps * points
+
+    def begin():
+        place.greet()
+        for work in works:
+            work.start()
+        for copy in swap:
+            copy.start()
+
+    def forward(i):
+        for work, order in zip(works, arrivals):
+            work.forward(order[i])
+
+    def end():
+        for work in works:
+            work.finish()
+        for copy in swap:
+            copy.wait()
+
+    plan = {}
+    count = len(arrivals[0])
+    plan[0, 0] = [begin]
+    for i in range(count):
+        at = 2 + i * (total - 3) // count
+        plan.setdefault(divmod(at, points), []).append(functools.partial(forward, i))
+    plan.setdefault(divmod(total, points), []).append(end)
+    return plan
+
+
+def scatter_plan(place, works, outs, swap, steps, points):
+    turns = [work.turn() for work in works]
+    total = steps * points
+    count = len(turns[0])
+
+    def begin():
+        place.greet()
+        for work in works:
+            work.start()
+        for copy in swap:
+            copy.start()
+
+    def add(i):
+        for work, order, out in zip(works, turns, outs):
+            work.add(order[i], out if i == count - 1 else None)
+
+    def end():
+        for work in works:
+            work.finish()
+        for copy in swap:
+            copy.wait()
+
+    plan = {(0, 0): [begin]}
+    for i in range(count):
+        at = 1 + i // 2 if i < count // 2 else 6 + (i - count // 2) * (total - 6) // (count - count // 2)
+        plan.setdefault(divmod(at, points), []).append(functools.partial(add, i))
+    plan.setdefault(divmod(total, points), []).append(end)
+    return plan
 
 
 def dot_nt(a, b):
@@ -30,12 +429,13 @@
     return jnp.where(rows >= keys, s, -1e30)
 
 
-def forward_kernel(q_ref, kv_ref, o_ref, lse_ref, vt_s):
+def forward_body(q_ref, kv_ref, o_ref, lse_ref, vt_s, point=lambda i: None):
     groups, chunks, rows, _ = q_ref.shape
     seq = kv_ref.shape[0]
     for h in range(2):
         vt_s[h] = kv_ref[:, h * 128 : (h + 1) * 128].astype(F32).T[DH:].astype(BF)
     for i in range(groups * chunks):
+        point(i)
         q = q_ref[i % groups, i // groups].astype(F32) * 0.125
         outs = []
         for h in range(2):
@@ -65,32 +465,93 @@
         o_ref[i % groups, i // groups] = jnp.concatenate(outs, axis=0).T.astype(BF)
 
 
-def attention_forward(q, kv):
+def forward_kernel(q_ref, kv_ref, o_ref, lse_ref, vt_s):
+    forward_body(q_ref, kv_ref, o_ref, lse_ref, vt_s)
+
+
+def forward_gather_kernel(dp, cuts, orders, pairs, *refs):
+    q_ref, kv_ref, x_in = refs[:3]
+    sources = 1 + max(cut[0] for cut in cuts)
+    srcs, refs = refs[3 : 3 + sources], refs[3 + sources :]
+    o_ref, lse_ref, x_out = refs[:3]
+    outs, refs = refs[3 : 3 + sources], refs[3 + sources :]
+    vt_s, x_sem, sems = refs[0], refs[1], refs[2:]
+    place = Place(dp)
+    works = []
+    for number, (a, first, size) in enumerate(cuts):
+        cut = pl.ds(first, size)
+        works.append(
+            Gather(
+                place,
+                dp,
+                orders[number],
+                srcs[a].at[:, cut],
+                lambda at, a=a, cut=cut: outs[a].at[at, :, cut],
+                sems,
+                number,
+            )
+        )
+    points = q_ref.shape[0] * q_ref.shape[1]
+    plan = gather_plan(place, works, block_swap(x_in, x_out, x_sem, place), pairs, points)
+    forward_body(q_ref, kv_ref, o_ref, lse_ref, vt_s, lambda i: run_at(plan, i))
+    for point in range(points):
+        tasks = plan.get((pairs, point))
+        if tasks:
+
+            @pl.when(pl.program_id(0) == pairs - 1)
+            def _(tasks=tasks):
+                for task in tasks:
+                    task()
+
+
+def forward_specs(q, kv):
     groups, chunks, rows, cols = q.shape
     seq = kv.shape[0]
     pairs = cols // 128
+    tok = pl.BlockSpec((groups, chunks, rows, 128), lambda p: (0, 0, 0, p))
+    ins = [tok, pl.BlockSpec((seq, 256), lambda p: (0, p))]
+    outs = [tok, pl.BlockSpec((None, 2, seq), lambda p: (p, 0, 0))]
+    shapes = [jax.ShapeDtypeStruct(q.shape, BF), jax.ShapeDtypeStruct((pairs, 2, seq), F32)]
+    scratch = [pltpu.VMEM((2, DH, seq), BF)]
+    return pairs, ins, outs, shapes, scratch, cost(8 * pairs * seq * seq * 128)
+
+
+def attention_forward(q, kv):
+    pairs, ins, outs, shapes, scratch, estimate = forward_specs(q, kv)
     return pl.pallas_call(
         forward_kernel,
         grid=(pairs,),
-        in_specs=[
-            pl.BlockSpec((groups, chunks, rows, 128), lambda p: (0, 0, 0, p)),
-            pl.BlockSpec((seq, 256), lambda p: (0, p)),
-        ],
-        out_specs=[
-            pl.BlockSpec((groups, chunks, rows, 128), lambda p: (0, 0, 0, p)),
-            pl.BlockSpec((None, 2, seq), lambda p: (p, 0, 0)),
-        ],
-        out_shape=[
-            jax.ShapeDtypeStruct(q.shape, BF),
-            jax.ShapeDtypeStruct((pairs, 2, seq), F32),
-        ],
-        scratch_shapes=[pltpu.VMEM((2, DH, seq), BF)],
+        in_specs=ins,
+        out_specs=outs,
+        out_shape=shapes,
+        scratch_shapes=scratch,
         compiler_params=pltpu.CompilerParams(vmem_limit_bytes=56 * 2**20),
+        cost_estimate=estimate,
     )(q, kv)
 
 
-def backward_kernel(blk, q_ref, kv_ref, do_ref, o_ref, lse_ref, dq_ref, dkv_ref,
-                    kt_s, acc_s, dqt_s, qp_s, dop_s, delta_s):
+def attention_forward_gather(dp, q, kv, blocks, shards, cuts, orders):
+    pairs, ins, outs, shapes, scratch, estimate = forward_specs(q, kv)
+    anywhere = pl.BlockSpec(memory_space=pl.ANY)
+    count = len(shards)
+    return pl.pallas_call(
+        functools.partial(forward_gather_kernel, dp, cuts, orders, pairs),
+        grid=(pairs,),
+        in_specs=ins + [anywhere] * (1 + count),
+        out_specs=outs + [anywhere] * (1 + count),
+        out_shape=shapes
+        + [jax.ShapeDtypeStruct(blocks.shape, blocks.dtype)]
+        + [jax.ShapeDtypeStruct((4 * dp, *w.shape), w.dtype) for w in shards],
+        scratch_shapes=scratch + [pltpu.SemaphoreType.DMA((3,))] + gather_sems(dp, len(cuts)),
+        compiler_params=pltpu.CompilerParams(
+            vmem_limit_bytes=56 * 2**20, collective_id=2, has_side_effects=True
+        ),
+        cost_estimate=estimate,
+    )(q, kv, blocks, *shards)
+
+
+def backward_body(blk, q_ref, kv_ref, do_ref, o_ref, lse_ref, dq_ref, dkv_ref,
+                  kt_s, acc_s, dqt_s, qp_s, dop_s, delta_s, point=lambda i: None):
     groups, chunks, rows, _ = q_ref.shape
     seq = kv_ref.shape[0]
     n = groups * chunks
@@ -111,7 +572,7 @@
             delta_s[h, at] = jnp.sum(prod[cut], axis=0)
 
     def block(i, j, masked):
-        qat = pl.ds(pl.multiple_of(i * blk, blk), blk)
+        qat = pl.ds(i * blk, blk)
         kat = pl.ds(pl.multiple_of(j * blk, blk), blk)
         for h in range(2):
             kv = kv_ref[kat, h * 128 : (h + 1) * 128]
@@ -132,17 +593,15 @@
 
     m = seq // blk
 
-    def outer(i, _):
+    for i in range(m):
+        point(i)
         block(i, i, True)
 
-        def inner(j, _):
+        def inner(j, _, i=i):
             block(i, j, False)
             return 0
 
         lax.fori_loop(0, i, inner, 0)
-        return 0
-
-    lax.fori_loop(0, m, outer, 0)
     for i in range(n):
         at = pl.ds(i * rows, rows)
         dq_ref[i % groups, i // groups] = (dqt_s[:, at].T * 0.125).astype(BF)
@@ -150,28 +609,108 @@
         dkv_ref[:, h * 128 : (h + 1) * 128] = acc_s[h].astype(BF)
 
 
-def attention_backward(q, kv, do, o, lse, blk=512):
+def backward_kernel(blk, *refs):
+    backward_body(blk, *refs)
+
+
+def backward_scatter_kernel(dp, blk, cuts, orders, pairs, *refs):
+    ins, x_in, refs = refs[:5], refs[5], refs[6:]
+    sources = 1 + max(cut[0] for cut in cuts)
+    count = len(cuts)
+    terms, refs = refs[:sources], refs[sources:]
+    attn_outs, x_out, refs = refs[:2], refs[2], refs[3:]
+    outs, refs = refs[:sources], refs[sources:]
+    scratch, x_sem, refs = refs[:6], refs[6], refs[7:]
+    own_bufs, pair_bufs, ring_bufs = refs[:count], refs[count : 2 * count], refs[2 * count : 3 * count]
+    own_sem, sems = refs[3 * count], refs[3 * count + 1 :]
+    place = Place(dp)
+    works, targets = [], []
+    for number, (a, first, size) in enumerate(cuts):
+        cut = pl.ds(first, size)
+        works.append(
+            Scatter(
+                place,
+                dp,
+                orders[number],
+                lambda at, a=a, cut=cut: terms[a].at[at, :, cut],
+                pair_bufs[number],
+                ring_bufs[number],
+                sems,
+                number,
+                (own_bufs[number], own_sem),
+            )
+        )
+        targets.append(outs[a].at[:, cut])
+    points = ins[1].shape[0] // blk
+    plan = scatter_plan(place, works, targets, block_swap(x_in, x_out, x_sem, place), pairs, points)
+    backward_body(blk, *ins, *attn_outs, *scratch, point=lambda i: run_at(plan, i))
+    for point in range(points):
+        tasks = plan.get((pairs, point))
+        if tasks:
+
+            @pl.when(pl.program_id(0) == pairs - 1)
+            def _(tasks=tasks):
+                for task in tasks:
+                    task()
+
+
+def backward_specs(q, kv):
     groups, chunks, rows, cols = q.shape
     seq = kv.shape[0]
     pairs = cols // 128
     tok = pl.BlockSpec((groups, chunks, rows, 128), lambda p: (0, 0, 0, p))
+    wide = pl.BlockSpec((seq, 256), lambda p: (0, p))
+    ins = [tok, wide, tok, tok, pl.BlockSpec((None, 2, seq), lambda p: (p, 0, 0))]
+    outs = [tok, wide]
+    shapes = [jax.ShapeDtypeStruct(q.shape, BF), jax.ShapeDtypeStruct(kv.shape, BF)]
+    scratch = [
+        pltpu.VMEM((2, DH, seq), BF),
+        pltpu.VMEM((2, seq, 128), F32),
+        pltpu.VMEM((128, seq), F32),
+        pltpu.VMEM((2, seq, 128), BF),
+        pltpu.VMEM((2, seq, 128), BF),
+        pltpu.VMEM((2, seq), F32),
+    ]
+    return pairs, ins, outs, shapes, scratch, cost(16 * pairs * seq * seq * 128)
+
+
+def attention_backward(q, kv, do, o, lse, blk=512):
+    pairs, ins, outs, shapes, scratch, estimate = backward_specs(q, kv)
     return pl.pallas_call(
         functools.partial(backward_kernel, blk),
         grid=(pairs,),
-        in_specs=[tok, pl.BlockSpec((seq, 256), lambda p: (0, p)), tok, tok,
-                  pl.BlockSpec((None, 2, seq), lambda p: (p, 0, 0))],
-        out_specs=[tok, pl.BlockSpec((seq, 256), lambda p: (0, p))],
-        out_shape=[jax.ShapeDtypeStruct(q.shape, BF), jax.ShapeDtypeStruct(kv.shape, BF)],
-        scratch_shapes=[
-            pltpu.VMEM((2, DH, seq), BF),
-            pltpu.VMEM((2, seq, 128), F32),
-            pltpu.VMEM((128, seq), F32),
-            pltpu.VMEM((2, seq, 128), BF),
-            pltpu.VMEM((2, seq, 128), BF),
-            pltpu.VMEM((2, seq), F32),
-        ],
+        in_specs=ins,
+        out_specs=outs,
+        out_shape=shapes,
+        scratch_shapes=scratch,
         compiler_params=pltpu.CompilerParams(vmem_limit_bytes=56 * 2**20),
+        cost_estimate=estimate,
     )(q, kv, do, o, lse)
+
+
+def attention_backward_scatter(dp, q, kv, do, o, lse, blocks, terms, cuts, orders, blk=512):
+    pairs, ins, outs, shapes, scratch, estimate = backward_specs(q, kv)
+    anywhere = pl.BlockSpec(memory_space=pl.ANY)
+    count = len(cuts)
+    bufs = [pltpu.VMEM((2 * dp, terms[a].shape[1], size), BF) for a, _, size in cuts]
+    return pl.pallas_call(
+        functools.partial(backward_scatter_kernel, dp, blk, cuts, orders, pairs),
+        grid=(pairs,),
+        in_specs=ins + [anywhere] * (1 + len(terms)),
+        out_specs=outs + [anywhere] + [pl.BlockSpec(w.shape[1:], lambda p: (0, 0)) for w in terms],
+        out_shape=shapes
+        + [jax.ShapeDtypeStruct(blocks.shape, blocks.dtype)]
+        + [jax.ShapeDtypeStruct(w.shape[1:], F32) for w in terms],
+        scratch_shapes=scratch
+        + [pltpu.SemaphoreType.DMA((3,))]
+        + bufs * 3
+        + [pltpu.SemaphoreType.DMA((count, 2 * dp))]
+        + scatter_sems(dp, count),
+        compiler_params=pltpu.CompilerParams(
+            vmem_limit_bytes=60 * 2**20, collective_id=3, has_side_effects=True
+        ),
+        cost_estimate=estimate,
+    )(q, kv, do, o, lse, blocks, *terms)
 
 
 HEADS = 16
@@ -240,28 +779,27 @@
     cols = heads * DH
     drows = width // devices
 
-    gains = jnp.concatenate(
-        [norm_gain[:, None], ffn_gain[:, None], jnp.zeros((drows, 126), BF)], axis=1
-    )
-    expand_rows = expansion_weight.reshape(drows, -1)
-    attn_weights = jnp.concatenate([w_query, w_latent, w_output, expand_rows, gains], axis=1)
-    attn_full = lax.all_gather(attn_weights, ALL, axis=0, tiled=True)
+    dp = lax.axis_size("dp")
+    ring = groups == 2 and seqs == 2 and dp % 2 == 0
+    expand_rows = expansion_weight.reshape(-1, expansion_weight.shape[2])
+    gains = jnp.pad(jnp.concatenate([norm_gain, ffn_gain])[None], ((0, 15), (0, 128 - 2 * drows)))
+    if ring:
+        shards = (w_query, w_latent, expand_rows, gains)
+        full, own_inputs = own_gather(dp, shards, inputs, ("xzy",) * 4)
+    else:
+        shards = (w_query, w_latent, expand_rows, gains, w_output)
+        full = [lax.all_gather(w, ALL, axis=0) for w in shards]
+        own_inputs = swap_sequences(inputs, seqs)
     ffn_full = lax.all_gather(jnp.concatenate([w_gate, w_up], axis=1), ALL, axis=0, tiled=True)
     down_full = lax.all_gather(w_down, ALL, axis=0, tiled=True)
-    query_full = attn_full[:, :width]
-    latent_full = attn_full[:, width : width + KVH * LATD]
-    output_full = attn_full[:, width + KVH * LATD : 2 * width + KVH * LATD]
-    ecols = expand_rows.shape[1]
-    at = 2 * width + KVH * LATD
-    expand_full = attn_full[:, at : at + ecols].reshape(devices, KVH, LATD // devices, -1)
-    expand_full = expand_full.transpose(1, 0, 2, 3).reshape(KVH, LATD, -1)
-    gain_one = attn_full[:, at + ecols].astype(F32)
-    gain_two = attn_full[:, at + ecols + 1].astype(F32)
+    query_full = full[0].reshape(width, -1)
+    latent_full = full[1].reshape(width, -1)
+    expand_full = full[2].reshape(devices, KVH, LATD // devices, -1)
+    gain_one = full[3][:, 0, :drows].reshape(width).astype(F32)
+    gain_two = full[3][:, 0, drows : 2 * drows].reshape(width).astype(F32)
     gate_full = ffn_full[:, :hidden_size]
     up_full = ffn_full[:, hidden_size:]
 
-    own_inputs = swap_sequences(inputs, seqs)
-    own_cotangent = swap_sequences(cotangent, seqs)
 
     token_rows = own_inputs.astype(F32).reshape(count, width)
     normed, inverse_one = norm_parts(token_rows, gain_one)
@@ -278,10 +816,20 @@
     head_queries = swap_group(query_send)
     head_latent = swap_group(latent_send).transpose(1, 0, 2, 3).reshape(-1, LATD)
     expand_local = lax.dynamic_slice(
-        expand_full, (me * heads // HG, 0, me * heads % HG * 2 * DH), (1, LATD, heads * 2 * DH)
-    )[0]
+        expand_full,
+        (0, me * heads // HG, 0, me * heads % HG * 2 * DH),
+        (devices, 1, LATD // devices, heads * 2 * DH),
+    ).reshape(LATD, -1)
     head_pairs = dot_nn(head_latent, expand_local).astype(BF)
-    attended, logsum = attention_forward(head_queries, head_pairs)
+    if ring:
+        attended, logsum, own_cotangent, output_full = attention_forward_gather(
+            dp, head_queries, head_pairs, cotangent, (w_output,), ((0, 0, width),), ("xzy",)
+        )
+    else:
+        attended, logsum = attention_forward(head_queries, head_pairs)
+        own_cotangent = swap_sequences(cotangent, seqs)
+        output_full = full[4]
+    output_full = output_full.reshape(-1, width)
     token_attended = swap_group(attended).reshape(groups, count, cols)
     branch = sum(
         dot_nn(token_attended[j], output_full[j * cols : (j + 1) * cols]) for j in range(groups)
@@ -295,7 +843,7 @@
     activated = gate_pre * sigmoid
     hidden = (activated * upward).astype(BF)
     result = middle + dot_nn(hidden, down_full)
-    output = swap_sequences(result.astype(BF).reshape(seqs, rows, width), seqs)
+    own_output = result.astype(BF).reshape(seqs, rows, width)
 
     seq_group = lax.dynamic_index_in_dim(group_ids, lax.axis_index("seq"), 0, keepdims=False)
     chosen = (seq_group == jnp.arange(GROUPS)).astype(F32)
@@ -311,15 +859,39 @@
     normed_two_back = dot_nt(gate_back, gate_full) + dot_nt(up_back, up_full)
     middle_part, gain_two_grad = norm_back(middle, inverse_two, gain_two, normed_two_back)
     middle_grad = upstream + middle_part
-    ffn_share = lax.psum_scatter(
-        jnp.concatenate([gate_grad.astype(BF), up_grad.astype(BF)], axis=1),
-        ALL,
-        scatter_dimension=0,
-        tiled=True,
-    ).astype(F32)
-    down_share = lax.psum_scatter(
-        down_grad.astype(BF), ALL, scatter_dimension=0, tiled=True
-    ).astype(F32)
+    if ring:
+        both = jnp.concatenate([gate_grad.astype(BF), up_grad.astype(BF)], axis=1).reshape(
+            devices, drows, -1
+        )
+        whole = both.shape[2] // width * width
+        half = drows // 2
+        packed = jnp.concatenate(
+            [both[:, :, a : a + width] for a in range(0, whole, width)]
+            + [
+                jnp.concatenate([both[:, :half, whole:], both[:, half:, whole:]], axis=2),
+                down_grad.astype(BF).reshape(devices, -1, width),
+            ],
+            axis=1,
+        )
+        share = lax.psum_scatter(packed, ALL, scatter_dimension=0, tiled=True)[0].astype(F32)
+        tall = whole // width * drows
+        tail = share[tall : tall + half]
+        ffn_share = jnp.concatenate(
+            [share[a : a + drows] for a in range(0, tall, drows)]
+            + [jnp.concatenate([tail[:, : width // 2], tail[:, width // 2 :]], axis=0)],
+            axis=1,
+        )
+        down_share = share[tall + half :]
+    else:
+        ffn_share = lax.psum_scatter(
+            jnp.concatenate([gate_grad.astype(BF), up_grad.astype(BF)], axis=1),
+            ALL,
+            scatter_dimension=0,
+            tiled=True,
+        ).astype(F32)
+        down_share = lax.psum_scatter(
+            down_grad.astype(BF), ALL, scatter_dimension=0, tiled=True
+        ).astype(F32)
 
     branch_low = middle_grad.astype(BF)
     output_grad = jnp.concatenate(
@@ -332,15 +904,22 @@
         ]
     ).reshape(groups, seqs, rows, cols)
     head_upstream = swap_group(back_send)
-    query_back, pair_back = attention_backward(
-        head_queries, head_pairs, head_upstream, attended, logsum
-    )
+    terms = output_grad.astype(BF).reshape(devices, drows, width)
+    attention = (head_queries, head_pairs, head_upstream, attended, logsum)
+    if ring:
+        query_back, pair_back, output, output_share = attention_backward_scatter(
+            dp, *attention, own_output, (terms,), ((0, 0, width),), ("yzx",)
+        )
+    else:
+        query_back, pair_back = attention_backward(*attention)
+        output = swap_sequences(own_output, seqs)
+        output_share = lax.psum_scatter(terms, ALL, scatter_dimension=0, tiled=True)[0].astype(F32)
     latent_terms = dot_nt(pair_back, expand_local).astype(BF)
     expand_part = dot_tn(head_latent, pair_back)
     expand_grad = lax.dynamic_update_slice(
-        jnp.zeros(expand_full.shape, F32),
-        expand_part[None],
-        (me * heads // HG, 0, me * heads % HG * 2 * DH),
+        jnp.zeros(expand_full.shape, BF),
+        expand_part.astype(BF).reshape(devices, 1, LATD // devices, -1),
+        (0, me * heads // HG, 0, me * heads % HG * 2 * DH),
     )
     query_token = swap_group(query_back).reshape(groups, count, cols)
     latent_token = swap_group(
@@ -355,42 +934,33 @@
         dot_nt(latent_token[g], latent_full[:, g * LATD : (g + 1) * LATD]) for g in range(KVH)
     )
     input_part, gain_one_grad = norm_back(token_rows, inverse_one, gain_one, normed_back)
-    input_grad = swap_sequences(
-        (middle_grad + input_part).astype(BF).reshape(seqs, rows, width), seqs
+    own_input_grad = (middle_grad + input_part).astype(BF).reshape(seqs, rows, width)
+    gain_grads = jnp.concatenate(
+        [gain_one_grad.reshape(devices, 1, drows), gain_two_grad.reshape(devices, 1, drows)], axis=2
+    ).astype(BF)
+    gain_grads = jnp.pad(gain_grads, ((0, 0), (0, 15), (0, 128 - 2 * drows)))
+    terms = (
+        query_grad.astype(BF).reshape(devices, drows, -1),
+        latent_grad.astype(BF).reshape(devices, drows, -1),
+        expand_grad.reshape(devices, -1, expand_grad.shape[3]),
+        gain_grads,
     )
-    expand_out = (
-        expand_grad.astype(BF)
-        .reshape(KVH, devices, LATD // devices, -1)
-        .transpose(1, 0, 2, 3)
-        .reshape(width, -1)
-    )
-    gain_grads = jnp.concatenate(
-        [gain_one_grad[:, None], gain_two_grad[:, None], jnp.zeros((width, 126), F32)], axis=1
-    )
-    attn_share = lax.psum_scatter(
-        jnp.concatenate(
-            [
-                query_grad.astype(BF),
-                latent_grad.astype(BF),
-                output_grad.astype(BF),
-                expand_out,
-                gain_grads.astype(BF),
-            ],
-            axis=1,
-        ),
-        ALL,
-        scatter_dimension=0,
-        tiled=True,
-    ).astype(F32)
+    if ring:
+        sums, input_grad = own_scatter(dp, terms, ("yzx",) * 4, own_input_grad)
+    else:
+        sums = [
+            lax.psum_scatter(w, ALL, scatter_dimension=0, tiled=True)[0].astype(F32) for w in terms
+        ]
+        input_grad = swap_sequences(own_input_grad, seqs)
     return (
         output,
         input_grad,
-        attn_share[:, at + ecols],
-        attn_share[:, :width],
-        attn_share[:, width : width + KVH * LATD],
-        attn_share[:, at : at + ecols].reshape(expansion_weight.shape),
-        attn_share[:, width + KVH * LATD : at],
-        attn_share[:, at + ecols + 1],
+        sums[3][0, :drows],
+        sums[0],
+        sums[1],
+        sums[2].reshape(expansion_weight.shape),
+        output_share,
+        sums[3][0, drows : 2 * drows],
         ffn_share[:, :hidden_size],
         ffn_share[:, hidden_size:],
         down_share,

time: 783 us -> 499 us (0.64)
  waiting for transfers between devices: 374 us -> 17.2 us
  Pallas kernels: 97.9 us -> 217 us
  matrix products: 162 us -> 140 us
  blocking collectives: 17.8 us -> 0 us
    reduce_scatter x3 -> x1, waiting for transfers between devices: 167 us -> 0.01 us  [local(): lax.psum_scatter(packed, ALL, scatter_dimension=0, tiled=True)[0]]
    ppermute x4 -> x0, waiting for transfers between devices: 132 us -> none  [swap_sequences(): sent = lax.ppermute(blocks[1 - me], 'seq', [(0, 1), (1, 0)])]
    pallas_call x2 -> x4, Pallas kernels: 97.9 us -> 217 us  [the longest x1 74.9 us: attention_backward_scatter(): pl.pallas_call(functools.partial(backward_scatter_kernel, dp, blk, cuts,...]
    all_gather x1, waiting for transfers between devices: 47.9 us -> 0.01 us  [local(): down_full = lax.all_gather(w_down, ALL, axis=0, tiled=True)]
    unnamed x59 -> x108, local copies, waits for them, and re-layouts: 2.59 us -> 24 us
    all_to_all x3 -> x0, blocking collectives: 17.8 us -> none  [swap_group(): return lax.all_to_all(blocks, 'grp', 0, 0, tiled=True)]
    dot_general x10, matrix products: 63.9 us -> 46.8 us  [dot_nt(): lax.dot_general(a, b, (((1,), (1,)), ((), ())), preferred_element_type=F32)]
    dot_general x10, matrix products: 49 us -> 36.5 us  [dot_tn(): lax.dot_general(a, b, (((0,), (0,)), ((), ())), preferred_element_type=F32)]
  transfers between devices with their start and end apart: 13 -> 9, of which waited for: 10 -> 3; matrix products, arithmetic and copies ran while one was open for 27% -> 26% of each run, Pallas kernels for 13% -> 44%
where the time goes in v3:
time: 499 us; the launch traced here: 493 us
  Pallas kernels  217 us (43%)
  matrix products  140 us (28%)
  local copies, waits for them, and re-layouts  41.6 us (8%)
  other arithmetic  36.9 us (7%)
  starting transfers between devices  25 us (5%)
  waiting for transfers between devices  17.2 us (3%)
  between operations  15 us (3%)
    pallas_call x1, Pallas kernels, attention_backward_scatter(): pl.pallas_call(functools.partial(backward_scatter_kernel, dp, blk, cuts,...  74.9 us
    dot_general x10, matrix products, dot_nn(): lax.dot_general(a, b, (((1,), (0,)), ((), ())), preferred_element_type=F32)  56.4 us
    pallas_call x1, Pallas kernels, attention_forward_gather(): pl.pallas_call(functools.partial(forward_gather_kernel, dp, cuts, orders,...  50.3 us
    pallas_call x1, Pallas kernels, own_gather(): pl.pallas_call(functools.partial(gather_kernel, dp, orders), in_specs=[an...  47 us
    dot_general x10, matrix products, dot_nt(): lax.dot_general(a, b, (((1,), (1,)), ((), ())), preferred_element_type=F32)  46.8 us
    pallas_call x1, Pallas kernels, own_scatter(): pl.pallas_call(functools.partial(scatter_kernel, dp, orders, late), in_sp...  45.3 us
    dot_general x10, matrix products, dot_tn(): lax.dot_general(a, b, (((0,), (0,)), ((), ())), preferred_element_type=F32)  36.5 us
    all_to_all x6, starting transfers between devices, swap_group(): return lax.all_to_all(blocks, 'grp', 0, 0, tiled=True)  24.7 us
  transfers between devices with their start and end apart: 9, of which 3 were waited for; matrix products, arithmetic and copies ran while one was open for 26% of the time, Pallas kernels for 44%

profile of v3, /device:TPU:0, one launch (start us, length us, event | category | flops | bytes accessed | tf_op | source)
XLA Modules:
  0.0 492.8 jit_solution(3267684816658816687)
XLA Ops:
  11.1 47.0 %shard_map.212 = (bf16[32,32,1024]{2,1,0:T(8,128)(2,1)}, bf16[32,32,512]{2,1,0:T(8,128)(2,1)}, bf16[32,16,1024]{2,1,0:T(8,128)(2,1)}, bf16[32,16,128]{2,1,0:T(8,128)(2,1)}, bf16[2,512,1024]{2,1,0:T(8,128)(2,1)}) custom-call(bf16[32,1024]{1,0:T(8,128)(2,1)} %refs_0_.1, bf16[32,512]{1,0:T(8,128)(2,1)} %refs_1_.1, bf16[16,1024]{1,0:T(8,128)(2,1)} %bitcast.209, ...), custom_call_target="tpu_custom_call" | custom-call | tf_op jit(solution)/shard_map/pallas_call | solution.py:280
  66.7 3.6 all-to-all-start.1
  75.7 3.9 all-to-all-start
  80.7 4.3 convolution_convert_fusion.3.refs_1_
  86.4 50.3 %shard_map.213 = (bf16[2,2,512,512]{3,2,1,0:T(8,128)(2,1)}, f32[4,2,2048]{2,1,0:T(2,128)}, bf16[2,512,1024]{2,1,0:T(8,128)(2,1)}, bf16[32,32,1024]{2,1,0:T(8,128)(2,1)}) custom-call(bf16[2,2,512,512]{3,2,1,0:T(8,128)(2,1)} %copy-done.20, bf16[2048,1024]{1,0:T(8,128)(2,1)} %convolution_convert_fusion.3.refs_1_, bf16[2,512,1024]{2,1,0:T(8,128)(2,1)} %refs_2_.1, ...), custom_call_target="tpu_custom_call" | custom-call | flops 17179869184 | bytes 8388608 | tf_op jit(solution)/shard_map/pallas_call | solution.py:537
  136.7 3.8 all-to-all-start.2
  158.2 11.8 %fusion.60 = f32[1024,2816]{1,0:T(8,128)} fusion(bf16[1024,1024]{1,0:T(8,128)(2,1)} %bitcast_convert_fusion, bf16[2816,1024]{1,0:T(8,128)(2,1)} %all-gather.3.cloned.1.call-done), kind=kOutput, calls=%fused_computation.138 | convolution fusion | flops 5905580032 | bytes 19398656 | tf_op jit(solution)/shard_map/dot_general | solution.py:419
  170.0 12.5 %all-gather.5.cloned.1.call-done = bf16[1024,5632]{1,0:T(8,128)(2,1)} async-done(((bf16[32,5632]{1,0:T(8,128)(2,1)}), bf16[1024,5632]{1,0:T(8,128)(2,1)}) %all-gather.5.cloned.1.call-update) | async-done | bytes 11534352 | tf_op jit(solution)/shard_map/all_gather | solution.py:793
  182.4 11.7 %fusion.3 = f32[1024,2816]{1,0:T(8,128)} fusion(bf16[1024,1024]{1,0:T(8,128)(2,1)} %multiply_convert_fusion.3, bf16[1024,5632]{1,0:T(8,128)(2,1)} %all-gather.5.cloned.1.call-done), kind=kOutput, calls=%fused_computation.11 | convolution fusion | flops 5905580032 | bytes 19398656 | tf_op jit(solution)/shard_map/dot_general | solution.py:423
  194.2 21.5 %multiply_convert_fusion = (bf16[1024,2816]{1,0:T(8,128)(2,1)}, bf16[1024,2816]{1,0:T(8,128)(2,1)}, bf16[1024,2816]{1,0:T(8,128)(2,1)}) fusion(f32[1024,2816]{1,0:T(8,128)} %fusion.3, f32[1024,2816]{1,0:T(8,128)} %fusion.60, bf16[1024,1024]{1,0:T(8,128)(2,1)} %multiply_convert_fusion.3, bf16[1024,5632]{1,0:T(8,128)(2,1)} %all-gather.5.cloned.1.call-done), kind=kOutput, calls=%fused_computation.1 | convolution fusion | flops 5948833792 | bytes 48234496 | tf_op jit(solution)/shard_map/dot_general | solution.py:423
  215.7 10.0 %convolution_convert_fusion.1 = bf16[1024,2816]{1,0:T(8,128)(2,1)S(1)} fusion(bf16[1024,1024]{1,0:T(8,128)(2,1)} %multiply_convert_fusion.3, bf16[1024,2816]{1,0:T(8,128)(2,1)} %get-tuple-element.57), kind=kOutput, calls=%fused_computation.7 | convolution fusion | flops 5908463616 | bytes 13631488 | tf_op jit(solution)/shard_map/dot_general | solution.py:740
  225.7 6.8 %convolution_convert_fusion.2 = bf16[1024,2816]{1,0:T(8,128)(2,1)S(1)} fusion(bf16[1024,1024]{1,0:T(8,128)(2,1)S(1)} %copy-done.23, bf16[1024,2816]{1,0:T(8,128)(2,1)S(1)} %copy-done.45), kind=kOutput, calls=%fused_computation.8 | convolution fusion | flops 5908463616 | bytes 13631488 | tf_op jit(solution)/shard_map/dot_general | solution.py:740
  232.4 4.1 pad_maximum_fusion
  244.7 6.6 %convolution_convert_fusion = bf16[2816,1024]{1,0:T(8,128)(2,1)S(1)} fusion(bf16[1024,2816]{1,0:T(8,128)(2,1)S(1)} %bitcast.212, bf16[1024,1024]{1,0:T(8,128)(2,1)S(1)} %copy-done.19), kind=kOutput, calls=%fused_computation.6 | convolution fusion | flops 5908463616 | bytes 13631488 | tf_op jit(solution)/shard_map/dot_general | solution.py:740
  258.1 4.1 copy.33
  262.2 10.7 %fusion.1 = f32[1024,1024]{1,0:T(8,128)S(1)} fusion(bf16[1024,2816]{1,0:T(8,128)(2,1)} %get-tuple-element.56, bf16[1024,5632]{1,0:T(8,128)(2,1)} %all-gather.5.cloned.1.call-done), kind=kOutput, calls=%fused_computation.9 | convolution fusion | flops 5905580032 | bytes 15728640 | tf_op jit(solution)/shard_map/dot_general | solution.py:419
  272.9 11.5 %multiply_reduce_fusion = (bf16[1024]{0:T(1024)(128)(2,1)S(1)}, f32[1024]{0:T(1024)S(1)}, f32[1024,1024]{1,0:T(8,128)S(1)}) fusion(f32[1024,1024]{1,0:T(8,128)S(1)} %copy-done.2, f32[1024]{0:T(1024)S(1)} %get-tuple-element.84, f32[1024]{0:T(1024)S(1)} %reshape.289, f32[1024,1024]{1,0:T(8,128)S(1)} %fusion.1, bf16[1024,2816]{1,0:T(8,128)(2,1)} %get-tuple-element.57, ...), kind=kOutput, calls=%fused_computation.38 | convolution fusion | flops 5912918016 | bytes 24131584 | tf_op jit(solution)/shard_map/dot_general | solution.py:419
  292.3 4.9 all-to-all-start.3
  303.2 10.8 %add_convert_fusion = bf16[1024,1024]{1,0:T(8,128)(2,1)} fusion(f32[1024,1024]{1,0:T(8,128)S(1)} %copy-done.3, bf16[1024,2816]{1,0:T(8,128)(2,1)} %get-tuple-element.55, bf16[2816,1024]{1,0:T(8,128)(2,1)} %all-gather.3.cloned.1.call-done), kind=kOutput, calls=%fused_computation.40 | convolution fusion | flops 5907677184 | bytes 17825792 | tf_op jit(solution)/shard_map/dot_general | solution.py:423
  314.1 74.9 %shard_map.214 = (bf16[2,2,512,512]{3,2,1,0:T(8,128)(2,1)}, bf16[2048,1024]{1,0:T(8,128)(2,1)}, bf16[2,512,1024]{2,1,0:T(8,128)(2,1)}, f32[32,1024]{1,0:T(8,128)}) custom-call(bf16[2,2,512,512]{3,2,1,0:T(8,128)(2,1)} %copy-done.20, bf16[2048,1024]{1,0:T(8,128)(2,1)} %convolution_convert_fusion.3.refs_1_, bf16[2,2,512,512]{3,2,1,0:T(8,128)(2,1)} %all-to-all-done.3.refs_2_, ...), custom_call_target="tpu_custom_call" | custom-call | flops 34359738368 | bytes 8388608 | tf_op jit(solution)/shard_map/pallas_call | solution.py:696
  393.5 3.6 all-to-all-start.5
  399.2 4.8 all-to-all-start.4
  412.2 4.0 fusion.20
  431.6 45.3 %shard_map.215 = (f32[32,1024]{1,0:T(8,128)S(1)}, f32[32,512]{1,0:T(8,128)S(1)}, f32[16,1024]{1,0:T(8,128)S(1)}, f32[16,128]{1,0:T(8,128)S(1)}, bf16[2,512,1024]{2,1,0:T(8,128)(2,1)S(1)}) custom-call(bf16[32,32,1024]{2,1,0:T(8,128)(2,1)} %pad_maximum_fusion.4.refs_0_, bf16[32,32,512]{2,1,0:T(8,128)(2,1)S(1)} %pad_maximum_fusion.6.refs_1_, ...), custom_call_target="tpu_custom_call" | custom-call | tf_op jit(solution)/shard_map/pallas_call | solution.py:331
  (187 shorter events, 105.5 us)
Async XLA Ops:
  7.2 151.0 %all-gather.3.cloned.1.call-start = ((), (), s32[]{:S(2)}) async-start(), calls=%async_computation.7 | async-start | bytes 5947392 | tf_op jit(solution)/shard_map/all_gather | solution.py:794
  7.9 174.5 %all-gather.5.cloned.1.call-start = ((), (), s32[]{:S(2)}) async-start(), calls=%async_computation.8 | async-start | bytes 11894784 | tf_op jit(solution)/shard_map/all_gather | solution.py:793
  58.2 6.0 %copy-start.26 = (bf16[32,32,512]{2,1,0:T(8,128)(2,1)S(1)}, bf16[32,32,512]{2,1,0:T(8,128)(2,1)}, u32[]{:S(2)}) copy-start(bf16[32,32,512]{2,1,0:T(8,128)(2,1)} %get-tuple-element.32) | copy-start | bytes 3145732
  59.3 5.6 %copy-start.38 = (f32[1024]{0:T(1024)}, f32[1024]{0:T(1024)S(1)}, u32[]{:S(2)}) copy-start(f32[1024]{0:T(1024)S(1)} %reshape.288) | copy-start | bytes 12292
  66.7 9.0 %all-to-all-start.1 = ((bf16[2,2,512,256]{3,2,1,0:T(8,128)(2,1)}), bf16[2,2,512,256]{3,2,1,0:T(8,128)(2,1)S(1)}, u32[]{:S(2)}, u32[]{:S(2)}) async-start(bf16[2,2,512,256]{3,2,1,0:T(8,128)(2,1)} %pad_maximum_fusion.5), calls=%async_computation.1 | async-start | bytes 2097152 | tf_op jit(solution)/shard_map/all_to_all | solution.py:754
  75.7 9.4 %all-to-all-start = ((bf16[2,2,512,512]{3,2,1,0:T(8,128)(2,1)}), bf16[2,2,512,512]{3,2,1,0:T(8,128)(2,1)S(1)}, u32[]{:S(2)}, u32[]{:S(2)}) async-start(bf16[2,2,512,512]{3,2,1,0:T(8,128)(2,1)} %pad_maximum_fusion.1), calls=%async_computation | async-start | bytes 4194304 | tf_op jit(solution)/shard_map/all_to_all | solution.py:754
  136.7 4.7 copy-start.43
  136.7 9.1 %all-to-all-start.2 = ((bf16[2,2,512,512]{3,2,1,0:T(8,128)(2,1)}), bf16[2,2,512,512]{3,2,1,0:T(8,128)(2,1)S(1)}, u32[]{:S(2)}, u32[]{:S(2)}) async-start(bf16[2,2,512,512]{3,2,1,0:T(8,128)(2,1)} %get-tuple-element.35.refs_3_), calls=%async_computation.2 | async-start | bytes 4194304 | tf_op jit(solution)/shard_map/all_to_all | solution.py:754
  140.5 337.0 %reduce-scatter.2.cloned.1.call-start = ((), (), s32[]{:S(2)}) async-start(), calls=%async_computation.9 | async-start | bytes 17842176 | tf_op jit(solution)/shard_map/reduce_scatter | solution.py:876
  150.9 5.5 %copy-start.1 = (f32[1024,1024]{1,0:T(8,128)}, f32[1024,1024]{1,0:T(8,128)S(1)}, u32[]{:S(2)}) copy-start(f32[1024,1024]{1,0:T(8,128)S(1)} %get-tuple-element.86) | copy-start | bytes 12582916
  215.7 10.0 %copy-start.23 = (bf16[1024,1024]{1,0:T(8,128)(2,1)S(1)}, bf16[1024,1024]{1,0:T(8,128)(2,1)}, u32[]{:S(2)}) copy-start(bf16[1024,1024]{1,0:T(8,128)(2,1)} %multiply_convert_fusion.3) | copy-start | bytes 6291460
  215.7 10.0 %copy-start.45 = (bf16[1024,2816]{1,0:T(8,128)(2,1)S(1)}, bf16[1024,2816]{1,0:T(8,128)(2,1)}, u32[]{:S(2)}) copy-start(bf16[1024,2816]{1,0:T(8,128)(2,1)} %get-tuple-element.56) | copy-start | bytes 17301508
  238.1 6.6 %slice-start = ((s8[5767168]{0:T(1024)(128)(4,1)}), s8[4194304]{0:T(1024)(128)(4,1)S(1)}, s32[]{:S(2)}) async-start(s8[5767168]{0:T(1024)(128)(4,1)} %bitcast.211), calls=%async_computation.10 | async-start | bytes 8388608
  239.8 4.9 slice-start.1
  262.2 10.7 %copy-start.2 = (f32[1024,1024]{1,0:T(8,128)S(1)}, f32[1024,1024]{1,0:T(8,128)}, u32[]{:S(2)}) copy-start(f32[1024,1024]{1,0:T(8,128)} %copy-done.1) | copy-start | bytes 12582916
  272.9 11.5 %copy-start.5 = (f32[2,512,1024]{2,1,0:T(8,128)S(1)}, f32[2,512,1024]{2,1,0:T(8,128)}, u32[]{:S(2)}) copy-start(f32[2,512,1024]{2,1,0:T(8,128)} %copy-done.4) | copy-start | bytes 12582916
  272.9 11.5 %copy-start.41 = (f32[1024]{0:T(1024)S(1)}, f32[1024]{0:T(1024)}, u32[]{:S(2)}) copy-start(f32[1024]{0:T(1024)} %get-tuple-element.83) | copy-start | bytes 12292
  290.7 6.4 %copy-start.11 = (bf16[1,2,512,512]{3,2,1,0:T(8,128)(2,1)S(1)}, bf16[1,2,512,512]{3,2,1,0:T(8,128)(2,1)}, u32[]{:S(2)}) copy-start(bf16[1,2,512,512]{3,2,1,0:T(8,128)(2,1)} %copy-done.10) | copy-start | bytes 3145732
  292.3 21.8 %all-to-all-start.3 = ((bf16[2,2,512,512]{3,2,1,0:T(8,128)(2,1)}), bf16[2,2,512,512]{3,2,1,0:T(8,128)(2,1)}, u32[]{:S(2)}, u32[]{:S(2)}) async-start(bf16[2,2,512,512]{3,2,1,0:T(8,128)(2,1)} %pad_maximum_fusion.2), calls=%async_computation.3 | async-start | bytes 4194304 | tf_op jit(solution)/shard_map/all_to_all | solution.py:754
  314.1 74.9 %copy-start.34 = (bf16[32,16,1024]{2,1,0:T(8,128)(2,1)S(1)}, bf16[32,16,1024]{2,1,0:T(8,128)(2,1)}, u32[]{:S(2)}) copy-start(bf16[32,16,1024]{2,1,0:T(8,128)(2,1)} %get-tuple-element.33) | copy-start | bytes 3145732
  393.5 5.7 %all-to-all-start.5 = ((bf16[2,2,512,256]{3,2,1,0:T(8,128)(2,1)}), bf16[2,2,512,256]{3,2,1,0:T(8,128)(2,1)S(1)}, u32[]{:S(2)}, u32[]{:S(2)}) async-start(bf16[2,2,512,256]{3,2,1,0:T(8,128)(2,1)} %bitcast.172), calls=%async_computation.5 | async-start | bytes 2097152 | tf_op jit(solution)/shard_map/all_to_all | solution.py:754
  399.2 7.8 %all-to-all-start.4 = ((bf16[2,2,512,512]{3,2,1,0:T(8,128)(2,1)}), bf16[2,2,512,512]{3,2,1,0:T(8,128)(2,1)}, u32[]{:S(2)}, u32[]{:S(2)}) async-start(bf16[2,2,512,512]{3,2,1,0:T(8,128)(2,1)} %get-tuple-element.39), calls=%async_computation.4 | async-start | bytes 4194304 | tf_op jit(solution)/shard_map/all_to_all | solution.py:754
  416.4 5.1 %copy-start.22 = (bf16[1024,1024]{1,0:T(8,128)(2,1)S(1)}, bf16[1024,1024]{1,0:T(8,128)(2,1)}, u32[]{:S(2)}) copy-start(bf16[1024,1024]{1,0:T(8,128)(2,1)} %copy.33) | copy-start | bytes 6291460
  480.6 4.6 copy-start.35
  (33 other events, 76.1 us)
Sparse Core Ops, SparseCore 0:
  10.8 73.3 all-gather.2
  87.7 94.6 all-gather.4
  255.7 216.4 reduce-scatter.1

commit v4 on v3

--- a/solution.py
+++ b/solution.py
@@ -8,6 +8,7 @@
 from jax.experimental.pallas import tpu as pltpu
 
 DH = 64
+EPSILON = 1e-05
 F32 = jnp.float32
 BF = jnp.bfloat16
 
@@ -421,6 +422,10 @@
 
 def dot_nn(a, b):
     return lax.dot_general(a, b, (((1,), (0,)), ((), ())), preferred_element_type=F32)
+
+
+def dot_tn(a, b):
+    return lax.dot_general(a, b, (((0,), (0,)), ((), ())), preferred_element_type=F32)
 
 
 def causal(s, first_key, first_query):
@@ -713,12 +718,368 @@
     )(q, kv, do, o, lse, blocks, *terms)
 
 
+CUT = 256
+PART = 512
+TALL = 512
+DOWN = 8
+
+
+class BlockSums:
+
+    def __init__(self, dp, stage, pair_buf, ring_buf, send, recv, out_ref):
+        self.place = Place(dp)
+        self.stage, self.pair_buf, self.ring_buf = stage, pair_buf, ring_buf
+        self.send, self.recv, self.out_ref = send, recv, out_ref
+        self.total = pair_buf.shape[1]
+        self.unit = out_ref.shape[0]
+
+    def order(self):
+        return [
+            self.place.index({"y": y, "x": x, "z": z}, other)
+            for other in (False, True)
+            for y in range(2)
+            for x in range(2)
+            for z in range(self.place.sizes["z"])
+        ]
+
+    def pair(self, j):
+        return remote(
+            self.stage.at[lax.rem(j, 2), pl.ds(self.total, self.total)],
+            self.pair_buf.at[j],
+            self.send.at[j, 0],
+            self.recv.at[j, 0],
+            self.place.pair(),
+        )
+
+    def hop(self, j, axis, step, first, size, number):
+        rows = pl.ds(first, size)
+        offset = {"x": 0, "y": 0, "z": 0, axis: step}
+        return remote(
+            self.pair_buf.at[j, rows],
+            self.ring_buf.at[j, rows],
+            self.send.at[j, number],
+            self.recv.at[j, number],
+            self.place.device(offset),
+        )
+
+    def hops(self, odd, phase):
+        q = self.total // 4
+        if phase == 3:
+            sizes = range(1, self.place.sizes["z"])
+            return [("z", z, z * self.unit, self.unit, 3 + z) for z in sizes]
+        if odd:
+            return ([("x", 1, q, q, 1), ("x", 1, 3 * q, q, 2)], [("y", 1, 2 * q, q, 3)])[phase - 1]
+        return ([("y", 1, 2 * q, 2 * q, 1)], [("x", 1, q, q, 3)])[phase - 1]
+
+    def add(self, j, to, size, came):
+        self.pair_buf[j, to : to + size] = (
+            self.pair_buf[j, to : to + size].astype(F32) + came.astype(F32)
+        ).astype(BF)
+
+    def advance(self, j, odd, phase):
+        q = self.total // 4
+        if phase == 1:
+            self.pair(j).wait_recv()
+            self.add(j, 0, self.total, self.stage[lax.rem(j, 2), : self.total])
+        else:
+            for hop in self.hops(odd, phase - 1):
+                self.hop(j, *hop).wait_recv()
+        if phase == 2 and odd:
+            self.add(j, 0, q, self.ring_buf[j, q : 2 * q])
+            self.add(j, 2 * q, q, self.ring_buf[j, 3 * q :])
+        elif phase == 2:
+            self.add(j, 0, 2 * q, self.ring_buf[j, 2 * q :])
+        elif phase == 3:
+            first = 2 * q if odd else q
+            self.add(j, 0, q, self.ring_buf[j, first : first + q])
+        elif phase == 4:
+            total = self.pair_buf[j, : self.unit].astype(F32)
+            for z in range(1, self.place.sizes["z"]):
+                total = total + self.ring_buf[j, z * self.unit : (z + 1) * self.unit].astype(F32)
+            wide = total.shape[1]
+            self.out_ref[:, pl.ds(pl.multiple_of(j * wide, wide), wide)] = total
+        if phase < 4:
+            for hop in self.hops(odd, phase):
+                self.hop(j, *hop).start()
+
+    def finish(self, blocks):
+        for j in range(blocks):
+            for phase in range(1, 4):
+                for hop in self.hops(j % 2, phase):
+                    self.hop(j, *hop).wait_send()
+
+
+def ffn_kernel(dp, scale_ref, x_ref, att_ref, wo_ref, gain_ref, cot_ref, gu_ref, down_ref,
+               res_ref, mid_ref, nb_ref, gu_out, down_out, *refs):
+    n2_s, n2t_s, up_s, acc_s, ht_s, back_s, gu_stage, down_stage, gu_sem, down_sem = refs[:10]
+    step = pl.program_id(0)
+    rows, width = x_ref.shape
+    part = min(PART, rows)
+    heads, _, cols = att_ref.shape
+    blocks = ht_s.shape[0] // CUT
+    wide = 2 * CUT
+    tall = ht_s.shape[0] // DOWN
+    chunks = [pl.ds(a, part) for a in range(0, rows, part)]
+    sums = BlockSums(dp, gu_stage, *refs[10:], gu_out) if dp else None
+
+    @pl.when(step == 0)
+    def _():
+        if dp:
+            sums.place.greet()
+        gain = gain_ref[...].astype(F32)
+        scale = scale_ref[0, 0]
+        for at in chunks:
+            mid = x_ref[at].astype(F32)
+            for j in range(heads):
+                mid = mid + dot_nn(att_ref[j, at], wo_ref[j * cols : (j + 1) * cols])
+            mid_ref[at] = mid
+            inverse = lax.rsqrt(jnp.mean(mid * mid, axis=-1, keepdims=True) + EPSILON)
+            low = (mid * inverse * gain).astype(BF)
+            n2_s[at] = low
+            if dp:
+                gu_stage[0, :, :part] = low.T
+                unit = gu_out.shape[0]
+                for i, shard in enumerate(sums.order()):
+                    there = pl.ds(pl.multiple_of(shard * unit, unit), unit)
+                    n2t_s[i * unit : (i + 1) * unit, at] = gu_stage[0, there, :part]
+            else:
+                n2t_s[:, at] = low.T
+            up_s[at] = (cot_ref[at].astype(F32) * scale).astype(BF)
+        acc_s[...] = jnp.zeros_like(acc_s)
+        nb_ref[...] = jnp.zeros_like(nb_ref)
+
+    def gu_copy(j):
+        slot = lax.rem(j, 2)
+        return pltpu.make_async_copy(
+            gu_stage.at[slot],
+            gu_out.at[:, pl.ds(pl.multiple_of(j * wide, wide), wide)],
+            gu_sem.at[slot],
+        )
+
+    def advance(phases):
+        for phase in phases:
+            j = step - phase
+            for odd in range(2):
+
+                @pl.when(
+                    jnp.logical_and(
+                        jnp.logical_and(step >= phase, step < phase + blocks), lax.rem(j, 2) == odd
+                    )
+                )
+                def _(j=j, odd=odd, phase=phase):
+                    sums.advance(j, odd, phase)
+
+    @pl.when(step < blocks)
+    def _():
+        for at in chunks:
+            both = dot_nn(n2_s[at], gu_ref[...])
+            gate, up = both[:, :CUT], both[:, CUT:]
+            back = dot_nt(up_s[at], down_ref[...])
+            sig = 0.5 * jnp.tanh(0.5 * gate) + 0.5
+            act = gate * sig
+            hidden = (act * up).astype(BF)
+            ht_s[pl.ds(pl.multiple_of(step * CUT, CUT), CUT), at] = hidden.T
+            back_s[at, :CUT] = (back * up * sig * (1.0 + gate * (1.0 - sig))).astype(BF)
+            back_s[at, CUT:] = (back * act).astype(BF)
+            acc_s[at] += dot_nn(hidden, down_ref[...])
+            nb_ref[at] += dot_nt(back_s[at], gu_ref[...])
+
+    if dp:
+        advance((4, 3, 2, 1))
+
+    @pl.when(jnp.logical_and(step >= 2, step < blocks))
+    def _():
+        if dp:
+            sums.pair(step - 2).wait_send()
+        else:
+            gu_copy(step - 2).wait()
+
+    @pl.when(step < blocks)
+    def _():
+        for a in range(0, width, TALL):
+            gu_stage[lax.rem(step, 2), a : a + TALL] = dot_nn(
+                n2t_s[a : a + TALL], back_s[...]
+            ).astype(BF)
+        if dp:
+            sums.pair(step).start()
+        else:
+            gu_copy(step).start()
+
+    def down_copy(p):
+        slot = lax.rem(p, 2)
+        there = down_out.at[pl.ds(pl.multiple_of(p * tall, tall), tall)]
+        return pltpu.make_async_copy(down_stage.at[slot], there, down_sem.at[slot])
+
+    @pl.when(step >= blocks)
+    def _():
+        p = step - blocks
+
+        @pl.when(p == 0)
+        def _():
+            for at in chunks:
+                res_ref[at] = (mid_ref[at] + acc_s[at]).astype(BF)
+
+        @pl.when(p >= 2)
+        def _():
+            down_copy(p - 2).wait()
+
+        grad = dot_nn(ht_s[pl.ds(pl.multiple_of(p * tall, tall), tall)], up_s[...])
+        down_stage[lax.rem(p, 2)] = grad.astype(BF)
+        down_copy(p).start()
+
+        @pl.when(p == DOWN - 1)
+        def _():
+            if dp:
+                sums.pair(blocks - 2).wait_send()
+                sums.pair(blocks - 1).wait_send()
+                sums.finish(blocks)
+            else:
+                gu_copy(blocks - 2).wait()
+                gu_copy(blocks - 1).wait()
+            down_copy(p - 1).wait()
+            down_copy(p).wait()
+
+
+def feed_forward(dp, scale, x, att, wo, gain, cot, gu, down):
+    rows, width = x.shape
+    size = down.shape[0]
+    blocks, tall = size // CUT, size // DOWN
+    once = pl.Buffered(1)
+
+    def whole(w):
+        return pl.BlockSpec(w.shape, lambda i: (0,) * len(w.shape), pipeline_mode=once)
+
+    def last(i):
+        return jnp.minimum(i, blocks - 1)
+
+    shape = jax.ShapeDtypeStruct
+    anywhere = pl.BlockSpec(memory_space=pl.ANY)
+    out = [shape((rows, width), BF), shape((rows, width), F32), shape((rows, width), F32)]
+    out_specs = [whole(w) for w in out]
+    scratch = []
+    params = {}
+    if dp:
+        out.append(shape((width // (4 * dp), 2 * size), F32))
+        out_specs.append(whole(out[-1]))
+        sem = pltpu.SemaphoreType.DMA((blocks, 3 + dp // 2))
+        scratch = [pltpu.VMEM((blocks, width // 2, 2 * CUT), BF)] * 2 + [sem] * 2
+        params = {"collective_id": 4, "has_side_effects": True}
+    else:
+        out.append(shape((width, 2 * size), BF))
+        out_specs.append(anywhere)
+    out.append(shape((size, width), BF))
+    out_specs.append(anywhere)
+    return pl.pallas_call(
+        functools.partial(ffn_kernel, dp),
+        grid=(blocks + DOWN,),
+        in_specs=[
+            pl.BlockSpec(memory_space=pltpu.SMEM),
+            whole(x),
+            whole(att),
+            whole(wo),
+            whole(gain),
+            whole(cot),
+            pl.BlockSpec((width, 2 * CUT), lambda i: (0, last(i))),
+            pl.BlockSpec((CUT, width), lambda i: (last(i), 0)),
+        ],
+        out_specs=out_specs,
+        out_shape=out,
+        scratch_shapes=[
+            pltpu.VMEM((rows, width), BF),
+            pltpu.VMEM((width, rows), BF),
+            pltpu.VMEM((rows, width), BF),
+            pltpu.VMEM((rows, width), F32),
+            pltpu.VMEM((size, rows), BF),
+            pltpu.VMEM((rows, 2 * CUT), BF),
+            pltpu.VMEM((2, width, 2 * CUT), BF),
+            pltpu.VMEM((2, tall, width), BF),
+            pltpu.SemaphoreType.DMA((2,)),
+            pltpu.SemaphoreType.DMA((2,)),
+            *scratch,
+        ],
+        compiler_params=pltpu.CompilerParams(vmem_limit_bytes=63 * 2**20, **params),
+        cost_estimate=cost(18 * rows * width * size),
+    )(scale, x, att, wo, gain, cot, gu, down)
+
+
+def branch_kernel(scale_ref, mid_ref, nb_ref, cot_ref, att_ref, wo_ref, gain_ref,
+                  mg_ref, send_ref, og_ref, gg_ref, branch_s):
+    step = pl.program_id(0)
+    part, width = mid_ref.shape
+    heads, rows, cols = att_ref.shape
+    mid, nback, gain = mid_ref[...], nb_ref[...], gain_ref[...].astype(F32)
+    inverse = lax.rsqrt(jnp.mean(mid * mid, axis=-1, keepdims=True) + EPSILON)
+    scaled = nback * gain
+    middle_grad = cot_ref[...].astype(F32) * scale_ref[0, 0] + (
+        inverse * scaled
+        - mid * (inverse * inverse * inverse) * jnp.mean(scaled * mid, axis=-1, keepdims=True)
+    )
+    gain_part = jnp.sum(nback * mid * inverse, axis=0, keepdims=True)
+    mg_ref[...] = middle_grad
+    branch = middle_grad.astype(BF)
+    branch_s[pl.ds(pl.multiple_of(step * part, part), part)] = branch
+    for j in range(heads):
+        send_ref[j] = dot_nt(branch, wo_ref[j * cols : (j + 1) * cols]).astype(BF)
+
+    @pl.when(step == 0)
+    def _():
+        gg_ref[...] = gain_part
+
+    @pl.when(step > 0)
+    def _():
+        gg_ref[...] += gain_part
+
+    @pl.when(step == rows // part - 1)
+    def _():
+        for j in range(heads):
+            og_ref[j * cols : (j + 1) * cols] = dot_tn(att_ref[j], branch_s[...]).astype(BF)
+
+
+def branch_back(scale, mid, nback, cot, att, wo, gain):
+    rows, width = mid.shape
+    heads, _, cols = att.shape
+    part = min(256, rows)
+    rowwise = pl.BlockSpec((part, width), lambda i: (i, 0))
+
+    def whole(w):
+        return pl.BlockSpec(w.shape, lambda i: (0,) * len(w.shape))
+
+    out = [
+        jax.ShapeDtypeStruct((rows, width), F32),
+        jax.ShapeDtypeStruct((heads, rows, cols), BF),
+        jax.ShapeDtypeStruct((width, width), BF),
+        jax.ShapeDtypeStruct((1, width), F32),
+    ]
+    return pl.pallas_call(
+        branch_kernel,
+        grid=(rows // part,),
+        in_specs=[
+            pl.BlockSpec(memory_space=pltpu.SMEM),
+            rowwise,
+            rowwise,
+            rowwise,
+            whole(att),
+            whole(wo),
+            whole(gain),
+        ],
+        out_specs=[
+            rowwise,
+            pl.BlockSpec((heads, part, cols), lambda i: (0, i, 0)),
+            whole(out[2]),
+            whole(out[3]),
+        ],
+        out_shape=out,
+        scratch_shapes=[pltpu.VMEM((rows, width), BF)],
+        compiler_params=pltpu.CompilerParams(vmem_limit_bytes=48 * 2**20),
+        cost_estimate=cost(4 * rows * width * width),
+    )(scale, mid, nback, cot, att, wo, gain)
+
+
 HEADS = 16
 KVH = 2
 LATD = 256
 HG = 8
 GROUPS = 8
-EPSILON = 1e-05
 ALL = ("dp", "seq", "grp")
 
 
@@ -734,10 +1095,6 @@
         scaled * values, axis=-1, keepdims=True
     )
     return (input_part, gain_grad)
-
-
-def dot_tn(a, b):
-    return lax.dot_general(a, b, (((0,), (0,)), ((), ())), preferred_element_type=F32)
 
 
 def swap_sequences(blocks, count):
@@ -787,19 +1144,18 @@
         shards = (w_query, w_latent, expand_rows, gains)
         full, own_inputs = own_gather(dp, shards, inputs, ("xzy",) * 4)
     else:
-        shards = (w_query, w_latent, expand_rows, gains, w_output)
+        shards = (w_query, w_latent, expand_rows, gains, w_output, w_down)
         full = [lax.all_gather(w, ALL, axis=0) for w in shards]
         own_inputs = swap_sequences(inputs, seqs)
-    ffn_full = lax.all_gather(jnp.concatenate([w_gate, w_up], axis=1), ALL, axis=0, tiled=True)
-    down_full = lax.all_gather(w_down, ALL, axis=0, tiled=True)
+    gate_up = jnp.stack(
+        [w_gate.reshape(drows, -1, CUT), w_up.reshape(drows, -1, CUT)], axis=2
+    ).reshape(drows, -1)
+    gu_full = lax.all_gather(gate_up, ALL, axis=0, tiled=True)
     query_full = full[0].reshape(width, -1)
     latent_full = full[1].reshape(width, -1)
     expand_full = full[2].reshape(devices, KVH, LATD // devices, -1)
     gain_one = full[3][:, 0, :drows].reshape(width).astype(F32)
-    gain_two = full[3][:, 0, drows : 2 * drows].reshape(width).astype(F32)
-    gate_full = ffn_full[:, :hidden_size]
-    up_full = ffn_full[:, hidden_size:]
-
+    gain_two = full[3][:, 0, drows : 2 * drows].reshape(1, width)
 
     token_rows = own_inputs.astype(F32).reshape(count, width)
     normed, inverse_one = norm_parts(token_rows, gain_one)
@@ -822,98 +1178,65 @@
     ).reshape(LATD, -1)
     head_pairs = dot_nn(head_latent, expand_local).astype(BF)
     if ring:
-        attended, logsum, own_cotangent, output_full = attention_forward_gather(
-            dp, head_queries, head_pairs, cotangent, (w_output,), ((0, 0, width),), ("xzy",)
+        half = width // 2
+        attended, logsum, own_cotangent, output_full, down_full = attention_forward_gather(
+            dp,
+            head_queries,
+            head_pairs,
+            cotangent,
+            (w_output, w_down),
+            ((0, 0, width), (1, 0, half), (1, half, half)),
+            ("xzy", "zyx", "zxy"),
         )
     else:
         attended, logsum = attention_forward(head_queries, head_pairs)
         own_cotangent = swap_sequences(cotangent, seqs)
-        output_full = full[4]
+        output_full, down_full = full[4:]
     output_full = output_full.reshape(-1, width)
+    down_full = down_full.reshape(-1, width)
     token_attended = swap_group(attended).reshape(groups, count, cols)
-    branch = sum(
-        dot_nn(token_attended[j], output_full[j * cols : (j + 1) * cols]) for j in range(groups)
-    )
-    middle = token_rows + branch
-    normed_two, inverse_two = norm_parts(middle, gain_two)
-    normed_two_low = normed_two.astype(BF)
-    gate_pre = dot_nn(normed_two_low, gate_full)
-    upward = dot_nn(normed_two_low, up_full)
-    sigmoid = jax.nn.sigmoid(gate_pre)
-    activated = gate_pre * sigmoid
-    hidden = (activated * upward).astype(BF)
-    result = middle + dot_nn(hidden, down_full)
-    own_output = result.astype(BF).reshape(seqs, rows, width)
-
     seq_group = lax.dynamic_index_in_dim(group_ids, lax.axis_index("seq"), 0, keepdims=False)
     chosen = (seq_group == jnp.arange(GROUPS)).astype(F32)
-    seq_scale = jnp.sum(chosen * group_scale)
-    upstream = own_cotangent.astype(F32).reshape(count, width) * seq_scale
-    upstream_low = upstream.astype(BF)
-    down_grad = dot_tn(hidden, upstream_low)
-    hidden_back = dot_nt(upstream_low, down_full)
-    gate_back = (hidden_back * upward * sigmoid * (1.0 + gate_pre * (1.0 - sigmoid))).astype(BF)
-    up_back = (hidden_back * activated).astype(BF)
-    gate_grad = dot_tn(normed_two_low, gate_back)
-    up_grad = dot_tn(normed_two_low, up_back)
-    normed_two_back = dot_nt(gate_back, gate_full) + dot_nt(up_back, up_full)
-    middle_part, gain_two_grad = norm_back(middle, inverse_two, gain_two, normed_two_back)
-    middle_grad = upstream + middle_part
-    if ring:
-        both = jnp.concatenate([gate_grad.astype(BF), up_grad.astype(BF)], axis=1).reshape(
-            devices, drows, -1
-        )
-        whole = both.shape[2] // width * width
-        half = drows // 2
-        packed = jnp.concatenate(
-            [both[:, :, a : a + width] for a in range(0, whole, width)]
-            + [
-                jnp.concatenate([both[:, :half, whole:], both[:, half:, whole:]], axis=2),
-                down_grad.astype(BF).reshape(devices, -1, width),
-            ],
-            axis=1,
-        )
-        share = lax.psum_scatter(packed, ALL, scatter_dimension=0, tiled=True)[0].astype(F32)
-        tall = whole // width * drows
-        tail = share[tall : tall + half]
-        ffn_share = jnp.concatenate(
-            [share[a : a + drows] for a in range(0, tall, drows)]
-            + [jnp.concatenate([tail[:, : width // 2], tail[:, width // 2 :]], axis=0)],
-            axis=1,
-        )
-        down_share = share[tall + half :]
-    else:
-        ffn_share = lax.psum_scatter(
-            jnp.concatenate([gate_grad.astype(BF), up_grad.astype(BF)], axis=1),
-            ALL,
-            scatter_dimension=0,
-            tiled=True,
-        ).astype(F32)
-        down_share = lax.psum_scatter(
-            down_grad.astype(BF), ALL, scatter_dimension=0, tiled=True
-        ).astype(F32)
-
-    branch_low = middle_grad.astype(BF)
-    output_grad = jnp.concatenate(
-        [dot_tn(token_attended[j], branch_low) for j in range(groups)], axis=0
+    seq_scale = jnp.sum(chosen * group_scale).reshape(1, 1)
+    x_rows = own_inputs.reshape(count, width)
+    cot_rows = own_cotangent.reshape(count, width)
+    result, middle, normed_two_back, gu_share, down_grad = feed_forward(
+        dp if ring else None,
+        seq_scale,
+        x_rows,
+        token_attended,
+        output_full,
+        gain_two,
+        cot_rows,
+        gu_full,
+        down_full,
     )
-    back_send = jnp.stack(
-        [
-            dot_nt(branch_low, output_full[j * cols : (j + 1) * cols]).astype(BF)
-            for j in range(groups)
-        ]
-    ).reshape(groups, seqs, rows, cols)
-    head_upstream = swap_group(back_send)
-    terms = output_grad.astype(BF).reshape(devices, drows, width)
+    own_output = result.reshape(seqs, rows, width)
+    if not ring:
+        gu_share = lax.psum_scatter(gu_share, ALL, scatter_dimension=0, tiled=True).astype(F32)
+    gu_share = gu_share.reshape(drows, -1, 2, CUT)
+    middle_grad, back_send, output_grad, gain_two_grad = branch_back(
+        seq_scale, middle, normed_two_back, cot_rows, token_attended, output_full, gain_two
+    )
+    head_upstream = swap_group(back_send.reshape(groups, seqs, rows, cols))
+    terms = (output_grad.reshape(devices, drows, width), down_grad.reshape(devices, -1, width))
     attention = (head_queries, head_pairs, head_upstream, attended, logsum)
     if ring:
-        query_back, pair_back, output, output_share = attention_backward_scatter(
-            dp, *attention, own_output, (terms,), ((0, 0, width),), ("yzx",)
+        half = width // 2
+        query_back, pair_back, output, output_share, down_share = attention_backward_scatter(
+            dp,
+            *attention,
+            own_output,
+            terms,
+            ((0, 0, width), (1, 0, half), (1, half, half)),
+            ("yzx", "yxz", "xyz"),
         )
     else:
         query_back, pair_back = attention_backward(*attention)
         output = swap_sequences(own_output, seqs)
-        output_share = lax.psum_scatter(terms, ALL, scatter_dimension=0, tiled=True)[0].astype(F32)
+        output_share, down_share = [
+            lax.psum_scatter(w, ALL, scatter_dimension=0, tiled=True)[0].astype(F32) for w in terms
+        ]
     latent_terms = dot_nt(pair_back, expand_local).astype(BF)
     expand_part = dot_tn(head_latent, pair_back)
     expand_grad = lax.dynamic_update_slice(
@@ -961,8 +1284,8 @@
         sums[2].reshape(expansion_weight.shape),
         output_share,
         sums[3][0, drows : 2 * drows],
-        ffn_share[:, :hidden_size],
-        ffn_share[:, hidden_size:],
+        gu_share[:, :, 0].reshape(drows, -1),
+        gu_share[:, :, 1].reshape(drows, -1),
         down_share,
     )
 

time: 499 us -> 517 us (1.036)
  Pallas kernels: 217 us -> 393 us
  matrix products: 140 us -> 27.1 us
  other arithmetic: 36.9 us -> 13.8 us
  waiting for transfers between devices: 17.2 us -> 0.03 us
  blocking collectives: 0 us -> 16.4 us
  starting transfers between devices: 25 us -> 14 us
  local copies, waits for them, and re-layouts: 41.6 us -> 31.2 us
    pallas_call x0 -> x2, Pallas kernels: none -> 139 us  [the longest x1 126 us: feed_forward(): pl.pallas_call(functools.partial(ffn_kernel, dp), grid=(blocks + DOWN,),...]
    dot_general x10 -> x5, matrix products: 56.4 us -> 9.22 us  [dot_nn(): lax.dot_general(a, b, (((1,), (0,)), ((), ())), preferred_element_type=F32)]
    dot_general x10 -> x5, matrix products: 46.8 us -> 10.3 us  [dot_nt(): lax.dot_general(a, b, (((1,), (1,)), ((), ())), preferred_element_type=F32)]
    pallas_call x1, Pallas kernels: 50.3 us -> 80.3 us  [attention_forward_gather(): pl.pallas_call(functools.partial(forward_gather_kernel, dp, cuts, orders,...]
    dot_general x10 -> x5, matrix products: 36.5 us -> 7.55 us  [dot_tn(): lax.dot_general(a, b, (((0,), (0,)), ((), ())), preferred_element_type=F32)]
    all_to_all x0 -> x3, blocking collectives: none -> 16.4 us  [swap_group(): return lax.all_to_all(blocks, 'grp', 0, 0, tiled=True)]
    pallas_call x1, Pallas kernels: 74.9 us -> 87.8 us  [attention_backward_scatter(): pl.pallas_call(functools.partial(backward_scatter_kernel, dp, blk, cuts,...]
    all_gather x2 -> x1, waiting for transfers between devices: 12.5 us -> 0.01 us  [local(): gu_full = lax.all_gather(gate_up, ALL, axis=0, tiled=True)]
  transfers between devices with their start and end apart: 9 -> 4, of which waited for: 3 -> 0; matrix products, arithmetic and copies ran while one was open for 26% -> 5% of each run, Pallas kernels for 44% -> 26%
where the time goes in v4:
time: 517 us; the launch traced here: 510 us
  Pallas kernels  393 us (76%)
  local copies, waits for them, and re-layouts  31.2 us (6%)
  matrix products  27.1 us (5%)
  blocking collectives  16.4 us (3%)
  between operations  15 us (3%)
  starting transfers between devices  14 us (3%)
  other arithmetic  13.8 us (3%)
    pallas_call x1, Pallas kernels, feed_forward(): pl.pallas_call(functools.partial(ffn_kernel, dp), grid=(blocks + DOWN,),...  126 us
    pallas_call x1, Pallas kernels, attention_backward_scatter(): pl.pallas_call(functools.partial(backward_scatter_kernel, dp, blk, cuts,...  87.8 us
    pallas_call x1, Pallas kernels, attention_forward_gather(): pl.pallas_call(functools.partial(forward_gather_kernel, dp, cuts, orders,...  80.3 us
    pallas_call x1, Pallas kernels, own_gather(): pl.pallas_call(functools.partial(gather_kernel, dp, orders), in_specs=[an...  50.5 us
    pallas_call x1, Pallas kernels, own_scatter(): pl.pallas_call(functools.partial(scatter_kernel, dp, orders, late), in_sp...  35.2 us
    all_to_all x3, blocking collectives, swap_group(): return lax.all_to_all(blocks, 'grp', 0, 0, tiled=True)  16.4 us
    unnamed x76, local copies, waits for them, and re-layouts  16.1 us
    all_to_all x3, starting transfers between devices, swap_group(): return lax.all_to_all(blocks, 'grp', 0, 0, tiled=True)  13.9 us
  transfers between devices with their start and end apart: 4, of which 0 were waited for; matrix products, arithmetic and copies ran while one was open for 5% of the time, Pallas kernels for 26%

profile of v4, /device:TPU:0, one launch (start us, length us, event | category | flops | bytes accessed | tf_op | source)
XLA Modules:
  0.0 510.1 jit_solution(5053303786832589828)
XLA Ops:
  11.5 50.5 %shard_map.212 = (bf16[32,32,1024]{2,1,0:T(8,128)(2,1)}, bf16[32,32,512]{2,1,0:T(8,128)(2,1)}, bf16[32,16,1024]{2,1,0:T(8,128)(2,1)}, bf16[32,16,128]{2,1,0:T(8,128)(2,1)}, bf16[2,512,1024]{2,1,0:T(8,128)(2,1)}) custom-call(bf16[32,1024]{1,0:T(8,128)(2,1)} %refs_0_.1, bf16[32,512]{1,0:T(8,128)(2,1)} %refs_1_.1, bf16[16,1024]{1,0:T(8,128)(2,1)} %bitcast.157, ...), custom_call_target="tpu_custom_call" | custom-call | tf_op jit(solution)/shard_map/pallas_call | solution.py:281
  62.1 2.2 fusion
  69.0 3.6 all-to-all-start.1
  72.6 3.3 convolution_convert_fusion.5
  79.1 5.0 all-to-all-start
  85.7 3.3 convolution_convert_fusion.refs_1_
  89.0 80.3 %shard_map.213 = (bf16[2,2,512,512]{3,2,1,0:T(8,128)(2,1)}, f32[4,2,2048]{2,1,0:T(2,128)}, bf16[2,512,1024]{2,1,0:T(8,128)(2,1)}, bf16[32,32,1024]{2,1,0:T(8,128)(2,1)}, bf16[32,88,1024]{2,1,0:T(8,128)(2,1)}) custom-call(bf16[2,2,512,512]{3,2,1,0:T(8,128)(2,1)} %all-to-all-done.refs_0_, bf16[2048,1024]{1,0:T(8,128)(2,1)} %convolution_convert_fusion.refs_1_, ...), custom_call_target="tpu_custom_call" | custom-call | flops 17179869184 | bytes 8388608 | tf_op jit(solution)/shard_map/pallas_call | solution.py:542
  169.3 5.3 %all-to-all-start.2 = ((bf16[2,2,512,512]{3,2,1,0:T(8,128)(2,1)}), bf16[2,2,512,512]{3,2,1,0:T(8,128)(2,1)}, u32[]{:S(2)}, u32[]{:S(2)}) async-start(bf16[2,2,512,512]{3,2,1,0:T(8,128)(2,1)} %get-tuple-element.45.refs_3_), calls=%async_computation.2 | async-start | bytes 4194304 | tf_op jit(solution)/shard_map/all_to_all | solution.py:1111
  176.3 1.9 fusion.2
  178.2 4.0 copy.37
  184.0 125.7 %shard_map.214 = (bf16[1024,1024]{1,0:T(8,128)(2,1)}, f32[1024,1024]{1,0:T(8,128)}, f32[1024,1024]{1,0:T(8,128)}, f32[32,5632]{1,0:T(8,128)}, bf16[2816,1024]{1,0:T(8,128)(2,1)}) custom-call(f32[1,1]{1,0:T(1,128)} %bitcast.14.scale_ref, bf16[1024,1024]{1,0:T(8,128)(2,1)} %bitcast.116, bf16[2,1024,512]{2,1,0:T(8,128)(2,1)} %bitcast.16.att_ref, ...), custom_call_target="tpu_custom_call" | custom-call | flops 53150220288 | bytes 8388608 | tf_op jit(solution)/shard_map/pallas_call | solution.py:972
  309.7 13.0 %shard_map.215 = (f32[1024,1024]{1,0:T(8,128)}, bf16[2,1024,512]{2,1,0:T(8,128)(2,1)S(1)}, bf16[1024,1024]{1,0:T(8,128)(2,1)S(1)}, f32[1,1024]{1,0:T(1,128)S(1)}) custom-call(f32[1,1]{1,0:T(1,128)} %bitcast.14.scale_ref, f32[1024,1024]{1,0:T(8,128)} %get-tuple-element.49.mid_ref, f32[1024,1024]{1,0:T(8,128)} %get-tuple-element.50.nb_ref, ...), custom_call_target="tpu_custom_call" | custom-call | flops 4294967296 | bytes 8388608 | tf_op jit(solution)/shard_map/pallas_call | solution.py:1053
  322.7 6.3 %all_to_all.30.refs_2_ = bf16[2,2,512,512]{3,2,1,0:T(8,128)(2,1)} all-to-all(bf16[2,2,512,512]{3,2,1,0:T(8,128)(2,1)S(1)} %bitcast.113), channel_id=1, replica_groups=mesh['dp'=8,'seq'=2,'grp'=2] {'grp'}, dimensions={0} | all-to-all | bytes 4194304 | tf_op jit(solution)/shard_map/all_to_all | solution.py:1111
  329.0 87.8 %shard_map.216 = (bf16[2,2,512,512]{3,2,1,0:T(8,128)(2,1)}, bf16[2048,1024]{1,0:T(8,128)(2,1)}, bf16[2,512,1024]{2,1,0:T(8,128)(2,1)}, f32[32,1024]{1,0:T(8,128)}, f32[88,1024]{1,0:T(8,128)}) custom-call(bf16[2,2,512,512]{3,2,1,0:T(8,128)(2,1)} %all-to-all-done.refs_0_, bf16[2048,1024]{1,0:T(8,128)(2,1)} %convolution_convert_fusion.refs_1_, ...), custom_call_target="tpu_custom_call" | custom-call | flops 34359738368 | bytes 8388608 | tf_op jit(solution)/shard_map/pallas_call | solution.py:701
  416.9 3.5 convolution_convert_fusion.1
  420.4 4.7 all_to_all.31
  427.8 5.4 %all_to_all.32 = bf16[2,2,512,512]{3,2,1,0:T(8,128)(2,1)S(1)} all-to-all(bf16[2,2,512,512]{3,2,1,0:T(8,128)(2,1)S(1)} %copy-done.14), channel_id=1, replica_groups=mesh['dp'=8,'seq'=2,'grp'=2] {'grp'}, dimensions={0} | all-to-all | bytes 4194304 | tf_op jit(solution)/shard_map/all_to_all | solution.py:1111
  433.4 2.2 copy-done.24
  437.2 4.1 fusion.11
  441.6 3.6 fusion.13
  450.0 1.6 pad_maximum_fusion.1.refs_0_
  453.1 2.5 fusion.10
  455.6 35.2 %shard_map.217 = (f32[32,1024]{1,0:T(8,128)S(1)}, f32[32,512]{1,0:T(8,128)S(1)}, f32[16,1024]{1,0:T(8,128)S(1)}, f32[16,128]{1,0:T(8,128)S(1)}, bf16[2,512,1024]{2,1,0:T(8,128)(2,1)S(1)}) custom-call(bf16[32,32,1024]{2,1,0:T(8,128)(2,1)} %pad_maximum_fusion.1.refs_0_, bf16[32,32,512]{2,1,0:T(8,128)(2,1)S(1)} %pad_maximum_fusion.3.refs_1_, ...), custom_call_target="tpu_custom_call" | custom-call | tf_op jit(solution)/shard_map/pallas_call | solution.py:332
  493.0 2.0 slice_reduce_fusion
  (121 shorter events, 38.1 us)
Async XLA Ops:
  7.2 3.6 copy-start.30
  7.2 3.6 copy-start.29
  7.2 176.8 %all-gather.2.cloned.1.call-start = ((), (), s32[]{:S(2)}) async-start(), calls=%async_computation.6 | async-start | bytes 11894784 | tf_op jit(solution)/shard_map/all_gather | solution.py:1153
  62.0 3.2 copy-start.2
  69.0 10.1 %all-to-all-start.1 = ((bf16[2,2,512,256]{3,2,1,0:T(8,128)(2,1)}), bf16[2,2,512,256]{3,2,1,0:T(8,128)(2,1)S(1)}, u32[]{:S(2)}, u32[]{:S(2)}) async-start(bf16[2,2,512,256]{3,2,1,0:T(8,128)(2,1)} %pad_maximum_fusion.2), calls=%async_computation.1 | async-start | bytes 2097152 | tf_op jit(solution)/shard_map/all_to_all | solution.py:1111
  72.6 3.3 copy-start.13
  72.6 3.7 copy-start.23
  79.1 10.0 %all-to-all-start = ((bf16[2,2,512,512]{3,2,1,0:T(8,128)(2,1)}), bf16[2,2,512,512]{3,2,1,0:T(8,128)(2,1)}, u32[]{:S(2)}, u32[]{:S(2)}) async-start(bf16[2,2,512,512]{3,2,1,0:T(8,128)(2,1)} %pad_maximum_fusion), calls=%async_computation | async-start | bytes 4194304 | tf_op jit(solution)/shard_map/all_to_all | solution.py:1111
  169.3 14.6 %all-to-all-start.2 = ((bf16[2,2,512,512]{3,2,1,0:T(8,128)(2,1)}), bf16[2,2,512,512]{3,2,1,0:T(8,128)(2,1)}, u32[]{:S(2)}, u32[]{:S(2)}) async-start(bf16[2,2,512,512]{3,2,1,0:T(8,128)(2,1)} %get-tuple-element.45.refs_3_), calls=%async_computation.2 | async-start | bytes 4194304 | tf_op jit(solution)/shard_map/all_to_all | solution.py:1111
  178.2 4.0 copy-start.31
  178.2 4.5 copy-start.32
  184.0 125.7 %copy-start = (bf16[1,1024]{1,0:T(2,128)(2,1)S(1)}, bf16[1,1024]{1,0:T(2,128)(2,1)}, u32[]{:S(2)}) copy-start(bf16[1,1024]{1,0:T(2,128)(2,1)} %reshape_squeeze.10.gain_ref) | copy-start | bytes 6148
  322.7 6.3 %copy-start.1 = (bf16[1024,1024]{1,0:T(8,128)(2,1)}, bf16[1024,1024]{1,0:T(8,128)(2,1)S(1)}, u32[]{:S(2)}) copy-start(bf16[1024,1024]{1,0:T(8,128)(2,1)S(1)} %get-tuple-element.54) | copy-start | bytes 6291460
  329.0 87.8 %copy-start.27 = (bf16[32,16,1024]{2,1,0:T(8,128)(2,1)S(1)}, bf16[32,16,1024]{2,1,0:T(8,128)(2,1)}, u32[]{:S(2)}) copy-start(bf16[32,16,1024]{2,1,0:T(8,128)(2,1)} %get-tuple-element.44) | copy-start | bytes 3145732
  420.4 4.8 copy-start.20
  433.4 3.5 copy-start.21
  433.4 3.5 copy-start.8
  437.2 4.4 copy-start.6
  441.6 3.7 copy-start.11
  441.6 3.7 copy-start.18
  450.0 3.1 copy-start.4
  493.0 3.9 copy-start.10
  498.2 3.2 copy-start.28
  498.2 3.9 copy-start.25
  (13 other events, 19.2 us)
Sparse Core Ops, SparseCore 0:
  11.5 118.4 all-gather.1

commit v5 on v4

--- a/solution.py
+++ b/solution.py
@@ -8,6 +8,7 @@
 from jax.experimental.pallas import tpu as pltpu
 
 DH = 64
+KVH = 2
 EPSILON = 1e-05
 F32 = jnp.float32
 BF = jnp.bfloat16
@@ -290,59 +291,8 @@
     return out[:-1], out[-1]
 
 
-def scatter_kernel(dp, orders, late, *refs):
-    count = len(orders)
-    terms, x_in = refs[:count], refs[count]
-    outs, x_out = refs[count + 1 : 2 * count + 1], refs[2 * count + 1]
-    rest = refs[2 * count + 2 :]
-    pair_bufs, ring_bufs = rest[:count], rest[count : 2 * count]
-    sems, x_sem = rest[2 * count : -1], rest[-1]
-    place = Place(dp)
-    place.greet()
-    works = [
-        Scatter(
-            place, dp, orders[a], lambda at, a=a: terms[a].at[at], pair_bufs[a], ring_bufs[a], sems, a
-        )
-        for a in range(count)
-    ]
-    swap, kept = block_swap(x_in, x_out, x_sem, place)
-    for work in works:
-        work.start()
-    turns = [work.turn() for work in works]
-    for i in range(len(turns[0])):
-        if i == late:
-            swap.start()
-            kept.start()
-        for a in range(count):
-            works[a].add(turns[a][i], outs[a] if i == len(turns[0]) - 1 else None)
-    for work in works:
-        work.finish()
-    swap.wait()
-    kept.wait()
-
-
 def scatter_sems(dp, count):
     return [pltpu.SemaphoreType.DMA((count, 2 * dp))] * 4
-
-
-def own_scatter(dp, terms, orders, blocks, late=0):
-    count = len(terms)
-    anywhere = pl.BlockSpec(memory_space=pl.ANY)
-    inside = pl.BlockSpec(memory_space=pltpu.VMEM)
-    out = pl.pallas_call(
-        functools.partial(scatter_kernel, dp, orders, late),
-        in_specs=[inside] * count + [anywhere],
-        out_specs=[inside] * count + [anywhere],
-        out_shape=[jax.ShapeDtypeStruct(w.shape[1:], F32) for w in terms]
-        + [jax.ShapeDtypeStruct(blocks.shape, blocks.dtype)],
-        scratch_shapes=[pltpu.VMEM((2 * dp, *w.shape[1:]), BF) for w in terms] * 2
-        + scatter_sems(dp, count)
-        + [pltpu.SemaphoreType.DMA((3,))],
-        compiler_params=pltpu.CompilerParams(
-            collective_id=1, has_side_effects=True, vmem_limit_bytes=48 * 2**20
-        ),
-    )(*terms, blocks)
-    return out[:-1], out[-1]
 
 
 def run_at(plan, point):
@@ -722,6 +672,7 @@
 PART = 512
 TALL = 512
 DOWN = 8
+LAGS = (1, 3, 5, 7)
 
 
 class BlockSums:
@@ -744,7 +695,7 @@
 
     def pair(self, j):
         return remote(
-            self.stage.at[lax.rem(j, 2), pl.ds(self.total, self.total)],
+            self.stage.at[lax.rem(j, self.stage.shape[0]), pl.ds(self.total, self.total)],
             self.pair_buf.at[j],
             self.send.at[j, 0],
             self.recv.at[j, 0],
@@ -780,7 +731,7 @@
         q = self.total // 4
         if phase == 1:
             self.pair(j).wait_recv()
-            self.add(j, 0, self.total, self.stage[lax.rem(j, 2), : self.total])
+            self.add(j, 0, self.total, self.stage[lax.rem(j, self.stage.shape[0]), : self.total])
         else:
             for hop in self.hops(odd, phase - 1):
                 self.hop(j, *hop).wait_recv()
@@ -802,10 +753,10 @@
             for hop in self.hops(odd, phase):
                 self.hop(j, *hop).start()
 
-    def finish(self, blocks):
-        for j in range(blocks):
+    def finish(self, parities):
+        for j, odd in enumerate(parities):
             for phase in range(1, 4):
-                for hop in self.hops(j % 2, phase):
+                for hop in self.hops(odd, phase):
                     self.hop(j, *hop).wait_send()
 
 
@@ -858,12 +809,13 @@
 
     def advance(phases):
         for phase in phases:
-            j = step - phase
+            lag = LAGS[phase - 1]
+            j = step - lag
             for odd in range(2):
 
                 @pl.when(
                     jnp.logical_and(
-                        jnp.logical_and(step >= phase, step < phase + blocks), lax.rem(j, 2) == odd
+                        jnp.logical_and(step >= lag, step < lag + blocks), lax.rem(j, 2) == odd
                     )
                 )
                 def _(j=j, odd=odd, phase=phase):
@@ -932,7 +884,7 @@
             if dp:
                 sums.pair(blocks - 2).wait_send()
                 sums.pair(blocks - 1).wait_send()
-                sums.finish(blocks)
+                sums.finish([j % 2 for j in range(blocks)])
             else:
                 gu_copy(blocks - 2).wait()
                 gu_copy(blocks - 1).wait()
@@ -1075,8 +1027,185 @@
     )(scale, mid, nback, cot, att, wo, gain)
 
 
+def closing_kernel(dp, *refs):
+    dq_in, dkv_in, hl_in, ex_in, x_in, gain_ref, wq_in, wl_in, mg_in, gg_ref = refs[:10]
+    ig_out, q_out, e_out, g_out = refs[10:14]
+    dq, dkv, hl, ex, x, wq, wl, mg = refs[14:22]
+    far_dq, far_lat, lat_send, lat_own, e_s, g_s, n1t, flip, ig = refs[22:31]
+    q_stage, q_pair, q_ring, e_stage, e_pair, e_ring, g_stage, g_pair, g_ring = refs[31:40]
+    load_sem, far_send, far_recv, x_sem = refs[40:44]
+    q_send, q_recv, e_send, e_recv, g_send, g_recv = refs[44:]
+    place = Place(dp)
+    c, s = place.core, place.at["x"]
+    rows, width = x.shape
+    cols, lat = dq.shape[1], ex.shape[0]
+    part = rows // 2
+    unit = q_out.shape[0]
+
+    def at(index, size):
+        return pl.ds(pl.multiple_of(index * size, size), size)
+
+    loads = [(ex_in, ex), (dkv_in, dkv), (hl_in, hl), (x_in, x), (dq_in.at[c], dq)]
+    loads += [(wq_in, wq), (wl_in, wl), (mg_in, mg)]
+
+    def load(i):
+        return pltpu.make_async_copy(*loads[i], load_sem.at[i])
+
+    for i in range(len(loads)):
+        load(i).start()
+    place.greet()
+    far_q = remote(dq_in.at[1 - c], far_dq, far_send.at[0], far_recv.at[0], place.pair())
+    far_l = remote(lat_send, far_lat, far_send.at[1], far_recv.at[1], place.pair())
+    far_q.start()
+
+    q_sums = BlockSums(dp, q_stage, q_pair, q_ring, q_send, q_recv, q_out)
+    e_sums = BlockSums(dp, e_stage, e_pair, e_ring, e_send, e_recv, e_out)
+    g_sums = BlockSums(dp, g_stage, g_pair, g_ring, g_send, g_recv, g_out)
+    order = q_sums.order()
+
+    load(0).wait()
+    load(1).wait()
+    for u in range(2):
+        lat_send[u * part : (u + 1) * part] = dot_nt(dkv[at(u * 2 + 1 - c, part)], ex[...]).astype(BF)
+    far_l.start()
+    for u in range(2):
+        lat_own[u * part : (u + 1) * part] = dot_nt(dkv[at(u * 2 + c, part)], ex[...]).astype(BF)
+    load(3).wait()
+    gain = gain_ref[...].astype(F32)
+
+    def inverse_of(values):
+        return lax.rsqrt(jnp.mean(values * values, axis=-1, keepdims=True) + EPSILON)
+
+    for u in range(2):
+        chunk = slice(u * part, (u + 1) * part)
+        values = x[chunk].astype(F32)
+        flip[...] = (values * inverse_of(values) * gain).astype(BF).T
+        for i, shard in enumerate(order):
+            n1t[i * unit : (i + 1) * unit, chunk] = flip[at(shard, unit)]
+    for i in (4, 5, 6, 7):
+        load(i).wait()
+    far_q.wait_recv()
+    far_l.wait_recv()
+
+    def back(u):
+        chunk = at(u, part)
+        normed_back = (
+            dot_nt(dq[chunk], wq[:, at(c, cols)])
+            + dot_nt(far_dq[chunk], wq[:, at(1 - c, cols)])
+            + dot_nt(lat_own[chunk], wl[:, at(c, lat)])
+            + dot_nt(far_lat[chunk], wl[:, at(1 - c, lat)])
+        )
+        values = x[chunk].astype(F32)
+        inverse = inverse_of(values)
+        scaled = normed_back * gain
+        grad = mg[chunk] + (
+            inverse * scaled
+            - values
+            * (inverse * inverse * inverse)
+            * jnp.mean(scaled * values, axis=-1, keepdims=True)
+        )
+        ig[u] = grad.astype(BF)
+        return jnp.sum(normed_back * values * inverse, axis=0, keepdims=True)
+
+    gain_part = back(1 - s)
+    swap, kept = block_swap(ig, ig_out, x_sem, place)
+    swap.start()
+    q_stage[c] = dot_nn(n1t[...], dq[...]).astype(BF)
+    q_stage[1 - c] = dot_nn(n1t[...], far_dq[...]).astype(BF)
+    for j in range(2):
+        q_sums.pair(j).start()
+    q_stage[2, :, at(c, lat)] = dot_nn(n1t[...], lat_own[...]).astype(BF)
+    q_stage[2, :, at(1 - c, lat)] = dot_nn(n1t[...], far_lat[...]).astype(BF)
+    q_sums.pair(2).start()
+    load(2).wait()
+    e_s[...] = dot_tn(hl[...], dkv[...])
+    share = e_out.shape[0] // KVH
+    for i, shard in enumerate(order):
+        piece = e_s[at(shard, share)]
+        zero = jnp.zeros_like(piece)
+        whole = jnp.concatenate(
+            [jnp.where(c == 0, piece, zero), jnp.where(c == 0, zero, piece)], axis=0
+        ).astype(BF)
+        for j in range(2):
+            e_stage[j, i * 2 * share : (i + 1) * 2 * share] = whole[:, j * cols : (j + 1) * cols]
+    for j in range(2):
+        e_sums.pair(j).start()
+    for j in range(3):
+        q_sums.advance(j, j % 2, 1)
+    gain_part = gain_part + back(s)
+    kept.start()
+    g_s[...] = jnp.concatenate(
+        [gain_part, gg_ref[...], jnp.zeros((14, width), F32)], axis=0
+    ).astype(BF)
+    for i, shard in enumerate(order):
+        g_stage[0, i * 16 : (i + 1) * 16] = g_s[:, at(lax.div(shard * unit, 128), 128)]
+    g_sums.pair(0).start()
+    for j in range(2):
+        e_sums.advance(j, 1 - j, 1)
+    g_sums.advance(0, 1, 1)
+    for phase in (2, 3, 4):
+        for j in range(3):
+            q_sums.advance(j, j % 2, phase)
+        for j in range(2):
+            e_sums.advance(j, 1 - j, phase)
+        g_sums.advance(0, 1, phase)
+    far_q.wait_send()
+    far_l.wait_send()
+    for sums, parities in ((q_sums, (0, 1, 0)), (e_sums, (1, 0)), (g_sums, (1,))):
+        for j in range(len(parities)):
+            sums.pair(j).wait_send()
+        sums.finish(parities)
+    swap.wait()
+    kept.wait()
+
+
+def closing(dp, dq, dkv, head_latent, expand, x, gain, wq, wl, mg, gain_two_grad):
+    rows, width = x.shape
+    cols, lat = dq.shape[2], expand.shape[0]
+    unit = width // (4 * dp)
+    n = 2 * dp
+    anywhere = pl.BlockSpec(memory_space=pl.ANY)
+    inside = pl.BlockSpec(memory_space=pltpu.VMEM)
+    vmem = pltpu.VMEM
+    sem = pltpu.SemaphoreType.DMA
+    share = lat // (2 * n) * KVH
+    bulk = [((rows, cols), BF), (dkv.shape, BF), (head_latent.shape, BF), (expand.shape, BF)]
+    bulk += [(x.shape, BF), (wq.shape, BF), (wl.shape, BF), (mg.shape, F32)]
+    sums = []
+    for blocks, high, wide in ((3, unit, cols), (2, share, cols), (1, 16, 128)):
+        sums += [vmem((blocks, 2 * n * high, wide), BF)] + [vmem((blocks, n * high, wide), BF)] * 2
+    return pl.pallas_call(
+        functools.partial(closing_kernel, dp),
+        in_specs=[anywhere] * 5 + [inside] + [anywhere] * 3 + [inside],
+        out_specs=[anywhere] + [inside] * 3,
+        out_shape=[
+            jax.ShapeDtypeStruct((2, rows // 2, width), BF),
+            jax.ShapeDtypeStruct((unit, 3 * cols), F32),
+            jax.ShapeDtypeStruct((share, 2 * cols), F32),
+            jax.ShapeDtypeStruct((16, 128), F32),
+        ],
+        scratch_shapes=[vmem(*b) for b in bulk]
+        + [
+            vmem((rows, cols), BF),
+            vmem((rows, lat), BF),
+            vmem((rows, lat), BF),
+            vmem((rows, lat), BF),
+            vmem((lat, 2 * cols), F32),
+            vmem((16, width), BF),
+            vmem((width, rows), BF),
+            vmem((width, rows // 2), BF),
+            vmem((2, rows // 2, width), BF),
+        ]
+        + sums
+        + [sem((8,)), sem((2,)), sem((2,)), sem((3,))]
+        + [sem((blocks, 3 + dp // 2)) for blocks in (3, 3, 2, 2, 1, 1)],
+        compiler_params=pltpu.CompilerParams(
+            collective_id=1, has_side_effects=True, vmem_limit_bytes=60 * 2**20
+        ),
+    )(dq, dkv, head_latent, expand, x, gain, wq, wl, mg, gain_two_grad)
+
+
 HEADS = 16
-KVH = 2
 LATD = 256
 HG = 8
 GROUPS = 8
@@ -1144,13 +1273,14 @@
         shards = (w_query, w_latent, expand_rows, gains)
         full, own_inputs = own_gather(dp, shards, inputs, ("xzy",) * 4)
     else:
-        shards = (w_query, w_latent, expand_rows, gains, w_output, w_down)
+        shards = (w_query, w_latent, expand_rows, gains, w_output)
         full = [lax.all_gather(w, ALL, axis=0) for w in shards]
         own_inputs = swap_sequences(inputs, seqs)
     gate_up = jnp.stack(
         [w_gate.reshape(drows, -1, CUT), w_up.reshape(drows, -1, CUT)], axis=2
     ).reshape(drows, -1)
     gu_full = lax.all_gather(gate_up, ALL, axis=0, tiled=True)
+    down_full = lax.all_gather(w_down, ALL, axis=0, tiled=True)
     query_full = full[0].reshape(width, -1)
     latent_full = full[1].reshape(width, -1)
     expand_full = full[2].reshape(devices, KVH, LATD // devices, -1)
@@ -1178,22 +1308,14 @@
     ).reshape(LATD, -1)
     head_pairs = dot_nn(head_latent, expand_local).astype(BF)
     if ring:
-        half = width // 2
-        attended, logsum, own_cotangent, output_full, down_full = attention_forward_gather(
-            dp,
-            head_queries,
-            head_pairs,
-            cotangent,
-            (w_output, w_down),
-            ((0, 0, width), (1, 0, half), (1, half, half)),
-            ("xzy", "zyx", "zxy"),
+        attended, logsum, own_cotangent, output_full = attention_forward_gather(
+            dp, head_queries, head_pairs, cotangent, (w_output,), ((0, 0, width),), ("xzy",)
         )
     else:
         attended, logsum = attention_forward(head_queries, head_pairs)
         own_cotangent = swap_sequences(cotangent, seqs)
-        output_full, down_full = full[4:]
+        output_full = full[4]
     output_full = output_full.reshape(-1, width)
-    down_full = down_full.reshape(-1, width)
     token_attended = swap_group(attended).reshape(groups, count, cols)
     seq_group = lax.dynamic_index_in_dim(group_ids, lax.axis_index("seq"), 0, keepdims=False)
     chosen = (seq_group == jnp.arange(GROUPS)).astype(F32)
@@ -1229,7 +1351,7 @@
             own_output,
             terms,
             ((0, 0, width), (1, 0, half), (1, half, half)),
-            ("yzx", "yxz", "xyz"),
+            ("yzx", "yxz", "yzx"),
         )
     else:
         query_back, pair_back = attention_backward(*attention)
@@ -1237,53 +1359,69 @@
         output_share, down_share = [
             lax.psum_scatter(w, ALL, scatter_dimension=0, tiled=True)[0].astype(F32) for w in terms
         ]
-    latent_terms = dot_nt(pair_back, expand_local).astype(BF)
-    expand_part = dot_tn(head_latent, pair_back)
-    expand_grad = lax.dynamic_update_slice(
-        jnp.zeros(expand_full.shape, BF),
-        expand_part.astype(BF).reshape(devices, 1, LATD // devices, -1),
-        (0, me * heads // HG, 0, me * heads % HG * 2 * DH),
-    )
-    query_token = swap_group(query_back).reshape(groups, count, cols)
-    latent_token = swap_group(
-        latent_terms.reshape(seqs, groups, rows, LATD).transpose(1, 0, 2, 3)
-    ).reshape(KVH, groups // KVH, count, LATD)
-    latent_token = jnp.sum(latent_token.astype(F32), axis=1).astype(BF)
-    query_grad = jnp.concatenate([dot_tn(normed_low, query_token[j]) for j in range(groups)], axis=1)
-    latent_grad = jnp.concatenate([dot_tn(normed_low, latent_token[g]) for g in range(KVH)], axis=1)
-    normed_back = sum(
-        dot_nt(query_token[j], query_full[:, j * cols : (j + 1) * cols]) for j in range(groups)
-    ) + sum(
-        dot_nt(latent_token[g], latent_full[:, g * LATD : (g + 1) * LATD]) for g in range(KVH)
-    )
-    input_part, gain_one_grad = norm_back(token_rows, inverse_one, gain_one, normed_back)
-    own_input_grad = (middle_grad + input_part).astype(BF).reshape(seqs, rows, width)
-    gain_grads = jnp.concatenate(
-        [gain_one_grad.reshape(devices, 1, drows), gain_two_grad.reshape(devices, 1, drows)], axis=2
-    ).astype(BF)
-    gain_grads = jnp.pad(gain_grads, ((0, 0), (0, 15), (0, 128 - 2 * drows)))
-    terms = (
-        query_grad.astype(BF).reshape(devices, drows, -1),
-        latent_grad.astype(BF).reshape(devices, drows, -1),
-        expand_grad.reshape(devices, -1, expand_grad.shape[3]),
-        gain_grads,
-    )
     if ring:
-        sums, input_grad = own_scatter(dp, terms, ("yzx",) * 4, own_input_grad)
+        input_grad, q_share, e_share, g_share = closing(
+            dp,
+            query_back.reshape(groups, count, cols),
+            pair_back,
+            head_latent,
+            expand_local,
+            x_rows,
+            gain_one,
+            query_full,
+            latent_full,
+            middle_grad,
+            gain_two_grad,
+        )
+        shard = (lax.axis_index("dp") * 2 + lax.axis_index("seq")) * 2 + me
+        own_gains = lax.dynamic_slice(g_share, (0, shard * drows % 128), (2, drows))
+        sums = (q_share[:, :width], q_share[:, width:], e_share)
     else:
+        latent_terms = dot_nt(pair_back, expand_local).astype(BF)
+        expand_part = dot_tn(head_latent, pair_back)
+        expand_grad = lax.dynamic_update_slice(
+            jnp.zeros(expand_full.shape, BF),
+            expand_part.astype(BF).reshape(devices, 1, LATD // devices, -1),
+            (0, me * heads // HG, 0, me * heads % HG * 2 * DH),
+        )
+        query_token = swap_group(query_back).reshape(groups, count, cols)
+        latent_token = swap_group(
+            latent_terms.reshape(seqs, groups, rows, LATD).transpose(1, 0, 2, 3)
+        ).reshape(KVH, groups // KVH, count, LATD)
+        latent_token = jnp.sum(latent_token.astype(F32), axis=1).astype(BF)
+        query_grad = jnp.concatenate([dot_tn(normed_low, query_token[j]) for j in range(groups)], axis=1)
+        latent_grad = jnp.concatenate([dot_tn(normed_low, latent_token[g]) for g in range(KVH)], axis=1)
+        normed_back = sum(
+            dot_nt(query_token[j], query_full[:, j * cols : (j + 1) * cols]) for j in range(groups)
+        ) + sum(
+            dot_nt(latent_token[g], latent_full[:, g * LATD : (g + 1) * LATD]) for g in range(KVH)
+        )
+        input_part, gain_one_grad = norm_back(token_rows, inverse_one, gain_one, normed_back)
+        own_input_grad = (middle_grad + input_part).astype(BF).reshape(seqs, rows, width)
+        gain_grads = jnp.concatenate(
+            [gain_one_grad.reshape(devices, 1, drows), gain_two_grad.reshape(devices, 1, drows)], axis=2
+        ).astype(BF)
+        gain_grads = jnp.pad(gain_grads, ((0, 0), (0, 15), (0, 128 - 2 * drows)))
+        terms = (
+            query_grad.astype(BF).reshape(devices, drows, -1),
+            latent_grad.astype(BF).reshape(devices, drows, -1),
+            expand_grad.reshape(devices, -1, expand_grad.shape[3]),
+            gain_grads,
+        )
         sums = [
             lax.psum_scatter(w, ALL, scatter_dimension=0, tiled=True)[0].astype(F32) for w in terms
         ]
+        own_gains = sums[3][0, : 2 * drows].reshape(2, drows)
         input_grad = swap_sequences(own_input_grad, seqs)
     return (
         output,
         input_grad,
-        sums[3][0, :drows],
+        own_gains[0],
         sums[0],
         sums[1],
         sums[2].reshape(expansion_weight.shape),
         output_share,
-        sums[3][0, drows : 2 * drows],
+        own_gains[1],
         gu_share[:, :, 0].reshape(drows, -1),
         gu_share[:, :, 1].reshape(drows, -1),
         down_share,

time: 517 us -> 474 us (0.917)
  waiting for transfers between devices: 0.03 us -> 41 us
  Pallas kernels: 393 us -> 353 us
  matrix products: 27.1 us -> 8.62 us
  blocking collectives: 16.4 us -> 6.32 us
  local copies, waits for them, and re-layouts: 31.2 us -> 23.3 us
  other arithmetic: 13.8 us -> 7.61 us
    all_gather x1, waiting for transfers between devices: 0.01 us -> 40.3 us  [local(): gu_full = lax.all_gather(gate_up, ALL, axis=0, tiled=True)]
    pallas_call x1, Pallas kernels: 80.3 us -> 48.9 us  [attention_forward_gather(): pl.pallas_call(functools.partial(forward_gather_kernel, dp, cuts, orders,...]
    pallas_call x1, Pallas kernels: 126 us -> 97.6 us  [feed_forward(): pl.pallas_call(functools.partial(ffn_kernel, dp), grid=(blocks + DOWN,),...]
    pallas_call x1, Pallas kernels: 35.2 us -> 62 us  [closing(): pl.pallas_call(functools.partial(closing_kernel, dp), in_specs=[anywhere]...]
    dot_general x10 -> x0, matrix products: 17.9 us -> none  [the longest x5 10.3 us: dot_nt(): lax.dot_general(a, b, (((1,), (1,)), ((), ())), preferred_element_type=F32)]
    all_to_all x3 -> x1, blocking collectives: 16.4 us -> 6.32 us  [swap_group(): return lax.all_to_all(blocks, 'grp', 0, 0, tiled=True)]
    unnamed x76 -> x54, local copies, waits for them, and re-layouts: 16.1 us -> 9.86 us
  transfers between devices with their start and end apart: 4 -> 5, of which waited for: 0 -> 1; matrix products, arithmetic and copies ran while one was open for 5% -> 5% of each run, Pallas kernels for 26% -> 21%
where the time goes in v5:
time: 474 us; the launch traced here: 468 us
  Pallas kernels  353 us (74%)
  waiting for transfers between devices  41 us (9%)
  local copies, waits for them, and re-layouts  23.3 us (5%)
  between operations  14.7 us (3%)
  starting transfers between devices  12.8 us (3%)
  matrix products  8.62 us (2%)
  other arithmetic  7.61 us (2%)
  blocking collectives  6.32 us (1%)
    pallas_call x1, Pallas kernels, feed_forward(): pl.pallas_call(functools.partial(ffn_kernel, dp), grid=(blocks + DOWN,),...  97.6 us
    pallas_call x1, Pallas kernels, attention_backward_scatter(): pl.pallas_call(functools.partial(backward_scatter_kernel, dp, blk, cuts,...  84.7 us
    pallas_call x1, Pallas kernels, closing(): pl.pallas_call(functools.partial(closing_kernel, dp), in_specs=[anywhere]...  62 us
    pallas_call x1, Pallas kernels, attention_forward_gather(): pl.pallas_call(functools.partial(forward_gather_kernel, dp, cuts, orders,...  48.9 us
    pallas_call x1, Pallas kernels, own_gather(): pl.pallas_call(functools.partial(gather_kernel, dp, orders), in_specs=[an...  47 us
    all_gather x1, waiting for transfers between devices, local(): gu_full = lax.all_gather(gate_up, ALL, axis=0, tiled=True)  40.3 us
    pallas_call x1, Pallas kernels, branch_back(): pl.pallas_call(branch_kernel, grid=(rows // part,), in_specs=[pl.BlockSpe...  13 us
    all_to_all x3, starting transfers between devices, swap_group(): return lax.all_to_all(blocks, 'grp', 0, 0, tiled=True)  12.7 us
  transfers between devices with their start and end apart: 5, of which 1 were waited for; matrix products, arithmetic and copies ran while one was open for 5% of the time, Pallas kernels for 21%

profile of v5, /device:TPU:0, one launch (start us, length us, event | category | flops | bytes accessed | tf_op | source)
XLA Modules:
  0.0 467.7 jit_solution(14004116697860909425)
XLA Ops:
  12.2 47.0 %shard_map.212 = (bf16[32,32,1024]{2,1,0:T(8,128)(2,1)}, bf16[32,32,512]{2,1,0:T(8,128)(2,1)}, bf16[32,16,1024]{2,1,0:T(8,128)(2,1)}, bf16[32,16,128]{2,1,0:T(8,128)(2,1)}, bf16[2,512,1024]{2,1,0:T(8,128)(2,1)}) custom-call(bf16[32,1024]{1,0:T(8,128)(2,1)} %refs_0_.1, bf16[32,512]{1,0:T(8,128)(2,1)} %refs_1_.1, bf16[16,1024]{1,0:T(8,128)(2,1)} %bitcast.77, ...), custom_call_target="tpu_custom_call" | custom-call | tf_op jit(solution)/shard_map/pallas_call | solution.py:282
  59.3 2.2 multiply_reduce_fusion
  65.2 1.1 pad_maximum_fusion.1
  66.3 3.6 all-to-all-start.1
  69.9 2.6 convolution_convert_fusion.1
  72.5 1.3 convolution_convert_fusion.2
  73.8 1.5 pad_maximum_fusion
  75.3 5.4 %all-to-all-start = ((bf16[2,2,512,512]{3,2,1,0:T(8,128)(2,1)}), bf16[2,2,512,512]{3,2,1,0:T(8,128)(2,1)}, u32[]{:S(2)}, u32[]{:S(2)}) async-start(bf16[2,2,512,512]{3,2,1,0:T(8,128)(2,1)} %pad_maximum_fusion), calls=%async_computation | async-start | bytes 4194304 | tf_op jit(solution)/shard_map/all_to_all | solution.py:1240
  80.8 1.5 copy-done.15
  82.3 3.3 convolution_convert_fusion.refs_1_
  85.7 48.9 %shard_map.213 = (bf16[2,2,512,512]{3,2,1,0:T(8,128)(2,1)}, f32[4,2,2048]{2,1,0:T(2,128)}, bf16[2,512,1024]{2,1,0:T(8,128)(2,1)}, bf16[32,32,1024]{2,1,0:T(8,128)(2,1)}) custom-call(bf16[2,2,512,512]{3,2,1,0:T(8,128)(2,1)} %all-to-all-done.refs_0_, bf16[2048,1024]{1,0:T(8,128)(2,1)} %convolution_convert_fusion.refs_1_, bf16[2,512,1024]{2,1,0:T(8,128)(2,1)} %refs_2_.1, ...), custom_call_target="tpu_custom_call" | custom-call | flops 17179869184 | bytes 8388608 | tf_op jit(solution)/shard_map/pallas_call | solution.py:492
  134.7 3.8 all-to-all-start.2
  140.7 1.2 fusion.6
  141.9 40.3 %all-gather.3.cloned.1.call-done.gu_ref = bf16[1024,5632]{1,0:T(8,128)(2,1)} async-done(((bf16[32,5632]{1,0:T(8,128)(2,1)}), bf16[1024,5632]{1,0:T(8,128)(2,1)}) %all-gather.3.cloned.1.call-update) | async-done | bytes 11534352 | tf_op jit(solution)/shard_map/all_gather | solution.py:1282
  182.3 97.6 %shard_map.214 = (bf16[1024,1024]{1,0:T(8,128)(2,1)}, f32[1024,1024]{1,0:T(8,128)}, f32[1024,1024]{1,0:T(8,128)}, f32[32,5632]{1,0:T(8,128)}, bf16[2816,1024]{1,0:T(8,128)(2,1)}) custom-call(f32[1,1]{1,0:T(1,128)} %bitcast.14.scale_ref, bf16[1024,1024]{1,0:T(8,128)(2,1)} %bitcast.53, bf16[2,1024,512]{2,1,0:T(8,128)(2,1)} %bitcast.60, ...), custom_call_target="tpu_custom_call" | custom-call | flops 53150220288 | bytes 8388608 | tf_op jit(solution)/shard_map/pallas_call | solution.py:924
  279.9 13.0 %shard_map.215 = (f32[1024,1024]{1,0:T(8,128)}, bf16[2,1024,512]{2,1,0:T(8,128)(2,1)S(1)}, bf16[1024,1024]{1,0:T(8,128)(2,1)S(1)}, f32[1,1024]{1,0:T(1,128)S(1)}) custom-call(f32[1,1]{1,0:T(1,128)} %bitcast.14.scale_ref, f32[1024,1024]{1,0:T(8,128)} %get-tuple-element.46.mid_ref, f32[1024,1024]{1,0:T(8,128)} %get-tuple-element.47.nb_ref, ...), custom_call_target="tpu_custom_call" | custom-call | flops 4294967296 | bytes 8388608 | tf_op jit(solution)/shard_map/pallas_call | solution.py:1005
  293.0 6.3 %all_to_all.20.refs_2_ = bf16[2,2,512,512]{3,2,1,0:T(8,128)(2,1)} all-to-all(bf16[2,2,512,512]{3,2,1,0:T(8,128)(2,1)S(1)} %bitcast.51), channel_id=1, replica_groups=mesh['dp'=8,'seq'=2,'grp'=2] {'grp'}, dimensions={0} | all-to-all | bytes 4194304 | tf_op jit(solution)/shard_map/all_to_all | solution.py:1240
  299.3 84.7 %shard_map.216 = (bf16[2,2,512,512]{3,2,1,0:T(8,128)(2,1)}, bf16[2048,1024]{1,0:T(8,128)(2,1)}, bf16[2,512,1024]{2,1,0:T(8,128)(2,1)}, f32[32,1024]{1,0:T(8,128)}, f32[88,1024]{1,0:T(8,128)}) custom-call(bf16[2,2,512,512]{3,2,1,0:T(8,128)(2,1)} %all-to-all-done.refs_0_, bf16[2048,1024]{1,0:T(8,128)(2,1)} %convolution_convert_fusion.refs_1_, ...), custom_call_target="tpu_custom_call" | custom-call | flops 34359738368 | bytes 8388608 | tf_op jit(solution)/shard_map/pallas_call | solution.py:651
  384.0 62.0 %shard_map.217 = (bf16[2,512,1024]{2,1,0:T(8,128)(2,1)}, f32[32,1536]{1,0:T(8,128)}, f32[16,1024]{1,0:T(8,128)}, f32[16,128]{1,0:T(8,128)}) custom-call(bf16[2,1024,512]{2,1,0:T(8,128)(2,1)} %bitcast.65, bf16[2048,1024]{1,0:T(8,128)(2,1)} %get-tuple-element.55.refs_1_, bf16[2048,256]{1,0:T(8,128)(2,1)} %bitcast.56, bf16[256,1024]{1,0:T(8,128)(2,1)} %copy-done.5, ...), custom_call_target="tpu_custom_call" | custom-call | tf_op jit(solution)/shard_map/pallas_call | solution.py:1177
  446.0 1.5 slice.44
  447.5 1.6 slice.43
  451.0 2.0 slice_reduce_fusion
  454.9 1.3 copy.45
  457.3 1.3 copy.46
  (80 shorter events, 17.9 us)
Async XLA Ops:
  7.2 4.4 copy-start.19
  7.2 4.4 copy-start.20
  7.2 134.7 %all-gather.5.cloned.1.call-start = ((), (), s32[]{:S(2)}) async-start(), calls=%async_computation.5 | async-start | bytes 5947392 | tf_op jit(solution)/shard_map/all_gather | solution.py:1283
  7.9 174.3 %all-gather.3.cloned.1.call-start = ((), (), s32[]{:S(2)}) async-start(), calls=%async_computation.4 | async-start | bytes 11894784 | tf_op jit(solution)/shard_map/all_gather | solution.py:1282
  59.3 3.2 copy-start.3
  65.2 4.7 %copy-start.8 = (bf16[1024,1024]{1,0:T(8,128)(2,1)S(1)}, bf16[1024,1024]{1,0:T(8,128)(2,1)}, u32[]{:S(2)}) copy-start(bf16[1024,1024]{1,0:T(8,128)(2,1)} %copy-done.7) | copy-start | bytes 6291460
  66.3 9.0 %all-to-all-start.1 = ((bf16[2,2,512,256]{3,2,1,0:T(8,128)(2,1)}), bf16[2,2,512,256]{3,2,1,0:T(8,128)(2,1)S(1)}, u32[]{:S(2)}, u32[]{:S(2)}) async-start(bf16[2,2,512,256]{3,2,1,0:T(8,128)(2,1)} %pad_maximum_fusion.1), calls=%async_computation.1 | async-start | bytes 2097152 | tf_op jit(solution)/shard_map/all_to_all | solution.py:1240
  69.9 2.6 copy-start.11
  75.3 10.4 %all-to-all-start = ((bf16[2,2,512,512]{3,2,1,0:T(8,128)(2,1)}), bf16[2,2,512,512]{3,2,1,0:T(8,128)(2,1)}, u32[]{:S(2)}, u32[]{:S(2)}) async-start(bf16[2,2,512,512]{3,2,1,0:T(8,128)(2,1)} %pad_maximum_fusion), calls=%async_computation | async-start | bytes 4194304 | tf_op jit(solution)/shard_map/all_to_all | solution.py:1240
  80.7 1.6 copy-start.15
  80.8 4.9 %copy-start.4 = (bf16[2,2,512,256]{3,2,1,0:T(8,128)(2,1)}, bf16[2,2,512,256]{3,2,1,0:T(8,128)(2,1)S(1)}, u32[]{:S(2)}) copy-start(bf16[2,2,512,256]{3,2,1,0:T(8,128)(2,1)S(1)} %copy.33) | copy-start | bytes 3145732
  82.3 3.3 copy-start.5
  134.6 5.5 %copy-start.21 = (s32[2]{0:T(128)S(1)}, s32[2]{0:T(128)}, u32[]{:S(2)}) copy-start(s32[2]{0:T(128)} %param.15) | copy-start | bytes 28
  134.6 6.0 %copy-start.22 = (f32[8]{0:T(128)S(1)}, f32[8]{0:T(128)}, u32[]{:S(2)}) copy-start(f32[8]{0:T(128)} %param.16) | copy-start | bytes 100
  134.7 7.3 %all-to-all-start.2 = ((bf16[2,2,512,512]{3,2,1,0:T(8,128)(2,1)}), bf16[2,2,512,512]{3,2,1,0:T(8,128)(2,1)S(1)}, u32[]{:S(2)}, u32[]{:S(2)}) async-start(bf16[2,2,512,512]{3,2,1,0:T(8,128)(2,1)} %get-tuple-element.43.refs_3_), calls=%async_computation.2 | async-start | bytes 4194304 | tf_op jit(solution)/shard_map/all_to_all | solution.py:1240
  141.9 40.3 %copy-start.6 = (bf16[2,2,512,512]{3,2,1,0:T(8,128)(2,1)}, bf16[2,2,512,512]{3,2,1,0:T(8,128)(2,1)S(1)}, u32[]{:S(2)}) copy-start(bf16[2,2,512,512]{3,2,1,0:T(8,128)(2,1)S(1)} %all-to-all-done.2) | copy-start | bytes 6291460
  182.3 97.7 %copy-start = (bf16[1,1024]{1,0:T(2,128)(2,1)S(1)}, bf16[1,1024]{1,0:T(2,128)(2,1)}, u32[]{:S(2)}) copy-start(bf16[1,1024]{1,0:T(2,128)(2,1)} %reshape_squeeze.10.gain_ref) | copy-start | bytes 6148
  293.0 6.3 %copy-start.1 = (f32[1,1024]{1,0:T(1,128)}, f32[1,1024]{1,0:T(1,128)S(1)}, u32[]{:S(2)}) copy-start(f32[1,1024]{1,0:T(1,128)S(1)} %get-tuple-element.57.refs_9_) | copy-start | bytes 12292
  293.0 6.3 %copy-start.2 = (bf16[1024,1024]{1,0:T(8,128)(2,1)}, bf16[1024,1024]{1,0:T(8,128)(2,1)S(1)}, u32[]{:S(2)}) copy-start(bf16[1024,1024]{1,0:T(8,128)(2,1)S(1)} %get-tuple-element.51) | copy-start | bytes 6291460
  384.0 66.4 %copy-start.13 = (f32[32,5632]{1,0:T(8,128)S(1)}, f32[32,5632]{1,0:T(8,128)}, u32[]{:S(2)}) copy-start(f32[32,5632]{1,0:T(8,128)} %get-tuple-element.63) | copy-start | bytes 2162692
  451.0 3.9 copy-start.9
  454.9 2.3 copy-start.10
  457.3 2.0 copy-start.16
  457.3 2.6 copy-start.14
  (4 other events, 4.5 us)
Sparse Core Ops, SparseCore 0:
  10.9 74.0 all-gather.4
  88.4 93.8 all-gather.2

commit v6 on v5

--- a/solution.py
+++ b/solution.py
@@ -295,9 +295,11 @@
     return [pltpu.SemaphoreType.DMA((count, 2 * dp))] * 4
 
 
-def run_at(plan, point):
-    for step in sorted({k[0] for k in plan if k[1] == point}):
-        tasks = plan[step, point]
+def run_at(plan, point, when=None):
+    for step, at in sorted((k for k in plan if k[0] != "last"), key=str):
+        if at != (point if when is None else when):
+            continue
+        tasks = plan[step, at]
 
         @pl.when(pl.program_id(0) == step)
         def _(tasks=tasks):
@@ -305,9 +307,18 @@
                 task()
 
 
+GATHER_AT = (0, 2, 3, 4, 5, 6, 7, 9, 10, 11, 12, 13, 14, 15, 15)
+SCATTER_AT = (1, 1, 1, 1, 2, 2, 2, 2, 6, 7, 8, 9, 10, 11, 13, 16)
+
+
+def put(plan, number, count, table, steps, points, task):
+    at = table[number * len(table) // count] * steps * points // 16
+    key = ("last", 0) if at >= steps * points else divmod(at, points)
+    plan.setdefault(key, []).append(task)
+
+
 def gather_plan(place, works, swap, steps, points):
     arrivals = [work.arrivals() for work in works]
-    total = steps * points
 
     def begin():
         place.greet()
@@ -326,19 +337,15 @@
         for copy in swap:
             copy.wait()
 
-    plan = {}
-    count = len(arrivals[0])
-    plan[0, 0] = [begin]
-    for i in range(count):
-        at = 2 + i * (total - 3) // count
-        plan.setdefault(divmod(at, points), []).append(functools.partial(forward, i))
-    plan.setdefault(divmod(total, points), []).append(end)
+    plan = {(0, "first"): [begin]}
+    for i in range(len(arrivals[0])):
+        put(plan, i, len(arrivals[0]), GATHER_AT, steps, points, functools.partial(forward, i))
+    plan.setdefault(("last", 0), []).append(end)
     return plan
 
 
 def scatter_plan(place, works, outs, swap, steps, points):
     turns = [work.turn() for work in works]
-    total = steps * points
     count = len(turns[0])
 
     def begin():
@@ -360,9 +367,8 @@
 
     plan = {(0, 0): [begin]}
     for i in range(count):
-        at = 1 + i // 2 if i < count // 2 else 6 + (i - count // 2) * (total - 6) // (count - count // 2)
-        plan.setdefault(divmod(at, points), []).append(functools.partial(add, i))
-    plan.setdefault(divmod(total, points), []).append(end)
+        put(plan, i, count, SCATTER_AT, steps, points, functools.partial(add, i))
+    plan.setdefault(("last", 0), []).append(end)
     return plan
 
 
@@ -425,13 +431,15 @@
 
 
 def forward_gather_kernel(dp, cuts, orders, pairs, *refs):
-    q_ref, kv_ref, x_in = refs[:3]
+    x_ref, gain_ref, wq_ref, wl_ref, ex_ref, x_in = refs[:6]
     sources = 1 + max(cut[0] for cut in cuts)
-    srcs, refs = refs[3 : 3 + sources], refs[3 + sources :]
-    o_ref, lse_ref, x_out = refs[:3]
-    outs, refs = refs[3 : 3 + sources], refs[3 + sources :]
-    vt_s, x_sem, sems = refs[0], refs[1], refs[2:]
+    srcs, refs = refs[6 : 6 + sources], refs[6 + sources :]
+    o_ref, lse_ref, q_out, kv_out, hl_out, x_out = refs[:6]
+    outs, refs = refs[6 : 6 + sources], refs[6 + sources :]
+    vt_s, x_sem, low_s, q_send, lat_send, q_s, kv_s, hl_s, far_send, far_recv, save_sem = refs[:11]
+    sems = refs[11:]
     place = Place(dp)
+    c = place.core
     works = []
     for number, (a, first, size) in enumerate(cuts):
         cut = pl.ds(first, size)
@@ -446,17 +454,79 @@
                 number,
             )
         )
-    points = q_ref.shape[0] * q_ref.shape[1]
+    groups, chunks, rows, cols = q_s.shape
+    lat = hl_s.shape[1]
+    points = groups * chunks
     plan = gather_plan(place, works, block_swap(x_in, x_out, x_sem, place), pairs, points)
-    forward_body(q_ref, kv_ref, o_ref, lse_ref, vt_s, lambda i: run_at(plan, i))
-    for point in range(points):
-        tasks = plan.get((pairs, point))
-        if tasks:
-
-            @pl.when(pl.program_id(0) == pairs - 1)
-            def _(tasks=tasks):
-                for task in tasks:
-                    task()
+    run_at(plan, 0, "first")
+
+    def at(index, size):
+        return pl.ds(pl.multiple_of(index * size, size), size)
+
+    def far_q():
+        return remote(q_send, q_s.at[c], far_send.at[0], far_recv.at[0], place.pair())
+
+    def far_l(u):
+        return remote(
+            lat_send.at[u],
+            hl_s.at[at(u * groups + c, rows)],
+            far_send.at[1 + u],
+            far_recv.at[1 + u],
+            place.pair(),
+        )
+
+    def saves():
+        return [
+            pltpu.make_async_copy(src, dst, save_sem.at[i])
+            for i, (src, dst) in enumerate(((q_s, q_out), (kv_s, kv_out), (hl_s, hl_out)))
+        ]
+
+    @pl.when(pl.program_id(0) == 0)
+    def _():
+        gain = gain_ref[...].astype(F32)
+        for u in range(chunks):
+            chunk = slice(u * rows, (u + 1) * rows)
+            values = x_ref[chunk].astype(F32)
+            inverse = lax.rsqrt(jnp.mean(values * values, axis=-1, keepdims=True) + EPSILON)
+            low_s[chunk] = (values * inverse * gain).astype(BF)
+            lat_send[u] = dot_nn(low_s[chunk], wl_ref[:, at(1 - c, lat)]).astype(BF)
+            far_l(u).start()
+        for u in range(chunks):
+            chunk = slice(u * rows, (u + 1) * rows)
+            q_send[u] = dot_nn(low_s[chunk], wq_ref[:, at(1 - c, cols)]).astype(BF)
+        far_q().start()
+        for u in range(chunks):
+            chunk = slice(u * rows, (u + 1) * rows)
+            hl_s[at(u * groups + c, rows)] = dot_nn(low_s[chunk], wl_ref[:, at(c, lat)]).astype(BF)
+            q_s[c, u] = dot_nn(low_s[chunk], wq_ref[:, at(c, cols)]).astype(BF)
+        for u in range(chunks):
+            far_l(u).wait_recv()
+        for k in range(groups * chunks):
+            chunk = slice(k * rows, (k + 1) * rows)
+            kv_s[chunk] = dot_nn(hl_s[chunk], ex_ref[...]).astype(BF)
+        far_q().wait_recv()
+        for save in saves():
+            save.start()
+
+    pid = pl.program_id(0)
+    forward_body(
+        q_s.at[:, :, :, at(pid, 128)],
+        kv_s.at[:, at(pid, 256)],
+        o_ref,
+        lse_ref,
+        vt_s,
+        lambda i: run_at(plan, i),
+    )
+
+    @pl.when(pid == pairs - 1)
+    def _():
+        far_q().wait_send()
+        for u in range(chunks):
+            far_l(u).wait_send()
+        for save in saves():
+            save.wait()
+        for task in plan["last", 0]:
+            task()
 
 
 def forward_specs(q, kv):
@@ -485,24 +555,49 @@
     )(q, kv)
 
 
-def attention_forward_gather(dp, q, kv, blocks, shards, cuts, orders):
-    pairs, ins, outs, shapes, scratch, estimate = forward_specs(q, kv)
+def attention_forward_gather(dp, x, gain, wq, wl, expand, blocks, shards, cuts, orders):
+    rows, width = blocks.shape[1], x.shape[1]
+    cols, lat = width // 2, expand.shape[0]
+    seq = 4 * rows
+    q = jax.ShapeDtypeStruct((2, 2, rows, cols), BF)
+    kv = jax.ShapeDtypeStruct((seq, 2 * cols), BF)
+    hl = jax.ShapeDtypeStruct((seq, lat), BF)
+    pairs, _, outs, shapes, scratch, estimate = forward_specs(q, kv)
     anywhere = pl.BlockSpec(memory_space=pl.ANY)
     count = len(shards)
+    sem = pltpu.SemaphoreType.DMA
+
+    def whole(w):
+        return pl.BlockSpec(w.shape, lambda p: (0, 0), pipeline_mode=pl.Buffered(1))
+
     return pl.pallas_call(
         functools.partial(forward_gather_kernel, dp, cuts, orders, pairs),
         grid=(pairs,),
-        in_specs=ins + [anywhere] * (1 + count),
-        out_specs=outs + [anywhere] * (1 + count),
+        in_specs=[whole(w) for w in (x, gain, wq, wl, expand)] + [anywhere] * (1 + count),
+        out_specs=outs + [anywhere] * (4 + count),
         out_shape=shapes
+        + [q, kv, hl]
         + [jax.ShapeDtypeStruct(blocks.shape, blocks.dtype)]
         + [jax.ShapeDtypeStruct((4 * dp, *w.shape), w.dtype) for w in shards],
-        scratch_shapes=scratch + [pltpu.SemaphoreType.DMA((3,))] + gather_sems(dp, len(cuts)),
+        scratch_shapes=scratch
+        + [
+            sem((3,)),
+            pltpu.VMEM(x.shape, BF),
+            pltpu.VMEM((2, rows, cols), BF),
+            pltpu.VMEM((2, rows, lat), BF),
+            pltpu.VMEM(q.shape, BF),
+            pltpu.VMEM(kv.shape, BF),
+            pltpu.VMEM(hl.shape, BF),
+            sem((3,)),
+            sem((3,)),
+            sem((3,)),
+        ]
+        + gather_sems(dp, len(cuts)),
         compiler_params=pltpu.CompilerParams(
-            vmem_limit_bytes=56 * 2**20, collective_id=2, has_side_effects=True
+            vmem_limit_bytes=60 * 2**20, collective_id=2, has_side_effects=True
         ),
         cost_estimate=estimate,
-    )(q, kv, blocks, *shards)
+    )(x, gain, wq, wl, expand, blocks, *shards)
 
 
 def backward_body(blk, q_ref, kv_ref, do_ref, o_ref, lse_ref, dq_ref, dkv_ref,
@@ -599,14 +694,11 @@
     points = ins[1].shape[0] // blk
     plan = scatter_plan(place, works, targets, block_swap(x_in, x_out, x_sem, place), pairs, points)
     backward_body(blk, *ins, *attn_outs, *scratch, point=lambda i: run_at(plan, i))
-    for point in range(points):
-        tasks = plan.get((pairs, point))
-        if tasks:
-
-            @pl.when(pl.program_id(0) == pairs - 1)
-            def _(tasks=tasks):
-                for task in tasks:
-                    task()
+
+    @pl.when(pl.program_id(0) == pairs - 1)
+    def _():
+        for task in plan["last", 0]:
+            task()
 
 
 def backward_specs(q, kv):
@@ -677,7 +769,8 @@
 
 class BlockSums:
 
-    def __init__(self, dp, stage, pair_buf, ring_buf, send, recv, out_ref):
+    def __init__(self, dp, stage, pair_buf, ring_buf, send, recv, out_ref, last_ref=None):
+        self.last_ref = last_ref
         self.place = Place(dp)
         self.stage, self.pair_buf, self.ring_buf = stage, pair_buf, ring_buf
         self.send, self.recv, self.out_ref = send, recv, out_ref
@@ -748,7 +841,10 @@
             for z in range(1, self.place.sizes["z"]):
                 total = total + self.ring_buf[j, z * self.unit : (z + 1) * self.unit].astype(F32)
             wide = total.shape[1]
-            self.out_ref[:, pl.ds(pl.multiple_of(j * wide, wide), wide)] = total
+            if self.last_ref is not None and j == self.pair_buf.shape[0] - 1:
+                self.last_ref[...] = total
+            else:
+                self.out_ref[:, pl.ds(pl.multiple_of(j * wide, wide), wide)] = total
         if phase < 4:
             for hop in self.hops(odd, phase):
                 self.hop(j, *hop).start()
@@ -761,7 +857,12 @@
 
 
 def ffn_kernel(dp, scale_ref, x_ref, att_ref, wo_ref, gain_ref, cot_ref, gu_ref, down_ref,
-               res_ref, mid_ref, nb_ref, gu_out, down_out, *refs):
+               res_ref, nb_ref, gu_out, down_out, *refs):
+    if dp:
+        gg_ref, heads_out, og_out, refs = refs[0], refs[1], refs[2], refs[3:]
+        mid_ref, out_sem, far_sem, refs = refs[0], refs[1], refs[2], refs[3:]
+    else:
+        mid_ref, refs = refs[0], refs[1:]
     n2_s, n2t_s, up_s, acc_s, ht_s, back_s, gu_stage, down_stage, gu_sem, down_sem = refs[:10]
     step = pl.program_id(0)
     rows, width = x_ref.shape
@@ -862,7 +963,7 @@
         there = down_out.at[pl.ds(pl.multiple_of(p * tall, tall), tall)]
         return pltpu.make_async_copy(down_stage.at[slot], there, down_sem.at[slot])
 
-    @pl.when(step >= blocks)
+    @pl.when(jnp.logical_and(step >= blocks, step < blocks + DOWN))
     def _():
         p = step - blocks
 
@@ -884,13 +985,54 @@
             if dp:
                 sums.pair(blocks - 2).wait_send()
                 sums.pair(blocks - 1).wait_send()
-                sums.finish([j % 2 for j in range(blocks)])
             else:
                 gu_copy(blocks - 2).wait()
                 gu_copy(blocks - 1).wait()
             down_copy(p - 1).wait()
             down_copy(p).wait()
 
+    if not dp:
+        return
+    place = sums.place
+    c = place.core
+    ends = [
+        remote(gu_stage.at[1 - c], heads_out.at[c], far_sem.at[0], far_sem.at[1], place.pair()),
+        pltpu.make_async_copy(gu_stage.at[c], heads_out.at[c], out_sem.at[0]),
+        pltpu.make_async_copy(n2t_s, og_out, out_sem.at[1]),
+    ]
+    for q, at in enumerate(chunks):
+
+        @pl.when(step == blocks + DOWN + q)
+        def _(q=q, at=at):
+            mid, nback, gain = mid_ref[at], nb_ref[at], gain_ref[...].astype(F32)
+            inverse = lax.rsqrt(jnp.mean(mid * mid, axis=-1, keepdims=True) + EPSILON)
+            scaled = nback * gain
+            middle_grad = cot_ref[at].astype(F32) * scale_ref[0, 0] + (
+                inverse * scaled
+                - mid
+                * (inverse * inverse * inverse)
+                * jnp.mean(scaled * mid, axis=-1, keepdims=True)
+            )
+            gain_part = jnp.sum(nback * mid * inverse, axis=0, keepdims=True)
+            gg_ref[...] = gain_part if q == 0 else gg_ref[...] + gain_part
+            nb_ref[at] = middle_grad
+            branch = middle_grad.astype(BF)
+            n2_s[at] = branch
+            for j in range(heads):
+                gu_stage[j, at] = dot_nt(branch, wo_ref[j * cols : (j + 1) * cols]).astype(BF)
+            if q == len(chunks) - 1:
+                ends[0].start()
+                ends[1].start()
+
+    @pl.when(step == blocks + DOWN + len(chunks))
+    def _():
+        for j in range(heads):
+            n2t_s[j * cols : (j + 1) * cols] = dot_tn(att_ref[j], n2_s[...]).astype(BF)
+        ends[2].start()
+        sums.finish([j % 2 for j in range(blocks)])
+        for end in ends:
+            end.wait()
+
 
 def feed_forward(dp, scale, x, att, wo, gain, cot, gu, down):
     rows, width = x.shape
@@ -906,24 +1048,27 @@
 
     shape = jax.ShapeDtypeStruct
     anywhere = pl.BlockSpec(memory_space=pl.ANY)
-    out = [shape((rows, width), BF), shape((rows, width), F32), shape((rows, width), F32)]
+    out = [shape((rows, width), BF), shape((rows, width), F32)]
     out_specs = [whole(w) for w in out]
-    scratch = []
+    first, scratch = [], []
     params = {}
+    steps = blocks + DOWN
+    sem = pltpu.SemaphoreType.DMA
     if dp:
-        out.append(shape((width // (4 * dp), 2 * size), F32))
-        out_specs.append(whole(out[-1]))
-        sem = pltpu.SemaphoreType.DMA((blocks, 3 + dp // 2))
-        scratch = [pltpu.VMEM((blocks, width // 2, 2 * CUT), BF)] * 2 + [sem] * 2
+        out += [shape((width // (4 * dp), 2 * size), F32), shape((size, width), BF)]
+        out += [shape((1, width), F32), shape(att.shape, BF), shape((width, width), BF)]
+        out_specs += [whole(out[2]), anywhere, whole(out[4]), anywhere, anywhere]
+        first = [pltpu.VMEM((rows, width), F32), sem((2,)), sem((2,))]
+        sems = sem((blocks, 3 + dp // 2))
+        scratch = [pltpu.VMEM((blocks, width // 2, 2 * CUT), BF)] * 2 + [sems] * 2
         params = {"collective_id": 4, "has_side_effects": True}
+        steps += rows // min(PART, rows) + 1
     else:
-        out.append(shape((width, 2 * size), BF))
-        out_specs.append(anywhere)
-    out.append(shape((size, width), BF))
-    out_specs.append(anywhere)
+        out += [shape((width, 2 * size), BF), shape((size, width), BF), shape((rows, width), F32)]
+        out_specs += [anywhere, anywhere, whole(out[4])]
     return pl.pallas_call(
         functools.partial(ffn_kernel, dp),
-        grid=(blocks + DOWN,),
+        grid=(steps,),
         in_specs=[
             pl.BlockSpec(memory_space=pltpu.SMEM),
             whole(x),
@@ -937,6 +1082,7 @@
         out_specs=out_specs,
         out_shape=out,
         scratch_shapes=[
+            *first,
             pltpu.VMEM((rows, width), BF),
             pltpu.VMEM((width, rows), BF),
             pltpu.VMEM((rows, width), BF),
@@ -1029,7 +1175,8 @@
 
 def closing_kernel(dp, *refs):
     dq_in, dkv_in, hl_in, ex_in, x_in, gain_ref, wq_in, wl_in, mg_in, gg_ref = refs[:10]
-    ig_out, q_out, e_out, g_out = refs[10:14]
+    ig_out, q_out, l_out, e_out, g_out = refs[10:15]
+    refs = refs[:14] + refs[15:]
     dq, dkv, hl, ex, x, wq, wl, mg = refs[14:22]
     far_dq, far_lat, lat_send, lat_own, e_s, g_s, n1t, flip, ig = refs[22:31]
     q_stage, q_pair, q_ring, e_stage, e_pair, e_ring, g_stage, g_pair, g_ring = refs[31:40]
@@ -1058,7 +1205,7 @@
     far_l = remote(lat_send, far_lat, far_send.at[1], far_recv.at[1], place.pair())
     far_q.start()
 
-    q_sums = BlockSums(dp, q_stage, q_pair, q_ring, q_send, q_recv, q_out)
+    q_sums = BlockSums(dp, q_stage, q_pair, q_ring, q_send, q_recv, q_out, l_out)
     e_sums = BlockSums(dp, e_stage, e_pair, e_ring, e_send, e_recv, e_out)
     g_sums = BlockSums(dp, g_stage, g_pair, g_ring, g_send, g_recv, g_out)
     order = q_sums.order()
@@ -1177,10 +1324,11 @@
     return pl.pallas_call(
         functools.partial(closing_kernel, dp),
         in_specs=[anywhere] * 5 + [inside] + [anywhere] * 3 + [inside],
-        out_specs=[anywhere] + [inside] * 3,
+        out_specs=[anywhere] + [inside] * 4,
         out_shape=[
             jax.ShapeDtypeStruct((2, rows // 2, width), BF),
-            jax.ShapeDtypeStruct((unit, 3 * cols), F32),
+            jax.ShapeDtypeStruct((unit, 2 * cols), F32),
+            jax.ShapeDtypeStruct((unit, cols), F32),
             jax.ShapeDtypeStruct((share, 2 * cols), F32),
             jax.ShapeDtypeStruct((16, 128), F32),
         ],
@@ -1280,41 +1428,61 @@
         [w_gate.reshape(drows, -1, CUT), w_up.reshape(drows, -1, CUT)], axis=2
     ).reshape(drows, -1)
     gu_full = lax.all_gather(gate_up, ALL, axis=0, tiled=True)
-    down_full = lax.all_gather(w_down, ALL, axis=0, tiled=True)
     query_full = full[0].reshape(width, -1)
     latent_full = full[1].reshape(width, -1)
     expand_full = full[2].reshape(devices, KVH, LATD // devices, -1)
     gain_one = full[3][:, 0, :drows].reshape(width).astype(F32)
     gain_two = full[3][:, 0, drows : 2 * drows].reshape(1, width)
 
-    token_rows = own_inputs.astype(F32).reshape(count, width)
-    normed, inverse_one = norm_parts(token_rows, gain_one)
-    normed_low = normed.astype(BF)
-    query_send = jnp.stack(
-        [dot_nn(normed_low, query_full[:, j * cols : (j + 1) * cols]).astype(BF) for j in range(groups)]
-    ).reshape(groups, seqs, rows, cols)
-    latent_state = [
-        dot_nn(normed_low, latent_full[:, g * LATD : (g + 1) * LATD]).astype(BF) for g in range(KVH)
-    ]
-    latent_send = jnp.stack([latent_state[j * heads // HG] for j in range(groups)]).reshape(
-        groups, seqs, rows, LATD
-    )
-    head_queries = swap_group(query_send)
-    head_latent = swap_group(latent_send).transpose(1, 0, 2, 3).reshape(-1, LATD)
     expand_local = lax.dynamic_slice(
         expand_full,
         (0, me * heads // HG, 0, me * heads % HG * 2 * DH),
         (devices, 1, LATD // devices, heads * 2 * DH),
     ).reshape(LATD, -1)
-    head_pairs = dot_nn(head_latent, expand_local).astype(BF)
     if ring:
-        attended, logsum, own_cotangent, output_full = attention_forward_gather(
-            dp, head_queries, head_pairs, cotangent, (w_output,), ((0, 0, width),), ("xzy",)
-        )
+        half = width // 2
+        (
+            attended,
+            logsum,
+            head_queries,
+            head_pairs,
+            head_latent,
+            own_cotangent,
+            output_full,
+            down_full,
+        ) = attention_forward_gather(
+            dp,
+            own_inputs.reshape(count, width),
+            gain_one.reshape(1, width),
+            query_full,
+            latent_full,
+            expand_local,
+            cotangent,
+            (w_output, w_down),
+            ((0, 0, width), (1, 0, half), (1, half, half)),
+            ("xzy", "xzy", "zyx"),
+        )
+        down_full = down_full.reshape(-1, width)
     else:
+        token_rows = own_inputs.astype(F32).reshape(count, width)
+        normed, inverse_one = norm_parts(token_rows, gain_one)
+        normed_low = normed.astype(BF)
+        query_send = jnp.stack(
+            [dot_nn(normed_low, query_full[:, j * cols : (j + 1) * cols]).astype(BF) for j in range(groups)]
+        ).reshape(groups, seqs, rows, cols)
+        latent_state = [
+            dot_nn(normed_low, latent_full[:, g * LATD : (g + 1) * LATD]).astype(BF) for g in range(KVH)
+        ]
+        latent_send = jnp.stack([latent_state[j * heads // HG] for j in range(groups)]).reshape(
+            groups, seqs, rows, LATD
+        )
+        head_queries = swap_group(query_send)
+        head_latent = swap_group(latent_send).transpose(1, 0, 2, 3).reshape(-1, LATD)
+        head_pairs = dot_nn(head_latent, expand_local).astype(BF)
         attended, logsum = attention_forward(head_queries, head_pairs)
         own_cotangent = swap_sequences(cotangent, seqs)
         output_full = full[4]
+        down_full = lax.all_gather(w_down, ALL, axis=0, tiled=True)
     output_full = output_full.reshape(-1, width)
     token_attended = swap_group(attended).reshape(groups, count, cols)
     seq_group = lax.dynamic_index_in_dim(group_ids, lax.axis_index("seq"), 0, keepdims=False)
@@ -1322,7 +1490,7 @@
     seq_scale = jnp.sum(chosen * group_scale).reshape(1, 1)
     x_rows = own_inputs.reshape(count, width)
     cot_rows = own_cotangent.reshape(count, width)
-    result, middle, normed_two_back, gu_share, down_grad = feed_forward(
+    result, normed_two_back, gu_share, down_grad, *rest = feed_forward(
         dp if ring else None,
         seq_scale,
         x_rows,
@@ -1334,13 +1502,17 @@
         down_full,
     )
     own_output = result.reshape(seqs, rows, width)
-    if not ring:
+    if ring:
+        middle_grad = normed_two_back
+        gain_two_grad, head_upstream, output_grad = rest
+        head_upstream = head_upstream.reshape(groups, seqs, rows, cols)
+    else:
         gu_share = lax.psum_scatter(gu_share, ALL, scatter_dimension=0, tiled=True).astype(F32)
+        middle_grad, back_send, output_grad, gain_two_grad = branch_back(
+            seq_scale, *rest, normed_two_back, cot_rows, token_attended, output_full, gain_two
+        )
+        head_upstream = swap_group(back_send.reshape(groups, seqs, rows, cols))
     gu_share = gu_share.reshape(drows, -1, 2, CUT)
-    middle_grad, back_send, output_grad, gain_two_grad = branch_back(
-        seq_scale, middle, normed_two_back, cot_rows, token_attended, output_full, gain_two
-    )
-    head_upstream = swap_group(back_send.reshape(groups, seqs, rows, cols))
     terms = (output_grad.reshape(devices, drows, width), down_grad.reshape(devices, -1, width))
     attention = (head_queries, head_pairs, head_upstream, attended, logsum)
     if ring:
@@ -1360,7 +1532,7 @@
             lax.psum_scatter(w, ALL, scatter_dimension=0, tiled=True)[0].astype(F32) for w in terms
         ]
     if ring:
-        input_grad, q_share, e_share, g_share = closing(
+        input_grad, q_share, l_share, e_share, g_share = closing(
             dp,
             query_back.reshape(groups, count, cols),
             pair_back,
@@ -1375,7 +1547,7 @@
         )
         shard = (lax.axis_index("dp") * 2 + lax.axis_index("seq")) * 2 + me
         own_gains = lax.dynamic_slice(g_share, (0, shard * drows % 128), (2, drows))
-        sums = (q_share[:, :width], q_share[:, width:], e_share)
+        sums = (q_share, l_share, e_share)
     else:
         latent_terms = dot_nt(pair_back, expand_local).astype(BF)
         expand_part = dot_tn(head_latent, pair_back)

time: 474 us -> 443 us (0.935)
  Pallas kernels: 353 us -> 396 us
  waiting for transfers between devices: 41 us -> 0.02 us
  matrix products: 8.62 us -> 0 us
  starting transfers between devices: 12.8 us -> 4.87 us
  blocking collectives: 6.32 us -> 0 us
    pallas_call x1, Pallas kernels: 48.9 us -> 102 us  [attention_forward_gather(): pl.pallas_call(functools.partial(forward_gather_kernel, dp, cuts, orders,...]
    all_gather x1, waiting for transfers between devices: 40.3 us -> 0.01 us  [local(): gu_full = lax.all_gather(gate_up, ALL, axis=0, tiled=True)]
    dot_general x5 -> x0, matrix products: 8.62 us -> none  [dot_nn(): lax.dot_general(a, b, (((1,), (0,)), ((), ())), preferred_element_type=F32)]
    all_to_all x3 -> x1, starting transfers between devices: 12.7 us -> 4.83 us  [swap_group(): return lax.all_to_all(blocks, 'grp', 0, 0, tiled=True)]
    pallas_call x1, Pallas kernels: 84.7 us -> 77.5 us  [attention_backward_scatter(): pl.pallas_call(functools.partial(backward_scatter_kernel, dp, blk, cuts,...]
    all_to_all x1 -> x0, blocking collectives: 6.32 us -> none  [swap_group(): return lax.all_to_all(blocks, 'grp', 0, 0, tiled=True)]
    pallas_call x2 -> x1, Pallas kernels: 111 us -> 106 us  [feed_forward(): pl.pallas_call(functools.partial(ffn_kernel, dp), grid=(steps,), in_specs...]
    unnamed x54 -> x33, local copies, waits for them, and re-layouts: 9.86 us -> 8.92 us
  transfers between devices with their start and end apart: 5 -> 2, of which waited for: 1 -> 0; matrix products, arithmetic and copies ran while one was open for 5% -> 2% of each run, Pallas kernels for 21% -> 35%
where the time goes in v6:
time: 443 us; the launch traced here: 440 us
  Pallas kernels  396 us (89%)
  local copies, waits for them, and re-layouts  21.4 us (5%)
  between operations  14.5 us (3%)
  starting transfers between devices  4.87 us (1%)
    pallas_call x1, Pallas kernels, feed_forward(): pl.pallas_call(functools.partial(ffn_kernel, dp), grid=(steps,), in_specs...  106 us
    pallas_call x1, Pallas kernels, attention_forward_gather(): pl.pallas_call(functools.partial(forward_gather_kernel, dp, cuts, orders,...  102 us
    pallas_call x1, Pallas kernels, attention_backward_scatter(): pl.pallas_call(functools.partial(backward_scatter_kernel, dp, blk, cuts,...  77.5 us
    pallas_call x1, Pallas kernels, closing(): pl.pallas_call(functools.partial(closing_kernel, dp), in_specs=[anywhere]...  60.5 us
    pallas_call x1, Pallas kernels, own_gather(): pl.pallas_call(functools.partial(gather_kernel, dp, orders), in_specs=[an...  50.6 us
    unnamed x33, local copies, waits for them, and re-layouts  8.92 us
  transfers between devices with their start and end apart: 2, of which 0 were waited for; matrix products, arithmetic and copies ran while one was open for 2% of the time, Pallas kernels for 35%

profile of v6, /device:TPU:0, one launch (start us, length us, event | category | flops | bytes accessed | tf_op | source)
XLA Modules:
  0.0 440.1 jit_solution(3137233892161719736)
XLA Ops:
  7.2 1.0 stack_reshape.6
  8.3 1.0 stack_reshape.7
  9.8 1.0 reshape.105
  11.5 50.6 %shard_map.212 = (bf16[32,32,1024]{2,1,0:T(8,128)(2,1)}, bf16[32,32,512]{2,1,0:T(8,128)(2,1)}, bf16[32,16,1024]{2,1,0:T(8,128)(2,1)}, bf16[32,16,128]{2,1,0:T(8,128)(2,1)}, bf16[2,512,1024]{2,1,0:T(8,128)(2,1)}) custom-call(bf16[32,1024]{1,0:T(8,128)(2,1)} %refs_0_.1, bf16[32,512]{1,0:T(8,128)(2,1)} %refs_1_.1, bf16[16,1024]{1,0:T(8,128)(2,1)} %bitcast.47, ...), custom_call_target="tpu_custom_call" | custom-call | tf_op jit(solution)/shard_map/pallas_call | solution.py:282
  62.1 0.9 fusion.1
  63.0 0.7 reshape.114.refs_1_
  63.6 1.9 dynamic-slice_bitcast_fusion.refs_4_.refs_3_
  65.5 101.9 %shard_map.213 = (bf16[2,2,512,512]{3,2,1,0:T(8,128)(2,1)}, f32[4,2,2048]{2,1,0:T(2,128)}, bf16[2,2,512,512]{3,2,1,0:T(8,128)(2,1)}, bf16[2048,1024]{1,0:T(8,128...) custom-call(bf16[1024,1024]{1,0:T(8,128)(2,1)} %bitcast.36, ...), custom_call_target="tpu_custom_call" | custom-call | flops 17179869184 | bytes 8388608 | tf_op jit(solution)/shard_map/pallas_call | solution.py:573
  167.5 4.8 %all-to-all-start = ((bf16[2,2,512,512]{3,2,1,0:T(8,128)(2,1)}), bf16[2,2,512,512]{3,2,1,0:T(8,128)(2,1)}, u32[]{:S(2)}, u32[]{:S(2)}) async-start(bf16[2,2,512,512]{3,2,1,0:T(8,128)(2,1)} %get-tuple-element.48.refs_3_), calls=%async_computation | async-start | bytes 4194304 | tf_op jit(solution)/shard_map/all_to_all | solution.py:1388
  172.3 1.0 slice_convert_fusion
  174.0 0.7 reshape_squeeze.10.gain_ref
  175.3 1.2 fusion
  176.6 105.5 %shard_map.214 = (bf16[1024,1024]{1,0:T(8,128)(2,1)}, f32[1024,1024]{1,0:T(8,128)}, f32[32,5632]{1,0:T(8,128)}, bf16[2816,1024]{1,0:T(8,128)(2,1)}, f32[1,1024]{...) custom-call(f32[1,1]{1,0:T(1,128)} %bitcast.8.scale_ref, bf16[1024,1024]{1,0:T(8,128)(2,1)} %bitcast.37, ...), custom_call_target="tpu_custom_call" | custom-call | flops 53150220288 | bytes 8388608 | tf_op jit(solution)/shard_map/pallas_call | solution.py:1069
  282.1 77.5 %shard_map.215 = (bf16[2,2,512,512]{3,2,1,0:T(8,128)(2,1)}, bf16[2048,1024]{1,0:T(8,128)(2,1)}, bf16[2,512,1024]{2,1,0:T(8,128)(2,1)}, f32[32,1024]{1,0:T(8,128)}, f32[88,1024]{1,0:T(8,128)}) custom-call(bf16[2,2,512,512]{3,2,1,0:T(8,128)(2,1)} %get-tuple-element.46.refs_0_, bf16[2048,1024]{1,0:T(8,128)(2,1)} %get-tuple-element.47.refs_1_, ...), custom_call_target="tpu_custom_call" | custom-call | flops 34359738368 | bytes 8388608 | tf_op jit(solution)/shard_map/pallas_call | solution.py:743
  359.6 60.5 %shard_map.216 = (bf16[2,512,1024]{2,1,0:T(8,128)(2,1)}, f32[32,1024]{1,0:T(8,128)}, f32[32,512]{1,0:T(8,128)}, f32[16,1024]{1,0:T(8,128)}, f32[16,128]{1,0:T(8,128)}) custom-call(bf16[2,1024,512]{2,1,0:T(8,128)(2,1)} %bitcast.39, bf16[2048,1024]{1,0:T(8,128)(2,1)} %get-tuple-element.59.refs_1_, bf16[2048,256]{1,0:T(8,128)(2,1)} %get-tuple-element.60.refs_2_, ...), custom_call_target="tpu_custom_call" | custom-call | tf_op jit(solution)/shard_map/pallas_call | solution.py:1324
  420.1 0.8 constant_dynamic-slice_fusion
  421.3 0.7 reshape.113
  422.1 2.0 slice_reduce_fusion
  424.1 0.9 copy.31
  425.0 0.9 copy.30
  426.0 1.3 copy.39
  427.3 1.0 copy-done.1
  428.3 1.3 copy.40
  432.2 0.7 copy.45
  (38 shorter events, 5.6 us)
Async XLA Ops:
  7.2 3.6 copy-start.8
  7.2 3.6 copy-start.9
  7.2 169.4 %all-gather.2.cloned.1.call-start = ((), (), s32[]{:S(2)}) async-start(), calls=%async_computation.1 | async-start | bytes 11894784 | tf_op jit(solution)/shard_map/all_gather | solution.py:1430
  167.4 7.3 %copy-start.10 = (s32[2]{0:T(128)S(1)}, s32[2]{0:T(128)}, u32[]{:S(2)}) copy-start(s32[2]{0:T(128)} %param.15) | copy-start | bytes 28
  167.5 7.8 %copy-start.11 = (f32[8]{0:T(128)S(1)}, f32[8]{0:T(128)}, u32[]{:S(2)}) copy-start(f32[8]{0:T(128)} %param.16) | copy-start | bytes 100
  167.5 9.1 %all-to-all-start = ((bf16[2,2,512,512]{3,2,1,0:T(8,128)(2,1)}), bf16[2,2,512,512]{3,2,1,0:T(8,128)(2,1)}, u32[]{:S(2)}, u32[]{:S(2)}) async-start(bf16[2,2,512,512]{3,2,1,0:T(8,128)(2,1)} %get-tuple-element.48.refs_3_), calls=%async_computation | async-start | bytes 4194304 | tf_op jit(solution)/shard_map/all_to_all | solution.py:1388
  359.6 61.8 %copy-start.2 = (f32[32,5632]{1,0:T(8,128)S(1)}, f32[32,5632]{1,0:T(8,128)}, u32[]{:S(2)}) copy-start(f32[32,5632]{1,0:T(8,128)} %get-tuple-element.69) | copy-start | bytes 2162692
  422.1 3.9 copy-start
  425.9 2.3 copy-start.1
  428.3 1.3 copy-start.5
  428.3 2.0 copy-start.7
  428.3 2.6 copy-start.6
  428.3 3.3 copy-start.4
  428.3 3.9 copy-start.3
Sparse Core Ops, SparseCore 0:
  11.5 131.6 all-gather.1

commit v7 on v6

--- a/solution.py
+++ b/solution.py
@@ -434,10 +434,11 @@
     x_ref, gain_ref, wq_ref, wl_ref, ex_ref, x_in = refs[:6]
     sources = 1 + max(cut[0] for cut in cuts)
     srcs, refs = refs[6 : 6 + sources], refs[6 + sources :]
-    o_ref, lse_ref, q_out, kv_out, hl_out, x_out = refs[:6]
-    outs, refs = refs[6 : 6 + sources], refs[6 + sources :]
-    vt_s, x_sem, low_s, q_send, lat_send, q_s, kv_s, hl_s, far_send, far_recv, save_sem = refs[:11]
-    sems = refs[11:]
+    lse_ref, o_out, token_out, q_out, kv_out, hl_out, x_out = refs[:7]
+    outs, refs = refs[7 : 7 + sources], refs[7 + sources :]
+    vt_s, x_sem, low_s, q_send, lat_send, q_s, kv_s, hl_s, o_s = refs[:9]
+    far_send, far_recv, save_sem = refs[9:12]
+    sems = refs[12:]
     place = Place(dp)
     c = place.core
     works = []
@@ -479,6 +480,13 @@
         return [
             pltpu.make_async_copy(src, dst, save_sem.at[i])
             for i, (src, dst) in enumerate(((q_s, q_out), (kv_s, kv_out), (hl_s, hl_out)))
+        ]
+
+    def hand_over():
+        return [
+            remote(o_s.at[1 - c], token_out.at[c], far_send.at[3], far_recv.at[3], place.pair()),
+            pltpu.make_async_copy(o_s.at[c], token_out.at[c], save_sem.at[3]),
+            pltpu.make_async_copy(o_s, o_out, save_sem.at[4]),
         ]
 
     @pl.when(pl.program_id(0) == 0)
@@ -512,7 +520,7 @@
     forward_body(
         q_s.at[:, :, :, at(pid, 128)],
         kv_s.at[:, at(pid, 256)],
-        o_ref,
+        o_s.at[:, :, :, at(pid, 128)],
         lse_ref,
         vt_s,
         lambda i: run_at(plan, i),
@@ -520,11 +528,13 @@
 
     @pl.when(pid == pairs - 1)
     def _():
+        for copy in hand_over():
+            copy.start()
         far_q().wait_send()
         for u in range(chunks):
             far_l(u).wait_send()
-        for save in saves():
-            save.wait()
+        for copy in saves() + hand_over():
+            copy.wait()
         for task in plan["last", 0]:
             task()
 
@@ -574,9 +584,9 @@
         functools.partial(forward_gather_kernel, dp, cuts, orders, pairs),
         grid=(pairs,),
         in_specs=[whole(w) for w in (x, gain, wq, wl, expand)] + [anywhere] * (1 + count),
-        out_specs=outs + [anywhere] * (4 + count),
-        out_shape=shapes
-        + [q, kv, hl]
+        out_specs=outs[1:] + [anywhere] * (6 + count),
+        out_shape=shapes[1:]
+        + [q, q, q, kv, hl]
         + [jax.ShapeDtypeStruct(blocks.shape, blocks.dtype)]
         + [jax.ShapeDtypeStruct((4 * dp, *w.shape), w.dtype) for w in shards],
         scratch_shapes=scratch
@@ -588,9 +598,10 @@
             pltpu.VMEM(q.shape, BF),
             pltpu.VMEM(kv.shape, BF),
             pltpu.VMEM(hl.shape, BF),
-            sem((3,)),
-            sem((3,)),
-            sem((3,)),
+            pltpu.VMEM(q.shape, BF),
+            sem((4,)),
+            sem((4,)),
+            sem((5,)),
         ]
         + gather_sems(dp, len(cuts)),
         compiler_params=pltpu.CompilerParams(
@@ -806,12 +817,16 @@
             self.place.device(offset),
         )
 
-    def hops(self, odd, phase):
-        q = self.total // 4
+    def hops(self, way, phase):
+        q, unit = self.total // 4, self.unit
+        sizes = range(1, self.place.sizes["z"])
+        if way == 2:
+            far = [("z", z, z * unit, unit, 1 + 2 * z) for z in sizes]
+            far += [("z", z, q + z * unit, unit, 2 + 2 * z) for z in sizes]
+            return ([("y", 1, 2 * q, 2 * q, 1)], far, [("x", 1, q, unit, 2)])[phase - 1]
         if phase == 3:
-            sizes = range(1, self.place.sizes["z"])
-            return [("z", z, z * self.unit, self.unit, 3 + z) for z in sizes]
-        if odd:
+            return [("z", z, z * unit, unit, 3 + z) for z in sizes]
+        if way:
             return ([("x", 1, q, q, 1), ("x", 1, 3 * q, q, 2)], [("y", 1, 2 * q, q, 3)])[phase - 1]
         return ([("y", 1, 2 * q, 2 * q, 1)], [("x", 1, q, q, 3)])[phase - 1]
 
@@ -820,33 +835,41 @@
             self.pair_buf[j, to : to + size].astype(F32) + came.astype(F32)
         ).astype(BF)
 
-    def advance(self, j, odd, phase):
-        q = self.total // 4
+    def advance(self, j, way, phase):
+        q, unit = self.total // 4, self.unit
+        sizes = range(1, self.place.sizes["z"])
         if phase == 1:
             self.pair(j).wait_recv()
             self.add(j, 0, self.total, self.stage[lax.rem(j, self.stage.shape[0]), : self.total])
         else:
-            for hop in self.hops(odd, phase - 1):
+            for hop in self.hops(way, phase - 1):
                 self.hop(j, *hop).wait_recv()
-        if phase == 2 and odd:
+        if phase == 2 and way == 1:
             self.add(j, 0, q, self.ring_buf[j, q : 2 * q])
             self.add(j, 2 * q, q, self.ring_buf[j, 3 * q :])
         elif phase == 2:
             self.add(j, 0, 2 * q, self.ring_buf[j, 2 * q :])
+        elif phase == 3 and way == 2:
+            for first in (0, q):
+                total = self.pair_buf[j, first : first + unit].astype(F32)
+                for z in sizes:
+                    came = slice(first + z * unit, first + (z + 1) * unit)
+                    total = total + self.ring_buf[j, came].astype(F32)
+                self.pair_buf[j, first : first + unit] = total.astype(BF)
         elif phase == 3:
-            first = 2 * q if odd else q
+            first = 2 * q if way else q
             self.add(j, 0, q, self.ring_buf[j, first : first + q])
         elif phase == 4:
-            total = self.pair_buf[j, : self.unit].astype(F32)
-            for z in range(1, self.place.sizes["z"]):
-                total = total + self.ring_buf[j, z * self.unit : (z + 1) * self.unit].astype(F32)
+            total = self.pair_buf[j, :unit].astype(F32)
+            for first in (q,) if way == 2 else [z * unit for z in sizes]:
+                total = total + self.ring_buf[j, first : first + unit].astype(F32)
             wide = total.shape[1]
             if self.last_ref is not None and j == self.pair_buf.shape[0] - 1:
                 self.last_ref[...] = total
             else:
                 self.out_ref[:, pl.ds(pl.multiple_of(j * wide, wide), wide)] = total
         if phase < 4:
-            for hop in self.hops(odd, phase):
+            for hop in self.hops(way, phase):
                 self.hop(j, *hop).start()
 
     def finish(self, parities):
@@ -1034,7 +1057,7 @@
             end.wait()
 
 
-def feed_forward(dp, scale, x, att, wo, gain, cot, gu, down):
+def feed_forward(dp, scale, x, att, gain, cot, wide, down):
     rows, width = x.shape
     size = down.shape[0]
     blocks, tall = size // CUT, size // DOWN
@@ -1059,7 +1082,7 @@
         out += [shape((1, width), F32), shape(att.shape, BF), shape((width, width), BF)]
         out_specs += [whole(out[2]), anywhere, whole(out[4]), anywhere, anywhere]
         first = [pltpu.VMEM((rows, width), F32), sem((2,)), sem((2,))]
-        sems = sem((blocks, 3 + dp // 2))
+        sems = sem((blocks, dp + 1))
         scratch = [pltpu.VMEM((blocks, width // 2, 2 * CUT), BF)] * 2 + [sems] * 2
         params = {"collective_id": 4, "has_side_effects": True}
         steps += rows // min(PART, rows) + 1
@@ -1073,10 +1096,10 @@
             pl.BlockSpec(memory_space=pltpu.SMEM),
             whole(x),
             whole(att),
-            whole(wo),
+            pl.BlockSpec((width, width), lambda i: (0, 0), pipeline_mode=once),
             whole(gain),
             whole(cot),
-            pl.BlockSpec((width, 2 * CUT), lambda i: (0, last(i))),
+            pl.BlockSpec((width, 2 * CUT), lambda i: (0, last(i) + width // (2 * CUT))),
             pl.BlockSpec((CUT, width), lambda i: (last(i), 0)),
         ],
         out_specs=out_specs,
@@ -1097,7 +1120,7 @@
         ],
         compiler_params=pltpu.CompilerParams(vmem_limit_bytes=63 * 2**20, **params),
         cost_estimate=cost(18 * rows * width * size),
-    )(scale, x, att, wo, gain, cot, gu, down)
+    )(scale, x, att, wide, gain, cot, wide, down)
 
 
 def branch_kernel(scale_ref, mid_ref, nb_ref, cot_ref, att_ref, wo_ref, gain_ref,
@@ -1173,6 +1196,9 @@
     )(scale, mid, nback, cot, att, wo, gain)
 
 
+Q_WAYS = (2, 2, 0)
+
+
 def closing_kernel(dp, *refs):
     dq_in, dkv_in, hl_in, ex_in, x_in, gain_ref, wq_in, wl_in, mg_in, gg_ref = refs[:10]
     ig_out, q_out, l_out, e_out, g_out = refs[10:15]
@@ -1198,7 +1224,7 @@
     def load(i):
         return pltpu.make_async_copy(*loads[i], load_sem.at[i])
 
-    for i in range(len(loads)):
+    for i in (3, 4, 0, 1, 5, 6, 7, 2):
         load(i).start()
     place.greet()
     far_q = remote(dq_in.at[1 - c], far_dq, far_send.at[0], far_recv.at[0], place.pair())
@@ -1210,6 +1236,20 @@
     g_sums = BlockSums(dp, g_stage, g_pair, g_ring, g_send, g_recv, g_out)
     order = q_sums.order()
 
+    load(3).wait()
+    gain = gain_ref[...].astype(F32)
+
+    def inverse_of(values):
+        return lax.rsqrt(jnp.mean(values * values, axis=-1, keepdims=True) + EPSILON)
+
+    for u in range(2):
+        chunk = slice(u * part, (u + 1) * part)
+        values = x[chunk].astype(F32)
+        flip[...] = (values * inverse_of(values) * gain).astype(BF).T
+        for i, shard in enumerate(order):
+            n1t[i * unit : (i + 1) * unit, chunk] = flip[at(shard, unit)]
+    load(4).wait()
+    q_stage[c] = dot_nn(n1t[...], dq[...]).astype(BF)
     load(0).wait()
     load(1).wait()
     for u in range(2):
@@ -1217,21 +1257,12 @@
     far_l.start()
     for u in range(2):
         lat_own[u * part : (u + 1) * part] = dot_nt(dkv[at(u * 2 + c, part)], ex[...]).astype(BF)
-    load(3).wait()
-    gain = gain_ref[...].astype(F32)
-
-    def inverse_of(values):
-        return lax.rsqrt(jnp.mean(values * values, axis=-1, keepdims=True) + EPSILON)
-
-    for u in range(2):
-        chunk = slice(u * part, (u + 1) * part)
-        values = x[chunk].astype(F32)
-        flip[...] = (values * inverse_of(values) * gain).astype(BF).T
-        for i, shard in enumerate(order):
-            n1t[i * unit : (i + 1) * unit, chunk] = flip[at(shard, unit)]
-    for i in (4, 5, 6, 7):
+    far_q.wait_recv()
+    q_stage[1 - c] = dot_nn(n1t[...], far_dq[...]).astype(BF)
+    for j in range(2):
+        q_sums.pair(j).start()
+    for i in (5, 6, 7):
         load(i).wait()
-    far_q.wait_recv()
     far_l.wait_recv()
 
     def back(u):
@@ -1257,10 +1288,8 @@
     gain_part = back(1 - s)
     swap, kept = block_swap(ig, ig_out, x_sem, place)
     swap.start()
-    q_stage[c] = dot_nn(n1t[...], dq[...]).astype(BF)
-    q_stage[1 - c] = dot_nn(n1t[...], far_dq[...]).astype(BF)
     for j in range(2):
-        q_sums.pair(j).start()
+        q_sums.advance(j, 2, 1)
     q_stage[2, :, at(c, lat)] = dot_nn(n1t[...], lat_own[...]).astype(BF)
     q_stage[2, :, at(1 - c, lat)] = dot_nn(n1t[...], far_lat[...]).astype(BF)
     q_sums.pair(2).start()
@@ -1277,8 +1306,7 @@
             e_stage[j, i * 2 * share : (i + 1) * 2 * share] = whole[:, j * cols : (j + 1) * cols]
     for j in range(2):
         e_sums.pair(j).start()
-    for j in range(3):
-        q_sums.advance(j, j % 2, 1)
+    q_sums.advance(2, 0, 1)
     gain_part = gain_part + back(s)
     kept.start()
     g_s[...] = jnp.concatenate(
@@ -1288,17 +1316,17 @@
         g_stage[0, i * 16 : (i + 1) * 16] = g_s[:, at(lax.div(shard * unit, 128), 128)]
     g_sums.pair(0).start()
     for j in range(2):
-        e_sums.advance(j, 1 - j, 1)
-    g_sums.advance(0, 1, 1)
+        e_sums.advance(j, 2, 1)
+    g_sums.advance(0, 2, 1)
     for phase in (2, 3, 4):
         for j in range(3):
-            q_sums.advance(j, j % 2, phase)
+            q_sums.advance(j, Q_WAYS[j], phase)
         for j in range(2):
-            e_sums.advance(j, 1 - j, phase)
-        g_sums.advance(0, 1, phase)
+            e_sums.advance(j, 2, phase)
+        g_sums.advance(0, 2, phase)
     far_q.wait_send()
     far_l.wait_send()
-    for sums, parities in ((q_sums, (0, 1, 0)), (e_sums, (1, 0)), (g_sums, (1,))):
+    for sums, parities in ((q_sums, Q_WAYS), (e_sums, (2, 2)), (g_sums, (2,))):
         for j in range(len(parities)):
             sums.pair(j).wait_send()
         sums.finish(parities)
@@ -1346,7 +1374,7 @@
         ]
         + sums
         + [sem((8,)), sem((2,)), sem((2,)), sem((3,))]
-        + [sem((blocks, 3 + dp // 2)) for blocks in (3, 3, 2, 2, 1, 1)],
+        + [sem((blocks, dp + 1)) for blocks in (3, 3, 2, 2, 1, 1)],
         compiler_params=pltpu.CompilerParams(
             collective_id=1, has_side_effects=True, vmem_limit_bytes=60 * 2**20
         ),
@@ -1421,13 +1449,15 @@
         shards = (w_query, w_latent, expand_rows, gains)
         full, own_inputs = own_gather(dp, shards, inputs, ("xzy",) * 4)
     else:
-        shards = (w_query, w_latent, expand_rows, gains, w_output)
+        shards = (w_query, w_latent, expand_rows, gains)
         full = [lax.all_gather(w, ALL, axis=0) for w in shards]
         own_inputs = swap_sequences(inputs, seqs)
     gate_up = jnp.stack(
         [w_gate.reshape(drows, -1, CUT), w_up.reshape(drows, -1, CUT)], axis=2
     ).reshape(drows, -1)
-    gu_full = lax.all_gather(gate_up, ALL, axis=0, tiled=True)
+    wide_full = lax.all_gather(
+        jnp.concatenate([w_output, gate_up], axis=1), ALL, axis=0, tiled=True
+    )
     query_full = full[0].reshape(width, -1)
     latent_full = full[1].reshape(width, -1)
     expand_full = full[2].reshape(devices, KVH, LATD // devices, -1)
@@ -1442,13 +1472,13 @@
     if ring:
         half = width // 2
         (
+            logsum,
             attended,
-            logsum,
+            token_attended,
             head_queries,
             head_pairs,
             head_latent,
             own_cotangent,
-            output_full,
             down_full,
         ) = attention_forward_gather(
             dp,
@@ -1458,9 +1488,9 @@
             latent_full,
             expand_local,
             cotangent,
-            (w_output, w_down),
-            ((0, 0, width), (1, 0, half), (1, half, half)),
-            ("xzy", "xzy", "zyx"),
+            (w_down,),
+            ((0, 0, half), (0, half, half)),
+            ("xzy", "zxy"),
         )
         down_full = down_full.reshape(-1, width)
     else:
@@ -1480,11 +1510,10 @@
         head_latent = swap_group(latent_send).transpose(1, 0, 2, 3).reshape(-1, LATD)
         head_pairs = dot_nn(head_latent, expand_local).astype(BF)
         attended, logsum = attention_forward(head_queries, head_pairs)
+        token_attended = swap_group(attended)
         own_cotangent = swap_sequences(cotangent, seqs)
-        output_full = full[4]
         down_full = lax.all_gather(w_down, ALL, axis=0, tiled=True)
-    output_full = output_full.reshape(-1, width)
-    token_attended = swap_group(attended).reshape(groups, count, cols)
+    token_attended = token_attended.reshape(groups, count, cols)
     seq_group = lax.dynamic_index_in_dim(group_ids, lax.axis_index("seq"), 0, keepdims=False)
     chosen = (seq_group == jnp.arange(GROUPS)).astype(F32)
     seq_scale = jnp.sum(chosen * group_scale).reshape(1, 1)
@@ -1495,10 +1524,9 @@
         seq_scale,
         x_rows,
         token_attended,
-        output_full,
         gain_two,
         cot_rows,
-        gu_full,
+        wide_full,
         down_full,
     )
     own_output = result.reshape(seqs, rows, width)
@@ -1509,7 +1537,7 @@
     else:
         gu_share = lax.psum_scatter(gu_share, ALL, scatter_dimension=0, tiled=True).astype(F32)
         middle_grad, back_send, output_grad, gain_two_grad = branch_back(
-            seq_scale, *rest, normed_two_back, cot_rows, token_attended, output_full, gain_two
+            seq_scale, *rest, normed_two_back, cot_rows, token_attended, wide_full[:, :width], gain_two
         )
         head_upstream = swap_group(back_send.reshape(groups, seqs, rows, cols))
     gu_share = gu_share.reshape(drows, -1, 2, CUT)

time: 443 us -> 417 us (0.941)
  Pallas kernels: 396 us -> 375 us
  starting transfers between devices: 4.87 us -> 0.04 us
    pallas_call x1, Pallas kernels: 60.5 us -> 47.4 us  [closing(): pl.pallas_call(functools.partial(closing_kernel, dp), in_specs=[anywhere]...]
    pallas_call x1, Pallas kernels: 102 us -> 93.4 us  [attention_forward_gather(): pl.pallas_call(functools.partial(forward_gather_kernel, dp, cuts, orders,...]
    all_to_all x1 -> x0, starting transfers between devices: 4.83 us -> none  [swap_group(): return lax.all_to_all(blocks, 'grp', 0, 0, tiled=True)]
    unnamed x33 -> x35, local copies, waits for them, and re-layouts: 8.92 us -> 8.93 us
  transfers between devices with their start and end apart: 2 -> 1, of which waited for: 0 -> 0; matrix products, arithmetic and copies ran while one was open for 2% -> 2% of each run, Pallas kernels for 35% -> 35%
where the time goes in v7:
time: 417 us; the launch traced here: 414 us
  Pallas kernels  375 us (90%)
  local copies, waits for them, and re-layouts  20.7 us (5%)
  between operations  14.5 us (3%)
    pallas_call x1, Pallas kernels, feed_forward(): pl.pallas_call(functools.partial(ffn_kernel, dp), grid=(steps,), in_specs...  104 us
    pallas_call x1, Pallas kernels, attention_forward_gather(): pl.pallas_call(functools.partial(forward_gather_kernel, dp, cuts, orders,...  93.4 us
    pallas_call x1, Pallas kernels, attention_backward_scatter(): pl.pallas_call(functools.partial(backward_scatter_kernel, dp, blk, cuts,...  78.1 us
    pallas_call x1, Pallas kernels, own_gather(): pl.pallas_call(functools.partial(gather_kernel, dp, orders), in_specs=[an...  51.3 us
    pallas_call x1, Pallas kernels, closing(): pl.pallas_call(functools.partial(closing_kernel, dp), in_specs=[anywhere]...  47.4 us
    unnamed x35, local copies, waits for them, and re-layouts  8.93 us
  transfers between devices with their start and end apart: 1, of which 0 were waited for; matrix products, arithmetic and copies ran while one was open for 2% of the time, Pallas kernels for 35%

profile of v7, /device:TPU:0, one launch (start us, length us, event | category | flops | bytes accessed | tf_op | source)
XLA Modules:
  0.0 414.0 jit_solution(15716830185496145721)
XLA Ops:
  7.2 1.0 stack_reshape.6
  8.3 1.0 stack_reshape.7
  10.1 0.8 pad_maximum_fusion.1
  11.6 51.3 %shard_map.212 = (bf16[32,32,1024]{2,1,0:T(8,128)(2,1)}, bf16[32,32,512]{2,1,0:T(8,128)(2,1)}, bf16[32,16,1024]{2,1,0:T(8,128)(2,1)}, bf16[32,16,128]{2,1,0:T(8,128)(2,1)}, bf16[2,512,1024]{2,1,0:T(8,128)(2,1)}) custom-call(bf16[32,1024]{1,0:T(8,128)(2,1)} %refs_0_.1, bf16[32,512]{1,0:T(8,128)(2,1)} %refs_1_.1, bf16[16,1024]{1,0:T(8,128)(2,1)} %bitcast.46, ...), custom_call_target="tpu_custom_call" | custom-call | tf_op jit(solution)/shard_map/pallas_call | solution.py:282
  63.0 0.9 fusion.1
  63.9 0.7 reshape.110.refs_1_
  64.5 1.0 slice_convert_fusion
  65.6 0.7 reshape.111.refs_5_
  66.2 0.7 reshape_squeeze.10.gain_ref
  67.5 1.2 fusion
  68.7 1.9 dynamic-slice_bitcast_fusion.refs_4_.refs_3_
  70.6 93.4 %shard_map.213 = (f32[4,2,2048]{2,1,0:T(2,128)}, bf16[2,2,512,512]{3,2,1,0:T(8,128)(2,1)}, bf16[2,2,512,512]{3,2,1,0:T(8,128)(2,1)}, bf16[2,2,512,512]{3,2,1,0:T...) custom-call(bf16[1024,1024]{1,0:T(8,128)(2,1)} %bitcast.35, ...), custom_call_target="tpu_custom_call" | custom-call | flops 17179869184 | bytes 8388608 | tf_op jit(solution)/shard_map/pallas_call | solution.py:583
  164.0 104.4 %shard_map.214 = (bf16[1024,1024]{1,0:T(8,128)(2,1)}, f32[1024,1024]{1,0:T(8,128)}, f32[32,5632]{1,0:T(8,128)}, bf16[2816,1024]{1,0:T(8,128)(2,1)}, f32[1,1024]{...) custom-call(f32[1,1]{1,0:T(1,128)} %bitcast.8.scale_ref, bf16[1024,1024]{1,0:T(8,128)(2,1)} %bitcast.36, ...), custom_call_target="tpu_custom_call" | custom-call | flops 53150220288 | bytes 8388608 | tf_op jit(solution)/shard_map/pallas_call | solution.py:1092
  268.5 78.1 %shard_map.215 = (bf16[2,2,512,512]{3,2,1,0:T(8,128)(2,1)}, bf16[2048,1024]{1,0:T(8,128)(2,1)}, bf16[2,512,1024]{2,1,0:T(8,128)(2,1)}, f32[32,1024]{1,0:T(8,128)}, f32[88,1024]{1,0:T(8,128)}) custom-call(bf16[2,2,512,512]{3,2,1,0:T(8,128)(2,1)} %get-tuple-element.46.refs_0_, bf16[2048,1024]{1,0:T(8,128)(2,1)} %get-tuple-element.47.refs_1_, ...), custom_call_target="tpu_custom_call" | custom-call | flops 34359738368 | bytes 8388608 | tf_op jit(solution)/shard_map/pallas_call | solution.py:754
  346.6 47.4 %shard_map.216 = (bf16[2,512,1024]{2,1,0:T(8,128)(2,1)}, f32[32,1024]{1,0:T(8,128)}, f32[32,512]{1,0:T(8,128)}, f32[16,1024]{1,0:T(8,128)}, f32[16,128]{1,0:T(8,128)}) custom-call(bf16[2,1024,512]{2,1,0:T(8,128)(2,1)} %bitcast.38, bf16[2048,1024]{1,0:T(8,128)(2,1)} %get-tuple-element.59.refs_1_, bf16[2048,256]{1,0:T(8,128)(2,1)} %get-tuple-element.60.refs_2_, ...), custom_call_target="tpu_custom_call" | custom-call | tf_op jit(solution)/shard_map/pallas_call | solution.py:1352
  394.0 0.8 constant_dynamic-slice_fusion
  395.3 0.7 reshape.109
  396.0 2.0 slice_reduce_fusion
  398.0 0.9 copy.31
  399.0 0.9 copy.30
  399.9 1.3 copy.39
  401.2 1.0 copy-done.1
  402.3 1.3 copy.40
  406.2 0.7 copy.45
  (39 shorter events, 5.2 us)
Async XLA Ops:
  7.2 2.9 copy-start.8
  7.2 156.8 %all-gather.2.cloned.1.call-start = ((), (), s32[]{:S(2)}) async-start(), calls=%async_computation | async-start | bytes 14057472 | tf_op jit(solution)/shard_map/all_gather | solution.py:1458
  9.3 1.6 copy-start.9
  9.3 1.6 copy-start.10
  9.8 57.1 %copy-start.11 = (s32[2]{0:T(128)S(1)}, s32[2]{0:T(128)}, u32[]{:S(2)}) copy-start(s32[2]{0:T(128)} %param.15) | copy-start | bytes 28
  9.8 57.7 %copy-start.12 = (f32[8]{0:T(128)S(1)}, f32[8]{0:T(128)}, u32[]{:S(2)}) copy-start(f32[8]{0:T(128)} %param.16) | copy-start | bytes 100
  346.6 48.7 %copy-start.2 = (f32[32,5632]{1,0:T(8,128)S(1)}, f32[32,5632]{1,0:T(8,128)}, u32[]{:S(2)}) copy-start(f32[32,5632]{1,0:T(8,128)} %get-tuple-element.69) | copy-start | bytes 2162692
  396.0 3.9 copy-start
  399.9 2.3 copy-start.1
  402.3 1.3 copy-start.5
  402.3 2.0 copy-start.7
  402.3 2.6 copy-start.6
  402.3 3.3 copy-start.4
  402.3 3.9 copy-start.3
Sparse Core Ops, SparseCore 0:
  11.4 138.1 all-gather.1

commit v8 on v7

--- a/solution.py
+++ b/solution.py
@@ -431,14 +431,14 @@
 
 
 def forward_gather_kernel(dp, cuts, orders, pairs, *refs):
-    x_ref, gain_ref, wq_ref, wl_ref, ex_ref, x_in = refs[:6]
+    x_ref, tiles_ref, wq_ref, wl_ref, shards_ref, x_in = refs[:6]
     sources = 1 + max(cut[0] for cut in cuts)
     srcs, refs = refs[6 : 6 + sources], refs[6 + sources :]
-    lse_ref, o_out, token_out, q_out, kv_out, hl_out, x_out = refs[:7]
-    outs, refs = refs[7 : 7 + sources], refs[7 + sources :]
-    vt_s, x_sem, low_s, q_send, lat_send, q_s, kv_s, hl_s, o_s = refs[:9]
-    far_send, far_recv, save_sem = refs[9:12]
-    sems = refs[12:]
+    lse_ref, gain_ref, o_out, token_out, q_out, kv_out, hl_out, ex_out, x_out = refs[:9]
+    outs, refs = refs[9 : 9 + sources], refs[9 + sources :]
+    vt_s, x_sem, low_s, q_send, lat_send, q_s, kv_s, hl_s, o_s, ex_s = refs[:10]
+    far_send, far_recv, save_sem = refs[10:13]
+    sems = refs[13:]
     place = Place(dp)
     c = place.core
     works = []
@@ -479,19 +479,34 @@
     def saves():
         return [
             pltpu.make_async_copy(src, dst, save_sem.at[i])
-            for i, (src, dst) in enumerate(((q_s, q_out), (kv_s, kv_out), (hl_s, hl_out)))
+            for i, (src, dst) in enumerate(
+                ((q_s, q_out), (kv_s, kv_out), (hl_s, hl_out), (ex_s, ex_out))
+            )
         ]
 
     def hand_over():
         return [
             remote(o_s.at[1 - c], token_out.at[c], far_send.at[3], far_recv.at[3], place.pair()),
-            pltpu.make_async_copy(o_s.at[c], token_out.at[c], save_sem.at[3]),
-            pltpu.make_async_copy(o_s, o_out, save_sem.at[4]),
+            pltpu.make_async_copy(o_s.at[c], token_out.at[c], save_sem.at[4]),
+            pltpu.make_async_copy(o_s, o_out, save_sem.at[5]),
         ]
 
     @pl.when(pl.program_id(0) == 0)
     def _():
-        gain = gain_ref[...].astype(F32)
+        count = 128 * tiles_ref.shape[0] // gain_ref.shape[1]
+        for t in range(gain_ref.shape[1] // 128):
+            total = tiles_ref[t * count].astype(F32)
+            for i in range(1, count):
+                total = total + tiles_ref[t * count + i].astype(F32)
+            gain_ref[:, t * 128 : (t + 1) * 128] = total[:8]
+        share = shards_ref.shape[1] // KVH
+        for i in range(0, shards_ref.shape[0], KVH):
+            pieces = []
+            for k in range(KVH):
+                both = shards_ref[i + k].astype(F32)
+                pieces.append(jnp.where(c == 0, both[:share], both[share:]))
+            ex_s[i * share : (i + KVH) * share] = jnp.concatenate(pieces, axis=0).astype(BF)
+        gain = gain_ref[0:1]
         for u in range(chunks):
             chunk = slice(u * rows, (u + 1) * rows)
             values = x_ref[chunk].astype(F32)
@@ -511,7 +526,7 @@
             far_l(u).wait_recv()
         for k in range(groups * chunks):
             chunk = slice(k * rows, (k + 1) * rows)
-            kv_s[chunk] = dot_nn(hl_s[chunk], ex_ref[...]).astype(BF)
+            kv_s[chunk] = dot_nn(hl_s[chunk], ex_s[...]).astype(BF)
         far_q().wait_recv()
         for save in saves():
             save.start()
@@ -565,28 +580,30 @@
     )(q, kv)
 
 
-def attention_forward_gather(dp, x, gain, wq, wl, expand, blocks, shards, cuts, orders):
+def attention_forward_gather(dp, x, tiles, wq, wl, expand, blocks, shards, cuts, orders):
     rows, width = blocks.shape[1], x.shape[1]
-    cols, lat = width // 2, expand.shape[0]
+    cols, lat = width // 2, expand.shape[0] * expand.shape[1] // KVH
     seq = 4 * rows
     q = jax.ShapeDtypeStruct((2, 2, rows, cols), BF)
     kv = jax.ShapeDtypeStruct((seq, 2 * cols), BF)
     hl = jax.ShapeDtypeStruct((seq, lat), BF)
+    ex = jax.ShapeDtypeStruct((lat, 2 * cols), BF)
+    gains = jax.ShapeDtypeStruct((8, width), F32)
     pairs, _, outs, shapes, scratch, estimate = forward_specs(q, kv)
     anywhere = pl.BlockSpec(memory_space=pl.ANY)
     count = len(shards)
     sem = pltpu.SemaphoreType.DMA
 
     def whole(w):
-        return pl.BlockSpec(w.shape, lambda p: (0, 0), pipeline_mode=pl.Buffered(1))
+        return pl.BlockSpec(w.shape, lambda p: (0,) * len(w.shape), pipeline_mode=pl.Buffered(1))
 
     return pl.pallas_call(
         functools.partial(forward_gather_kernel, dp, cuts, orders, pairs),
         grid=(pairs,),
-        in_specs=[whole(w) for w in (x, gain, wq, wl, expand)] + [anywhere] * (1 + count),
-        out_specs=outs[1:] + [anywhere] * (6 + count),
+        in_specs=[whole(w) for w in (x, tiles, wq, wl, expand)] + [anywhere] * (1 + count),
+        out_specs=outs[1:] + [whole(gains)] + [anywhere] * (7 + count),
         out_shape=shapes[1:]
-        + [q, q, q, kv, hl]
+        + [gains, q, q, q, kv, hl, ex]
         + [jax.ShapeDtypeStruct(blocks.shape, blocks.dtype)]
         + [jax.ShapeDtypeStruct((4 * dp, *w.shape), w.dtype) for w in shards],
         scratch_shapes=scratch
@@ -599,16 +616,17 @@
             pltpu.VMEM(kv.shape, BF),
             pltpu.VMEM(hl.shape, BF),
             pltpu.VMEM(q.shape, BF),
+            pltpu.VMEM(ex.shape, BF),
             sem((4,)),
             sem((4,)),
-            sem((5,)),
+            sem((6,)),
         ]
         + gather_sems(dp, len(cuts)),
         compiler_params=pltpu.CompilerParams(
             vmem_limit_bytes=60 * 2**20, collective_id=2, has_side_effects=True
         ),
         cost_estimate=estimate,
-    )(x, gain, wq, wl, expand, blocks, *shards)
+    )(x, tiles, wq, wl, expand, blocks, *shards)
 
 
 def backward_body(blk, q_ref, kv_ref, do_ref, o_ref, lse_ref, dq_ref, dkv_ref,
@@ -775,7 +793,7 @@
 PART = 512
 TALL = 512
 DOWN = 8
-LAGS = (1, 3, 5, 7)
+LAGS = (1, 3, 6, 9)
 
 
 class BlockSums:
@@ -901,7 +919,7 @@
     def _():
         if dp:
             sums.place.greet()
-        gain = gain_ref[...].astype(F32)
+        gain = (gain_ref[1:2] if dp else gain_ref[...]).astype(F32)
         scale = scale_ref[0, 0]
         for at in chunks:
             mid = x_ref[at].astype(F32)
@@ -1027,7 +1045,7 @@
 
         @pl.when(step == blocks + DOWN + q)
         def _(q=q, at=at):
-            mid, nback, gain = mid_ref[at], nb_ref[at], gain_ref[...].astype(F32)
+            mid, nback, gain = mid_ref[at], nb_ref[at], gain_ref[1:2]
             inverse = lax.rsqrt(jnp.mean(mid * mid, axis=-1, keepdims=True) + EPSILON)
             scaled = nback * gain
             middle_grad = cot_ref[at].astype(F32) * scale_ref[0, 0] + (
@@ -1237,7 +1255,7 @@
     order = q_sums.order()
 
     load(3).wait()
-    gain = gain_ref[...].astype(F32)
+    gain = gain_ref[0:1]
 
     def inverse_of(values):
         return lax.rsqrt(jnp.mean(values * values, axis=-1, keepdims=True) + EPSILON)
@@ -1444,12 +1462,14 @@
     dp = lax.axis_size("dp")
     ring = groups == 2 and seqs == 2 and dp % 2 == 0
     expand_rows = expansion_weight.reshape(-1, expansion_weight.shape[2])
-    gains = jnp.pad(jnp.concatenate([norm_gain, ffn_gain])[None], ((0, 15), (0, 128 - 2 * drows)))
+    shard = (lax.axis_index("dp") * seqs + lax.axis_index("seq")) * groups + me
+    both_gains = jnp.stack([norm_gain, ffn_gain])
+    gains = lax.dynamic_update_slice(jnp.zeros((16, 128), BF), both_gains, (0, shard * drows % 128))
     if ring:
         shards = (w_query, w_latent, expand_rows, gains)
         full, own_inputs = own_gather(dp, shards, inputs, ("xzy",) * 4)
     else:
-        shards = (w_query, w_latent, expand_rows, gains)
+        shards = (w_query, w_latent, expand_rows)
         full = [lax.all_gather(w, ALL, axis=0) for w in shards]
         own_inputs = swap_sequences(inputs, seqs)
     gate_up = jnp.stack(
@@ -1461,39 +1481,42 @@
     query_full = full[0].reshape(width, -1)
     latent_full = full[1].reshape(width, -1)
     expand_full = full[2].reshape(devices, KVH, LATD // devices, -1)
-    gain_one = full[3][:, 0, :drows].reshape(width).astype(F32)
-    gain_two = full[3][:, 0, drows : 2 * drows].reshape(1, width)
-
-    expand_local = lax.dynamic_slice(
-        expand_full,
-        (0, me * heads // HG, 0, me * heads % HG * 2 * DH),
-        (devices, 1, LATD // devices, heads * 2 * DH),
-    ).reshape(LATD, -1)
     if ring:
         half = width // 2
         (
             logsum,
+            gain_rows,
             attended,
             token_attended,
             head_queries,
             head_pairs,
             head_latent,
+            expand_local,
             own_cotangent,
             down_full,
         ) = attention_forward_gather(
             dp,
             own_inputs.reshape(count, width),
-            gain_one.reshape(1, width),
+            full[3],
             query_full,
             latent_full,
-            expand_local,
+            full[2],
             cotangent,
             (w_down,),
             ((0, 0, half), (0, half, half)),
             ("xzy", "zxy"),
         )
         down_full = down_full.reshape(-1, width)
+        gain_one = gain_two = gain_rows
     else:
+        gain_one, gain_two = [
+            lax.all_gather(w, ALL, axis=0, tiled=True).reshape(1, width) for w in (norm_gain, ffn_gain)
+        ]
+        expand_local = lax.dynamic_slice(
+            expand_full,
+            (0, me * heads // HG, 0, me * heads % HG * 2 * DH),
+            (devices, 1, LATD // devices, heads * 2 * DH),
+        ).reshape(LATD, -1)
         token_rows = own_inputs.astype(F32).reshape(count, width)
         normed, inverse_one = norm_parts(token_rows, gain_one)
         normed_low = normed.astype(BF)
@@ -1573,7 +1596,6 @@
             middle_grad,
             gain_two_grad,
         )
-        shard = (lax.axis_index("dp") * 2 + lax.axis_index("seq")) * 2 + me
         own_gains = lax.dynamic_slice(g_share, (0, shard * drows % 128), (2, drows))
         sums = (q_share, l_share, e_share)
     else:

time: 417 us -> 405 us (0.971)
  Pallas kernels: 375 us -> 368 us
    pallas_call x1, Pallas kernels: 93.4 us -> 88.4 us  [attention_forward_gather(): pl.pallas_call(functools.partial(forward_gather_kernel, dp, cuts, orders,...]
    unnamed x35 -> x37, local copies, waits for them, and re-layouts: 8.93 us -> 9.51 us
  transfers between devices with their start and end apart: 1 -> 1, of which waited for: 0 -> 0; matrix products, arithmetic and copies ran while one was open for 2% -> 1% of each run, Pallas kernels for 35% -> 35%
where the time goes in v8:
time: 405 us; the launch traced here: 402 us
  Pallas kernels  368 us (91%)
  local copies, waits for them, and re-layouts  17.1 us (4%)
  between operations  14.5 us (4%)
    pallas_call x1, Pallas kernels, feed_forward(): pl.pallas_call(functools.partial(ffn_kernel, dp), grid=(steps,), in_specs...  102 us
    pallas_call x1, Pallas kernels, attention_forward_gather(): pl.pallas_call(functools.partial(forward_gather_kernel, dp, cuts, orders,...  88.4 us
    pallas_call x1, Pallas kernels, attention_backward_scatter(): pl.pallas_call(functools.partial(backward_scatter_kernel, dp, blk, cuts,...  77.3 us
    pallas_call x1, Pallas kernels, own_gather(): pl.pallas_call(functools.partial(gather_kernel, dp, orders), in_specs=[an...  51.8 us
    pallas_call x1, Pallas kernels, closing(): pl.pallas_call(functools.partial(closing_kernel, dp), in_specs=[anywhere]...  48.8 us
    unnamed x37, local copies, waits for them, and re-layouts  9.51 us
  transfers between devices with their start and end apart: 1, of which 0 were waited for; matrix products, arithmetic and copies ran while one was open for 1% of the time, Pallas kernels for 35%

profile of v8, /device:TPU:0, one launch (start us, length us, event | category | flops | bytes accessed | tf_op | source)
XLA Modules:
  0.0 402.1 jit_solution(6476236194179922115)
XLA Ops:
  7.2 1.0 stack_reshape.6
  8.3 1.0 stack_reshape.7
  10.1 0.8 pad_maximum_fusion.1
  10.9 0.6 dynamic_slice.7
  11.9 0.6 copy-done.9
  12.5 51.8 %shard_map.212 = (bf16[32,32,1024]{2,1,0:T(8,128)(2,1)}, bf16[32,32,512]{2,1,0:T(8,128)(2,1)}, bf16[32,16,1024]{2,1,0:T(8,128)(2,1)}, bf16[32,16,128]{2,1,0:T(8,128)(2,1)}, bf16[2,512,1024]{2,1,0:T(8,128)(2,1)}) custom-call(bf16[32,1024]{1,0:T(8,128)(2,1)} %refs_0_.1, bf16[32,512]{1,0:T(8,128)(2,1)} %refs_1_.1, bf16[16,1024]{1,0:T(8,128)(2,1)} %bitcast.38, ...), custom_call_target="tpu_custom_call" | custom-call | tf_op jit(solution)/shard_map/pallas_call | solution.py:282
  64.2 1.2 fusion
  65.5 88.4 %shard_map.213 = (f32[4,2,2048]{2,1,0:T(2,128)}, f32[8,1024]{1,0:T(8,128)}, bf16[2,2,512,512]{3,2,1,0:T(8,128)(2,1)}, bf16[2,2,512,512]{3,2,1,0:T(8,128)(2,1)}, ...) custom-call(bf16[1024,1024]{1,0:T(8,128)(2,1)} %bitcast.27, ...), custom_call_target="tpu_custom_call" | custom-call | flops 17179869184 | bytes 8388608 | tf_op jit(solution)/shard_map/pallas_call | solution.py:600
  153.9 102.0 %shard_map.214 = (bf16[1024,1024]{1,0:T(8,128)(2,1)}, f32[1024,1024]{1,0:T(8,128)}, f32[32,5632]{1,0:T(8,128)}, bf16[2816,1024]{1,0:T(8,128)(2,1)}, f32[1,1024]{...) custom-call(f32[1,1]{1,0:T(1,128)} %bitcast.7.scale_ref, bf16[1024,1024]{1,0:T(8,128)(2,1)} %bitcast.28, ...), custom_call_target="tpu_custom_call" | custom-call | flops 53150220288 | bytes 8388608 | tf_op jit(solution)/shard_map/pallas_call | solution.py:1110
  256.0 77.3 %shard_map.215 = (bf16[2,2,512,512]{3,2,1,0:T(8,128)(2,1)}, bf16[2048,1024]{1,0:T(8,128)(2,1)}, bf16[2,512,1024]{2,1,0:T(8,128)(2,1)}, f32[32,1024]{1,0:T(8,128)}, f32[88,1024]{1,0:T(8,128)}) custom-call(bf16[2,2,512,512]{3,2,1,0:T(8,128)(2,1)} %get-tuple-element.48.refs_0_, bf16[2048,1024]{1,0:T(8,128)(2,1)} %get-tuple-element.49.refs_1_, ...), custom_call_target="tpu_custom_call" | custom-call | flops 34359738368 | bytes 8388608 | tf_op jit(solution)/shard_map/pallas_call | solution.py:772
  333.3 48.8 %shard_map.216 = (bf16[2,512,1024]{2,1,0:T(8,128)(2,1)}, f32[32,1024]{1,0:T(8,128)}, f32[32,512]{1,0:T(8,128)}, f32[16,1024]{1,0:T(8,128)}, f32[16,128]{1,0:T(8,128)}) custom-call(bf16[2,1024,512]{2,1,0:T(8,128)(2,1)} %bitcast.30, bf16[2048,1024]{1,0:T(8,128)(2,1)} %get-tuple-element.62.refs_1_, bf16[2048,256]{1,0:T(8,128)(2,1)} %get-tuple-element.63.refs_2_, ...), custom_call_target="tpu_custom_call" | custom-call | tf_op jit(solution)/shard_map/pallas_call | solution.py:1370
  382.1 0.8 constant_dynamic-slice_fusion
  383.4 0.7 reshape.86
  384.1 2.0 slice_reduce_fusion
  386.1 0.9 copy.28
  387.0 0.9 copy.27
  388.0 1.3 copy.37
  389.3 1.0 copy-done.1
  390.4 1.3 copy.38
  391.7 0.7 copy.39
  392.3 0.6 copy.40
  393.0 0.6 copy.41
  393.6 0.7 copy.42
  394.3 0.7 copy.43
  (36 shorter events, 1.7 us)
Async XLA Ops:
  7.2 2.9 copy-start.8
  7.2 146.7 %all-gather.2.cloned.1.call-start = ((), (), s32[]{:S(2)}) async-start(), calls=%async_computation | async-start | bytes 14057472 | tf_op jit(solution)/shard_map/all_gather | solution.py:1478
  9.3 1.6 copy-start.10
  9.3 2.2 copy-start.11
  9.4 2.2 copy-start.12
  9.8 54.4 %copy-start.13 = (f32[8]{0:T(128)S(1)}, f32[8]{0:T(128)}, u32[]{:S(2)}) copy-start(f32[8]{0:T(128)} %param.16) | copy-start | bytes 100
  11.9 0.6 copy-start.9
  333.3 50.1 %copy-start.2 = (f32[32,5632]{1,0:T(8,128)S(1)}, f32[32,5632]{1,0:T(8,128)}, u32[]{:S(2)}) copy-start(f32[32,5632]{1,0:T(8,128)} %get-tuple-element.73) | copy-start | bytes 2162692
  384.1 3.9 copy-start
  388.0 2.3 copy-start.1
  390.3 1.3 copy-start.5
  390.3 2.0 copy-start.7
  390.3 2.6 copy-start.6
  390.4 3.3 copy-start.4
  390.4 3.9 copy-start.3
Sparse Core Ops, SparseCore 0:
  11.4 138.2 all-gather.1

commit v9 on v8

--- a/solution.py
+++ b/solution.py
@@ -1504,7 +1504,7 @@
             cotangent,
             (w_down,),
             ((0, 0, half), (0, half, half)),
-            ("xzy", "zxy"),
+            ("yzx", "xzy"),
         )
         down_full = down_full.reshape(-1, width)
         gain_one = gain_two = gain_rows

time: 405 us -> 409 us (level)
  no operation moved by 1% of the time
where the time goes in v9:
time: 409 us; the launch traced here: 406 us
  Pallas kernels  372 us (91%)
  local copies, waits for them, and re-layouts  17.1 us (4%)
  between operations  14.5 us (4%)
    pallas_call x1, Pallas kernels, feed_forward(): pl.pallas_call(functools.partial(ffn_kernel, dp), grid=(steps,), in_specs...  103 us
    pallas_call x1, Pallas kernels, attention_forward_gather(): pl.pallas_call(functools.partial(forward_gather_kernel, dp, cuts, orders,...  92.3 us
    pallas_call x1, Pallas kernels, attention_backward_scatter(): pl.pallas_call(functools.partial(backward_scatter_kernel, dp, blk, cuts,...  77.4 us
    pallas_call x1, Pallas kernels, own_gather(): pl.pallas_call(functools.partial(gather_kernel, dp, orders), in_specs=[an...  51.8 us
    pallas_call x1, Pallas kernels, closing(): pl.pallas_call(functools.partial(closing_kernel, dp), in_specs=[anywhere]...  47.8 us
    unnamed x37, local copies, waits for them, and re-layouts  9.51 us
  transfers between devices with their start and end apart: 1, of which 0 were waited for; matrix products, arithmetic and copies ran while one was open for 1% of the time, Pallas kernels for 35%

profile of v9, /device:TPU:0, one launch (start us, length us, event | category | flops | bytes accessed | tf_op | source)
XLA Modules:
  0.0 406.2 jit_solution(7746319759367921750)
XLA Ops:
  7.2 1.0 stack_reshape.6
  8.3 1.0 stack_reshape.7
  10.1 0.8 pad_maximum_fusion.1
  10.9 0.6 dynamic_slice.7
  11.9 0.6 copy-done.9
  12.5 51.8 %shard_map.212 = (bf16[32,32,1024]{2,1,0:T(8,128)(2,1)}, bf16[32,32,512]{2,1,0:T(8,128)(2,1)}, bf16[32,16,1024]{2,1,0:T(8,128)(2,1)}, bf16[32,16,128]{2,1,0:T(8,128)(2,1)}, bf16[2,512,1024]{2,1,0:T(8,128)(2,1)}) custom-call(bf16[32,1024]{1,0:T(8,128)(2,1)} %refs_0_.1, bf16[32,512]{1,0:T(8,128)(2,1)} %refs_1_.1, bf16[16,1024]{1,0:T(8,128)(2,1)} %bitcast.38, ...), custom_call_target="tpu_custom_call" | custom-call | tf_op jit(solution)/shard_map/pallas_call | solution.py:282
  64.2 1.2 fusion
  65.5 92.3 %shard_map.213 = (f32[4,2,2048]{2,1,0:T(2,128)}, f32[8,1024]{1,0:T(8,128)}, bf16[2,2,512,512]{3,2,1,0:T(8,128)(2,1)}, bf16[2,2,512,512]{3,2,1,0:T(8,128)(2,1)}, ...) custom-call(bf16[1024,1024]{1,0:T(8,128)(2,1)} %bitcast.27, ...), custom_call_target="tpu_custom_call" | custom-call | flops 17179869184 | bytes 8388608 | tf_op jit(solution)/shard_map/pallas_call | solution.py:600
  157.8 103.1 %shard_map.214 = (bf16[1024,1024]{1,0:T(8,128)(2,1)}, f32[1024,1024]{1,0:T(8,128)}, f32[32,5632]{1,0:T(8,128)}, bf16[2816,1024]{1,0:T(8,128)(2,1)}, f32[1,1024]{...) custom-call(f32[1,1]{1,0:T(1,128)} %bitcast.7.scale_ref, bf16[1024,1024]{1,0:T(8,128)(2,1)} %bitcast.28, ...), custom_call_target="tpu_custom_call" | custom-call | flops 53150220288 | bytes 8388608 | tf_op jit(solution)/shard_map/pallas_call | solution.py:1110
  261.0 77.4 %shard_map.215 = (bf16[2,2,512,512]{3,2,1,0:T(8,128)(2,1)}, bf16[2048,1024]{1,0:T(8,128)(2,1)}, bf16[2,512,1024]{2,1,0:T(8,128)(2,1)}, f32[32,1024]{1,0:T(8,128)}, f32[88,1024]{1,0:T(8,128)}) custom-call(bf16[2,2,512,512]{3,2,1,0:T(8,128)(2,1)} %get-tuple-element.48.refs_0_, bf16[2048,1024]{1,0:T(8,128)(2,1)} %get-tuple-element.49.refs_1_, ...), custom_call_target="tpu_custom_call" | custom-call | flops 34359738368 | bytes 8388608 | tf_op jit(solution)/shard_map/pallas_call | solution.py:772
  338.4 47.8 %shard_map.216 = (bf16[2,512,1024]{2,1,0:T(8,128)(2,1)}, f32[32,1024]{1,0:T(8,128)}, f32[32,512]{1,0:T(8,128)}, f32[16,1024]{1,0:T(8,128)}, f32[16,128]{1,0:T(8,128)}) custom-call(bf16[2,1024,512]{2,1,0:T(8,128)(2,1)} %bitcast.30, bf16[2048,1024]{1,0:T(8,128)(2,1)} %get-tuple-element.62.refs_1_, bf16[2048,256]{1,0:T(8,128)(2,1)} %get-tuple-element.63.refs_2_, ...), custom_call_target="tpu_custom_call" | custom-call | tf_op jit(solution)/shard_map/pallas_call | solution.py:1370
  386.2 0.8 constant_dynamic-slice_fusion
  387.5 0.7 reshape.86
  388.2 2.0 slice_reduce_fusion
  390.2 0.9 copy.28
  391.2 0.9 copy.27
  392.1 1.3 copy.37
  393.4 1.0 copy-done.1
  394.5 1.3 copy.38
  395.8 0.7 copy.39
  396.5 0.6 copy.40
  397.1 0.6 copy.41
  397.7 0.7 copy.42
  398.4 0.7 copy.43
  (36 shorter events, 1.7 us)
Async XLA Ops:
  7.2 2.9 copy-start.8
  7.2 150.6 %all-gather.2.cloned.1.call-start = ((), (), s32[]{:S(2)}) async-start(), calls=%async_computation | async-start | bytes 14057472 | tf_op jit(solution)/shard_map/all_gather | solution.py:1478
  9.3 1.6 copy-start.10
  9.3 2.2 copy-start.11
  9.4 2.2 copy-start.12
  9.8 54.4 %copy-start.13 = (f32[8]{0:T(128)S(1)}, f32[8]{0:T(128)}, u32[]{:S(2)}) copy-start(f32[8]{0:T(128)} %param.16) | copy-start | bytes 100
  11.9 0.6 copy-start.9
  338.4 49.1 %copy-start.2 = (f32[32,5632]{1,0:T(8,128)S(1)}, f32[32,5632]{1,0:T(8,128)}, u32[]{:S(2)}) copy-start(f32[32,5632]{1,0:T(8,128)} %get-tuple-element.73) | copy-start | bytes 2162692
  388.2 3.9 copy-start
  392.1 2.3 copy-start.1
  394.5 1.3 copy-start.5
  394.5 2.0 copy-start.7
  394.5 2.6 copy-start.6
  394.5 3.3 copy-start.4
  394.5 3.9 copy-start.3
Sparse Core Ops, SparseCore 0:
  11.4 145.2 all-gather.1
